TPU v7x, 32 devices: a whole 2x2x4 slice. The times are simulated.
32 devices in a mesh: wide: 8 (over z, y), pair: 4 (over x, core).
Axes of the slice: x: 2, y: 2, z: 4, core: 2. Of those that a mesh axis runs over, the one named last changes fastest.
Arguments:
- three_center: bfloat16 [32, 8, 1024], P('wide'), may hold values from -1.25 to 1.25
- occ_green: bfloat16 [32, 8, 8, 8], P('wide', 'pair'), may hold values from -2 to 2
- virt_green: bfloat16 [32, 8, 8, 8], P('wide', 'pair'), may hold values from -2 to 2
- occ_column: int32 [32, 8], P('wide', 'pair'), may hold values from 0 to 31, as said below
- partner_live: int32 [32, 8], P('wide', 'pair'), may hold values 0 or 1
Outputs:
- response: float32 [128, 128], P('pair')
Inputs may be any that keep to these rules, and one draw needn't show every extreme that they name: `occ_column`: for each index of pair and each index w of wide, the slots of that group on the 4 atom blocks w * 4 to w * 4 + 3 name partner blocks k such that no value of k // 4 occurs more than 2 times, and some value occurs exactly 2 times.
All inputs are finite; a program needn't handle non-finite values. No bound on the sum of `partner_live` on one device may be relied on, other than what follows from the above.
Results may differ from a plain program's by a relative error of at most 0.004.
Values may be sent and summed in bfloat16 or wider, within the bound.
No kernel may reach another device: no remote copies, remote signals or barrier semaphores. Data moves between devices by JAX's collectives and lax.ppermute only.
A program may use at most 64 MiB of HBM per device.

v0:
```python
import jax
import jax.numpy as jnp
from jax import lax
from jax.sharding import PartitionSpec as P

CAP = 2


def apply_virtual(occupied, virt_blocks, block_size):
    shaped = occupied.reshape(occupied.shape[:-1] + (block_size, -1))
    product = jnp.einsum(
        "...lnp,...ns->...lsp", shaped, virt_blocks, preferred_element_type=jnp.float32
    )
    return product.astype(jnp.bfloat16).reshape(occupied.shape)


def slot_ranks(owners):
    unit_count = owners.shape[-1]
    same_owner = owners[..., :, None] == owners[..., None, :]
    before = jnp.arange(unit_count)[None, :] < jnp.arange(unit_count)[:, None]
    return jnp.sum(same_owner & before, axis=-1)


def local(three_center, occ_green, virt_green, occ_column, partner_live):
    local_atoms, block_size, wide_row = three_center.shape
    aux_count = wide_row // block_size
    wide_count = lax.axis_size("wide")
    slot_total = wide_count * CAP
    unit_count = occ_green.shape[0] * occ_green.shape[1]
    listed = lax.all_gather(occ_column, "wide", axis=0, tiled=True).reshape(wide_count, unit_count)
    listed_owner = listed // local_atoms
    listed_rank = slot_ranks(listed_owner)
    to_here = listed_owner == lax.axis_index("wide")
    chosen = to_here[:, None, :] & (listed_rank[:, None, :] == jnp.arange(CAP)[None, :, None])
    slot_atom = jnp.sum(jnp.where(chosen, (listed % local_atoms)[:, None, :], 0), axis=2).reshape(
        slot_total
    )
    slot_used = jnp.any(chosen, axis=2).reshape(slot_total)
    occupied = jnp.einsum(
        "amnl,anx->amlx", occ_green, three_center, preferred_element_type=jnp.float32
    )
    occupied = occupied * partner_live.astype(jnp.float32)[:, :, None, None]
    occupied = occupied.astype(jnp.bfloat16).reshape(unit_count, block_size, wide_row)
    owners = (occ_column // local_atoms).reshape(unit_count)
    position = owners * CAP + slot_ranks(owners)
    virt_units = virt_green.reshape(unit_count, block_size, block_size)
    own_rows = three_center.astype(jnp.float32).reshape(-1, aux_count)
    both = apply_virtual(occupied, virt_units, block_size)
    outgoing = jnp.zeros((slot_total, block_size, wide_row), jnp.bfloat16).at[position].set(both)
    arrived = lax.all_to_all(
        outgoing.reshape(wide_count, CAP, block_size, wide_row),
        "wide",
        split_axis=0,
        concat_axis=0,
        tiled=True,
    )
    routing = (
        (slot_atom[None, :] == jnp.arange(local_atoms)[:, None]) & slot_used[None, :]
    ).astype(jnp.bfloat16)
    partner_sum = jnp.dot(
        routing, arrived.reshape(slot_total, -1), preferred_element_type=jnp.float32
    )
    partner_rows = partner_sum.reshape(-1, aux_count)
    response_part = lax.dot_general(
        partner_rows,
        own_rows,
        (((0,), (0,)), ((), ())),
        precision=lax.Precision.HIGHEST,
        preferred_element_type=jnp.float32,
    )
    total = lax.psum(response_part, ("wide", "pair"))
    row_count = aux_count // lax.axis_size("pair")
    result = lax.dynamic_slice_in_dim(total, lax.axis_index("pair") * row_count, row_count, 0)
    return result


def solution(mesh):
    placed = (
        P("wide", None, None),
        P("wide", "pair", None, None),
        P("wide", "pair", None, None),
        P("wide", "pair"),
        P("wide", "pair"),
    )
    return jax.shard_map(
        local, mesh=mesh, in_specs=placed, out_specs=P("pair", None), check_vma=False
    )
```

profile of v0, /device:TPU:0, one launch (start us, length us, event | category | flops | bytes accessed | tf_op | source)
XLA Modules:
  0.0 167.5 jit_solution(17364678757003102876)
XLA Ops:
  6.5 0.7 broadcast_multiply_fusion
  7.3 0.1 copy.46
  7.4 0.1 copy.47
  7.6 0.2 convert_reduce_fusion.1
  7.8 0.5 copy-done.4
  8.3 0.1 copy.49
  8.4 1.1 fusion
  9.5 0.2 fusion.1
  9.8 0.7 broadcast_in_dim.12
  10.5 2.1 %scatter_fusion = bf16[16,8,1024]{2,1,0:T(8,128)(2,1)} fusion(bf16[16,8,1024]{2,1,0:T(8,128)(2,1)} %broadcast_in_dim.12, s32[8]{0:T(128)S(1)} %fusion.13, bf16[8,8,1024]{2,1,0:T(8,128)(2,1)S(1)} %reshape.166), kind=kCustom, calls=%fused_computation | custom fusion | bytes 393248 | tf_op jit(solution)/shard_map/scatter | solution.py:49
  12.6 7.4 %all-to-all-start = ((bf16[8,2,8,1024]{3,2,1,0:T(8,128)(2,1)}), bf16[8,2,8,1024]{3,2,1,0:T(8,128)(2,1)S(1)}, u32[]{:S(2)}, u32[]{:S(2)}) async-start(bf16[8,2,8,1024]{3,2,1,0:T(8,128)(2,1)} %bitcast.10), calls=%async_computation | async-start | bytes 524288 | tf_op jit(solution)/shard_map/all_to_all | solution.py:50
  20.1 0.7 copy-done.3
  20.7 20.9 %all-gather = s32[8,4,2]{1,2,0:T(2,128)S(1)} all-gather(s32[1,4,2]{1,2,0:T(2,128)S(1)} %bitcast.38), channel_id=1, replica_groups=mesh['wide'=8,'pair'=4] {'wide'}, dimensions={0}, use_global_device_ids=true | all-gather | bytes 288 | tf_op jit(solution)/shard_map/all_gather | solution.py:30
  41.6 0.1 copy.39
  42.0 0.3 convert_reduce_fusion
  42.3 0.1 select_reduce_fusion
  42.6 0.2 fusion.5
  42.8 0.1 copy.45
  43.0 0.2 copy.57
  43.2 0.2 fusion.9
  43.3 0.1 reshape.160
  43.4 0.9 fusion.14
  44.4 114.9 %all-reduce.2.cloned.1.call-done = f32[128,128]{1,0:T(8,128)} async-done(((f32[128,128]{1,0:T(8,128)}), f32[128,128]{1,0:T(8,128)}) %all-reduce.2.cloned.1.call-update) | async-done | bytes 65552 | tf_op jit(solution)/shard_map/psum | solution.py:71
  159.3 1.3 constant_dynamic-slice_fusion
  (26 shorter events, 0.9 us)
Async XLA Ops:
  6.5 2.9 %copy-start = (bf16[4,2,8,8]{3,2,1,0:T(8,128)(2,1)S(1)}, bf16[4,2,8,8]{3,2,1,0:T(8,128)(2,1)}, u32[]{:S(2)}) copy-start(bf16[4,2,8,8]{3,2,1,0:T(8,128)(2,1)} %param.7) | copy-start | bytes 3076
  6.5 1.9 %copy-start.2 = (bf16[4,2,8,8]{3,2,1,0:T(8,128)(2,1)S(1)}, bf16[4,2,8,8]{3,2,1,0:T(8,128)(2,1)}, u32[]{:S(2)}) copy-start(bf16[4,2,8,8]{3,2,1,0:T(8,128)(2,1)} %param.6) | copy-start | bytes 3076
  7.6 0.7 copy-start.4
  12.6 29.2 %copy-start.1 = (bf16[4,8,1024]{2,1,0:T(8,128)(2,1)S(1)}, bf16[4,8,1024]{2,1,0:T(8,128)(2,1)}, u32[]{:S(2)}) copy-start(bf16[4,8,1024]{2,1,0:T(8,128)(2,1)} %param.5) | copy-start | bytes 196612
  12.6 30.4 %all-to-all-start = ((bf16[8,2,8,1024]{3,2,1,0:T(8,128)(2,1)}), bf16[8,2,8,1024]{3,2,1,0:T(8,128)(2,1)S(1)}, u32[]{:S(2)}, u32[]{:S(2)}) async-start(bf16[8,2,8,1024]{3,2,1,0:T(8,128)(2,1)} %bitcast.10), calls=%async_computation | async-start | bytes 524288 | tf_op jit(solution)/shard_map/all_to_all | solution.py:50
  20.0 139.3 %all-reduce.2.cloned.1.call-start = ((), (), s32[]{:S(2)}) async-start(), calls=%async_computation.1 | async-start | bytes 131072 | tf_op jit(solution)/shard_map/psum | solution.py:71
  20.0 0.7 copy-start.3
Sparse Core Ops, SparseCore 0:
  44.5 114.7 all-reduce.1
where the time goes:
time: 169 us; the launch traced here: 167 us
  waiting for transfers between devices  115 us (68%)
  blocking collectives  20.9 us (12%)
  between operations  13.5 us (8%)
  starting transfers between devices  7.45 us (4%)
  local copies, waits for them, and re-layouts  6.76 us (4%)
  matrix products  2.35 us (1%)
    psum x1, waiting for transfers between devices, local(): total = lax.psum(response_part, ('wide', 'pair'))  115 us
    all_gather x1, blocking collectives, local(): lax.all_gather(occ_column, 'wide', axis=0, tiled=True)  20.9 us
    all_to_all x1, starting transfers between devices, local(): lax.all_to_all(outgoing.reshape(wide_count, CAP, block_size, wide_row), '...  7.42 us
  transfers between devices with their start and end apart: 2, of which 1 were waited for; matrix products, arithmetic and copies ran while one was open for 1% of the time, Pallas kernels for 0%

commit v1 on v0

v1 whole, which is shorter than its diff:
```python
import functools

import jax
import jax.numpy as jnp
from jax import lax
from jax.experimental import pallas as pl
from jax.experimental.pallas import tpu as pltpu
from jax.sharding import PartitionSpec as P

CHUNK = 4
BASE = 256
F32, BF16 = jnp.float32, jnp.bfloat16


def ceil_to(value, step):
    return -(-value // step) * step


def small_layout(unit_count, block_size):
    chunk_count = -(-unit_count // CHUNK)
    column_at = chunk_count * 2 * CHUNK * block_size
    return chunk_count, column_at, ceil_to(column_at + 2 * unit_count, 128)


def iota(shape, axis):
    return lax.broadcasted_iota(jnp.int32, shape, axis)


def pack_kernel(half_ref, column_ref, live_ref, tc_ref, occ_ref, virt_ref, block_ref, small_ref):
    local_atoms, own_units, block_size, _ = occ_ref.shape
    wide_row = tc_ref.shape[2]
    unit_count = 2 * own_units
    _, column_at, lanes = small_layout(unit_count, block_size)
    half = half_ref[0]
    row, lane = iota((block_size, lanes), 0), iota((block_size, lanes), 1)
    packed = jnp.zeros((local_atoms * block_size, lanes), F32)
    columns = [jnp.zeros((block_size, lanes), F32) for _ in range(local_atoms)]
    for slot in range(own_units):
        unit = half * own_units + slot
        at = (unit // CHUNK) * (2 * CHUNK * block_size) + (unit % CHUNK) * block_size
        occ = jnp.concatenate(
            [
                occ_ref[atom, slot].astype(F32) * live_ref[atom, slot].astype(F32)
                for atom in range(local_atoms)
            ],
            axis=0,
        ).astype(BF16)
        virt = jnp.concatenate(
            [virt_ref[atom, slot].astype(F32) for atom in range(local_atoms)], axis=0
        ).astype(BF16)
        occ_place = (lane == at + row).astype(BF16)
        virt_place = (lane == at + CHUNK * block_size + row).astype(BF16)
        packed += jnp.dot(occ, occ_place, preferred_element_type=F32)
        packed += jnp.dot(virt, virt_place, preferred_element_type=F32)
        for atom in range(local_atoms):
            column = column_ref[atom, slot]
            high = column // BASE
            low = column - high * BASE
            columns[atom] += jnp.where(lane == column_at + unit, high.astype(F32), 0.0)
            columns[atom] += jnp.where(
                lane == column_at + unit_count + unit, low.astype(F32), 0.0
            )
    packed = (packed + jnp.concatenate(columns, axis=0)).astype(BF16)
    packed = packed.reshape(local_atoms, block_size, lanes)
    block_ref[:, :, :wide_row] = tc_ref[...]
    block_ref[:, :, wide_row:] = packed
    small_ref[...] = packed


def response_kernel(
    wide_count, unit_count, starts_ref, place_ref, *refs
):
    block_refs = refs[: -7]
    keep_ref, send_ref, rows_ref, small_ref, index_ref, column_ref, sem = refs[-7:]
    block_size = block_refs[0].shape[1]
    square = block_size * block_size
    aux_count = rows_ref.shape[2]
    chunk_count, column_at, lanes = small_layout(unit_count, block_size)
    atom_total = rows_ref.shape[0]
    local_atoms = atom_total // wide_count
    side, half = place_ref[0], place_ref[1]

    for number, block_ref in enumerate(block_refs):
        first = starts_ref[number]

        def place_atom(atom, block_ref=block_ref, first=first):
            rows_ref[first + atom] = jnp.concatenate(
                [
                    block_ref[atom, :, at * aux_count : (at + 1) * aux_count]
                    for at in range(block_size)
                ],
                axis=0,
            )
            small_ref[first + atom] = block_ref[atom, :, block_size * aux_count :]

        if block_ref.shape[0] <= 8:
            for atom in range(block_ref.shape[0]):
                place_atom(atom)
        else:
            pl.loop(0, block_ref.shape[0])(place_atom)

    own_atoms = index_ref.shape[0]
    column_tile = column_at // 128 * 128
    column_lane = column_at - column_tile

    def atom_of(position):
        return ((position // local_atoms) * 2 + (side ^ half) % 2) * local_atoms + position % local_atoms

    def place_column(position):
        digits = small_ref[atom_of(position)][:, column_tile:].astype(F32)
        index_ref[position] = digits[0:1, :].astype(jnp.int32)

    if own_atoms <= 16:
        for position in range(own_atoms):
            place_column(position)
    else:
        pl.loop(0, own_atoms)(place_column)
    copy = pltpu.make_async_copy(index_ref, column_ref, sem)
    copy.start()

    wide_unit = CHUNK * square
    spread_row, spread_lane = iota((128, 2 * wide_unit), 0), iota((128, 2 * wide_unit), 1)
    is_virt = spread_lane >= wide_unit
    inner = spread_lane % wide_unit
    unit_of, upper, lower = inner // square, (inner // block_size) % block_size, inner % block_size
    wanted = unit_of * block_size + jnp.where(is_virt, upper + CHUNK * block_size, lower)
    lane_row, lane = iota((block_size, wide_unit), 0), iota((block_size, wide_unit), 1)
    lane_unit, lane_upper, lane_lower = lane // square, (lane // block_size) % block_size, lane % block_size
    occ_mask = [(lane_upper == at).astype(F32) for at in range(block_size)]
    virt_mask = [
        ((lane_unit == at) & (lane_lower == lane_row)).astype(F32) for at in range(CHUNK)
    ]
    group = max(1, min(own_atoms, 16 // chunk_count))
    copy.wait()

    def work(step, total):
        for chunk in range(chunk_count):
            at = chunk * 2 * CHUNK * block_size
            tile = at // 128 * 128
            spread = (spread_row == wanted + (at - tile)).astype(BF16)
            atoms = [atom_of(step * group + member) for member in range(group)]
            smalls = jnp.concatenate(
                [small_ref[atom][:, tile : tile + 128] for atom in atoms], axis=0
            )
            wide = jnp.dot(smalls, spread, preferred_element_type=F32)
            for member in range(group):
                values = wide[member * block_size : (member + 1) * block_size]
                occ, virt = values[:, :wide_unit], values[:, wide_unit:]
                occ_weights = jnp.concatenate([occ * mask for mask in occ_mask], axis=0)
                virt_weights = jnp.concatenate(
                    [
                        jnp.broadcast_to(virt[nu : nu + 1], virt.shape) * virt_mask[unit]
                        for unit in range(CHUNK)
                        for nu in range(block_size)
                    ],
                    axis=0,
                )
                occupied = lax.dot_general(
                    rows_ref[atoms[member]],
                    occ_weights.astype(BF16),
                    (((0,), (0,)), ((), ())),
                    preferred_element_type=F32,
                ).astype(BF16)
                both = jnp.dot(
                    occupied, virt_weights.astype(BF16), preferred_element_type=F32
                ).astype(BF16)
                partner = []
                for unit in range(chunk * CHUNK, (chunk + 1) * CHUNK):
                    if unit < unit_count:
                        high = column_ref[step * group + member, 0, column_lane + unit]
                        low = column_ref[
                            step * group + member, 0, column_lane + unit_count + unit
                        ]
                        partner.append(rows_ref[high * BASE + low])
                    else:
                        partner.append(jnp.zeros((square, aux_count), BF16))
                total += jnp.dot(
                    both, jnp.concatenate(partner, axis=0), preferred_element_type=F32
                )
        return total

    steps = own_atoms // group
    total = jnp.zeros((aux_count, aux_count), F32)
    if steps == 1:
        total = work(0, total)
    else:
        total = lax.fori_loop(0, steps, work, total)
    row_count = keep_ref.shape[1]
    parts = [total[at * row_count : (at + 1) * row_count] for at in range(4)]
    keep = [jnp.where(half == 0, parts[2 * at], parts[2 * at + 1]) for at in range(2)]
    send = [jnp.where(half == 0, parts[2 * at + 1], parts[2 * at]) for at in range(2)]
    outer = place_ref[2]
    keep_ref[0] = jnp.where(outer == 0, keep[0], keep[1])
    keep_ref[1] = jnp.where(outer == 0, keep[1], keep[0])
    send_ref[0] = jnp.where(outer == 0, send[0], send[1])
    send_ref[1] = jnp.where(outer == 0, send[1], send[0])


VMEM = pl.BlockSpec(memory_space=pltpu.VMEM)
SMEM = pl.BlockSpec(memory_space=pltpu.SMEM)


def gather_over_wide(block, wide_count, pair_count):
    here = lax.axis_index("wide")
    if wide_count != 8:
        return [lax.all_gather(block, "wide", axis=0, tiled=True)], [jnp.int32(0)]
    half = lax.axis_index("pair") % 2
    partner = [(p, p ^ 1) for p in range(pair_count)]
    blocks, owners = [], []
    for even, odd in ((4, 5), (6, 7), (2, 3), (0, 1)):
        route = [
            ((w ^ d) * pair_count + p, w * pair_count + p)
            for w in range(wide_count)
            for p in range(pair_count)
            for d in (odd if p % 2 else even,)
            if d
        ]
        fetched = lax.ppermute(block, ("wide", "pair"), route)
        blocks += [fetched, lax.ppermute(fetched, "pair", partner)]
        owners += [here ^ jnp.where(half == 0, even, odd), here ^ jnp.where(half == 0, odd, even)]
    return blocks + [block], owners + [here]


def local(three_center, occ_green, virt_green, occ_column, partner_live):
    local_atoms, block_size, wide_row = three_center.shape
    own_units = occ_green.shape[1]
    aux_count = wide_row // block_size
    wide_count, pair_count = lax.axis_size("wide"), lax.axis_size("pair")
    unit_count = 2 * own_units
    _, column_at, lanes = small_layout(unit_count, block_size)
    pair_at = lax.axis_index("pair")
    half = pair_at % 2
    partner = [(p, p ^ 1) for p in range(pair_count)]

    block, small = pl.pallas_call(
        pack_kernel,
        out_shape=(
            jax.ShapeDtypeStruct((local_atoms, block_size, wide_row + lanes), BF16),
            jax.ShapeDtypeStruct((local_atoms, block_size, lanes), BF16),
        ),
        in_specs=[SMEM, SMEM, SMEM, VMEM, VMEM, VMEM],
        out_specs=(VMEM, VMEM),
        name="pack",
    )(half.reshape(1), occ_column, partner_live, three_center, occ_green, virt_green)
    merged = small + lax.ppermute(small, "pair", partner)
    block = lax.dynamic_update_slice(block, merged, (0, 0, wide_row))
    blocks, owners = gather_over_wide(block, wide_count, pair_count)
    starts = jnp.stack([owner * local_atoms for owner in owners]).astype(jnp.int32)
    place = jnp.stack([lax.axis_index("wide"), half, pair_at // 2]).astype(jnp.int32)

    atom_total = wide_count * local_atoms
    own_atoms = atom_total // 2
    index_lanes = lanes - column_at // 128 * 128
    row_count = aux_count // pair_count
    part = jax.ShapeDtypeStruct((2, row_count, aux_count), F32)
    keep, send = pl.pallas_call(
        functools.partial(response_kernel, wide_count, unit_count),
        out_shape=(part, part),
        in_specs=[SMEM, SMEM] + [VMEM] * len(blocks),
        out_specs=(VMEM, VMEM),
        scratch_shapes=[
            pltpu.VMEM((atom_total, block_size * block_size, aux_count), BF16),
            pltpu.VMEM((atom_total, block_size, lanes), BF16),
            pltpu.VMEM((own_atoms, 1, index_lanes), jnp.int32),
            pltpu.SMEM((own_atoms, 1, index_lanes), jnp.int32),
            pltpu.SemaphoreType.DMA,
        ],
        compiler_params=pltpu.CompilerParams(vmem_limit_bytes=56 * 2**20),
        name="response",
    )(starts, place, *blocks)
    summed = keep + lax.ppermute(send, "pair", partner)
    other = [(p, p ^ 2) for p in range(pair_count)]
    return summed[0] + lax.ppermute(summed[1], "pair", other)


def solution(mesh):
    placed = (
        P("wide", None, None),
        P("wide", "pair", None, None),
        P("wide", "pair", None, None),
        P("wide", "pair"),
        P("wide", "pair"),
    )
    return jax.shard_map(
        local, mesh=mesh, in_specs=placed, out_specs=P("pair", None), check_vma=False
    )
```

time: 169 us -> 36.4 us (0.22)
  waiting for transfers between devices: 115 us -> 6.94 us
  blocking collectives: 20.9 us -> 0 us
  between operations: 13.5 us -> 0.07 us
  starting transfers between devices: 7.45 us -> 15 us
  Pallas kernels: 0 us -> 7.08 us
  local copies, waits for them, and re-layouts: 6.76 us -> 3.7 us
  matrix products: 2.35 us -> 0 us
  other arithmetic: 1.52 us -> 3.27 us
    psum x1 -> x0, waiting for transfers between devices: 115 us -> none  [local(): total = lax.psum(response_part, ('wide', 'pair'))]
    all_gather x1 -> x0, blocking collectives: 20.9 us -> none  [local(): lax.all_gather(occ_column, 'wide', axis=0, tiled=True)]
    ppermute x0 -> x11, starting transfers between devices: none -> 15 us  [the longest x4 6.71 us: gather_over_wide(): blocks += [fetched, lax.ppermute(fetched, 'pair', partner)]]
    all_to_all x1 -> x0, starting transfers between devices: 7.42 us -> none  [local(): lax.all_to_all(outgoing.reshape(wide_count, CAP, block_size, wide_row), '...]
    pallas_call x0 -> x2, Pallas kernels: none -> 7.08 us  [the longest x1 5.44 us: local(): pl.pallas_call(functools.partial(response_kernel, wide_count, unit_count)...]
    ppermute x0 -> x11, waiting for transfers between devices: none -> 6.94 us  [the longest x1 2.25 us: local(): return summed[0] + lax.ppermute(summed[1], 'pair', other)]
    dot_general x4 -> x0, matrix products: 2.35 us -> none  [the longest x1 1.06 us: local(): jnp.einsum('amnl,anx->amlx', occ_green, three_center, preferred_element_t...]
    scatter x1 -> x0, local copies, waits for them, and re-layouts: 2.07 us -> none  [local(): jnp.zeros((slot_total, block_size, wide_row), jnp.bfloat16).at[position]]
  transfers between devices with their start and end apart: 2 -> 11, of which waited for: 1 -> 6; matrix products, arithmetic and copies ran while one was open for 1% -> 4% of each run, Pallas kernels for 0% -> 0%
where the time goes in v1:
time: 36.4 us; the launch traced here: 36 us
  starting transfers between devices  15 us (41%)
  Pallas kernels  7.08 us (19%)
  waiting for transfers between devices  6.94 us (19%)
  local copies, waits for them, and re-layouts  3.7 us (10%)
  other arithmetic  3.27 us (9%)
    ppermute x4, starting transfers between devices, gather_over_wide(): blocks += [fetched, lax.ppermute(fetched, 'pair', partner)]  6.71 us
    ppermute x4, starting transfers between devices, gather_over_wide(): fetched = lax.ppermute(block, ('wide', 'pair'), route)  6.23 us
    pallas_call x1, Pallas kernels, local(): pl.pallas_call(functools.partial(response_kernel, wide_count, unit_count)...  5.44 us
    unnamed x22, local copies, waits for them, and re-layouts  3.04 us
    ppermute x1, waiting for transfers between devices, local(): return summed[0] + lax.ppermute(summed[1], 'pair', other)  2.25 us
    ppermute x4, waiting for transfers between devices, gather_over_wide(): fetched = lax.ppermute(block, ('wide', 'pair'), route)  1.98 us
    pallas_call x1, Pallas kernels, local(): pl.pallas_call(pack_kernel, out_shape=(jax.ShapeDtypeStruct((local_atoms,...  1.64 us
    ppermute x1, starting transfers between devices, local(): return summed[0] + lax.ppermute(summed[1], 'pair', other)  1.49 us
  transfers between devices with their start and end apart: 11, of which 6 were waited for; matrix products, arithmetic and copies ran while one was open for 4% of the time, Pallas kernels for 0%

profile of v1, /device:TPU:0, one launch (start us, length us, event | category | flops | bytes accessed | tf_op | source)
XLA Modules:
  0.0 36.0 jit_solution(12461122745565390682)
XLA Ops:
  0.0 0.7 %copy-done.8 = s32[4,2]{0,1:T(2,128)S(1)} copy-done((s32[4,2]{0,1:T(2,128)S(1)}, s32[4,2]{0,1:T(2,128)}, u32[]{:S(2)}) %copy-start.8) | copy-done | bytes 56
  0.7 0.7 %copy.6.column_ref = s32[4,2]{1,0:T(4,128)} copy(s32[4,2]{0,1:T(2,128)S(1)} %copy-done.8) | data formatting | bytes 64 | tf_op args[3]
  1.4 0.7 %copy.7.live_ref = s32[4,2]{1,0:T(4,128)} copy(s32[4,2]{0,1:T(2,128)S(1)} %copy-done.9) | data formatting | bytes 64 | tf_op args[4]
  2.0 1.6 %pack.1 = (bf16[4,8,1152]{2,1,0:T(8,128)(2,1)}, bf16[4,8,128]{2,1,0:T(8,128)(2,1)}) custom-call(s32[1]{0:T(128)} %bitcast.10.half_ref, s32[4,2]{1,0:T(4,128)} %copy.6.column_ref, s32[4,2]{1,0:T(4,128)} %copy.7.live_ref, bf16[4,8,1024]{2,1,0:T(8,128)(2,1)} %tc_ref.1, bf16[4,2,8,8]{3,2,1,0:T(8,128)(2,1)} %occ_ref.1, bf16[4,2,8,8]{3,2,1,0:T(8,128)(2,1)} %virt_ref.1), custom_call_target="tpu_custom_call" | custom-call | tf_op jit(solution)/shard_map/pack/pallas_call | solution.py:235
  3.7 0.5 %collective-permute-start = (bf16[4,8,128]{2,1,0:T(8,128)(2,1)}, bf16[4,8,128]{2,1,0:T(8,128)(2,1)S(1)}, u32[]{:S(2)}, u32[]{:S(2)}) collective-permute-start(bf16[4,8,128]{2,1,0:T(8,128)(2,1)} %get-tuple-element.10), channel_id=1, source_target_pairs={{0,1},{1,0},{2,3},{3,2},{4,5},{5,4},{6,7},{7,6},{8,9},{9,8},{10,11... | collective-permute-start | bytes 24584 | tf_op jit(solution)/shard_map/ppermute | solution.py:245
  4.1 1.0 %collective-permute-done = bf16[4,8,128]{2,1,0:T(8,128)(2,1)S(1)} collective-permute-done((bf16[4,8,128]{2,1,0:T(8,128)(2,1)}, bf16[4,8,128]{2,1,0:T(8,128)(2,1)S(1)}, u32[]{:S(2)}, u32[]{:S(2)}) %collective-permute-start) | collective-permute-done | bytes 8224 | tf_op jit(solution)/shard_map/ppermute | solution.py:245
  5.2 1.3 %add_dynamic-update-slice_fusion.refs_8_ = bf16[4,8,1152]{2,1,0:T(8,128)(2,1)} fusion(bf16[4,8,1152]{2,1,0:T(8,128)(2,1)} %get-tuple-element.9, bf16[4,8,128]{2,1,0:T(8,128)(2,1)} %get-tuple-element.10, bf16[4,8,128]{2,1,0:T(8,128)(2,1)S(1)} %collective-permute-done), kind=kLoop, calls=%fused_computation.3 | loop fusion | flops 16384 | bytes 24576 | tf_op jit(solution)/shard_map/dynamic_update_slice | solution.py:246
  6.5 0.7 %collective-permute-start.7 = (bf16[4,8,1152]{2,1,0:T(8,128)(2,1)}, bf16[4,8,1152]{2,1,0:T(8,128)(2,1)S(1)}, u32[]{:S(2)}, u32[]{:S(2)}) collective-permute-start(bf16[4,8,1152]{2,1,0:T(8,128)(2,1)} %add_dynamic-update-slice_fusion.refs_8_), channel_id=1, source_target_pairs={{5,1},{7,3},{1,5},{3,7},{13,9},{15,11},{9,13},{11,15},{21,17},{23,... | collective-permute-start | bytes 221192 | tf_op jit(solution)/shard_map/ppermute | solution.py:218
  7.1 3.0 %collective-permute-start.5 = (bf16[4,8,1152]{2,1,0:T(8,128)(2,1)}, bf16[4,8,1152]{2,1,0:T(8,128)(2,1)S(1)}, u32[]{:S(2)}, u32[]{:S(2)}) collective-permute-start(bf16[4,8,1152]{2,1,0:T(8,128)(2,1)} %add_dynamic-update-slice_fusion.refs_8_), channel_id=1, source_target_pairs={{8,0},{13,1},{10,2},{15,3},{12,4},{9,5},{14,6},{11,7},{0,8},{5,9},... | collective-permute-start | bytes 221192 | tf_op jit(solution)/shard_map/ppermute | solution.py:218
  10.1 2.5 %collective-permute-start.3 = (bf16[4,8,1152]{2,1,0:T(8,128)(2,1)}, bf16[4,8,1152]{2,1,0:T(8,128)(2,1)S(1)}, u32[]{:S(2)}, u32[]{:S(2)}) collective-permute-start(bf16[4,8,1152]{2,1,0:T(8,128)(2,1)} %add_dynamic-update-slice_fusion.refs_8_), channel_id=1, source_target_pairs={{24,0},{29,1},{26,2},{31,3},{28,4},{25,5},{30,6},{27,7},{16,8},{21... | collective-permute-start | bytes 221192 | tf_op jit(solution)/shard_map/ppermute | solution.py:218
  12.7 0.7 %stack.51.starts_ref = s32[9]{0:T(128)} concatenate(s32[1]{0:T(128)} %bitcast, s32[1]{0:T(128)} %bitcast.1, s32[1]{0:T(128)} %bitcast.2, s32[1]{0:T(128)} %bitcast.3, s32[1]{0:T(128)} %bitcast.4, s32[1]{0:T(128)} %bitcast.5, s32[1]{0:T(128)} %bitcast.6, s32[1]{0:T(128)} %bitcast.7, s32[1]{0:T(128)} %bitcast.8), dimensions={0} | concatenate | bytes 72 | tf_op jit(solution)/shard_map/stack | solution.py:248
  13.4 3.0 %collective-permute-start.8 = (bf16[4,8,1152]{2,1,0:T(8,128)(2,1)S(1)}, bf16[4,8,1152]{2,1,0:T(8,128)(2,1)S(1)}, u32[]{:S(2)}, u32[]{:S(2)}) collective-permute-start(bf16[4,8,1152]{2,1,0:T(8,128)(2,1)S(1)} %collective-permute-done.7.refs_6_), channel_id=1, source_target_pairs={{0,1},{1,0},{2,3},{3,2},{4,5},{5,4},{6,7},{7,6},{8,9},{9,8},{10,11... | collective-permute-start | bytes 221192 | tf_op jit(solution)/shard_map/ppermute | solution.py:219
  16.4 0.5 %collective-permute-done.3.refs_2_ = bf16[4,8,1152]{2,1,0:T(8,128)(2,1)S(1)} collective-permute-done((bf16[4,8,1152]{2,1,0:T(8,128)(2,1)}, bf16[4,8,1152]{2,1,0:T(8,128)(2,1)S(1)}, u32[]{:S(2)}, u32[]{:S(2)}) %collective-permute-start.3) | collective-permute-done | bytes 73760 | tf_op jit(solution)/shard_map/ppermute | solution.py:218
  17.0 2.6 %collective-permute-start.4 = (bf16[4,8,1152]{2,1,0:T(8,128)(2,1)S(1)}, bf16[4,8,1152]{2,1,0:T(8,128)(2,1)S(1)}, u32[]{:S(2)}, u32[]{:S(2)}) collective-permute-start(bf16[4,8,1152]{2,1,0:T(8,128)(2,1)S(1)} %collective-permute-done.3.refs_2_), channel_id=1, source_target_pairs={{0,1},{1,0},{2,3},{3,2},{4,5},{5,4},{6,7},{7,6},{8,9},{9,8},{10,11... | collective-permute-start | bytes 221192 | tf_op jit(solution)/shard_map/ppermute | solution.py:219
  19.5 1.4 %collective-permute-done.1.refs_0_ = bf16[4,8,1152]{2,1,0:T(8,128)(2,1)S(1)} collective-permute-done((bf16[4,8,1152]{2,1,0:T(8,128)(2,1)}, bf16[4,8,1152]{2,1,0:T(8,128)(2,1)S(1)}, u32[]{:S(2)}, u32[]{:S(2)}) %collective-permute-start.1) | collective-permute-done | bytes 73760 | tf_op jit(solution)/shard_map/ppermute | solution.py:218
  21.0 1.1 %collective-permute-start.2 = (bf16[4,8,1152]{2,1,0:T(8,128)(2,1)S(1)}, bf16[4,8,1152]{2,1,0:T(8,128)(2,1)S(1)}, u32[]{:S(2)}, u32[]{:S(2)}) collective-permute-start(bf16[4,8,1152]{2,1,0:T(8,128)(2,1)S(1)} %collective-permute-done.1.refs_0_), channel_id=1, source_target_pairs={{0,1},{1,0},{2,3},{3,2},{4,5},{5,4},{6,7},{7,6},{8,9},{9,8},{10,11... | collective-permute-start | bytes 221192 | tf_op jit(solution)/shard_map/ppermute | solution.py:219
  22.1 0.6 %pad_add_fusion.place_ref = s32[3]{0:T(128)} fusion(s32[1]{0:T(128)} %bitcast.11, s32[1]{0:T(128)} %bitcast.10.half_ref, s32[1]{0:T(128)} %bitcast.9), kind=kLoop, calls=%fused_computation.4 | loop fusion | flops 6 | bytes 24 | tf_op jit(solution)/shard_map/stack | solution.py:249
  23.4 0.6 %copy-done.7 = bf16[4,8,1152]{2,1,0:T(8,128)(2,1)} copy-done((bf16[4,8,1152]{2,1,0:T(8,128)(2,1)}, bf16[4,8,1152]{2,1,0:T(8,128)(2,1)S(1)}, u32[]{:S(2)}) %copy-start.7) | copy-done | bytes 73752
  24.0 5.4 %response.1 = (f32[2,32,128]{2,1,0:T(8,128)}, f32[2,32,128]{2,1,0:T(8,128)}) custom-call(s32[9]{0:T(128)} %stack.51.starts_ref, s32[3]{0:T(128)} %pad_add_fusion.place_ref, bf16[4,8,1152]{2,1,0:T(8,128)(2,1)} %copy-done.3, bf16[4,8,1152]{2,1,0:T(8,128)(2,1)} %copy-done.7, bf16[4,8,1152]{2,1,0:T(8,128)(2,1)} %copy-done.2, bf16[4,8,1152]{2,1,0:T(8,128)(2,1)} %copy-done.6, ...), custom_call_target="tpu_custom_call" | custom-call | tf_op jit(solution)/shard_map/response/pallas_call | solution.py:256
  29.5 1.4 %collective-permute-done.9 = f32[2,32,128]{2,1,0:T(8,128)S(1)} collective-permute-done((f32[2,32,128]{2,1,0:T(8,128)}, f32[2,32,128]{2,1,0:T(8,128)S(1)}, u32[]{:S(2)}, u32[]{:S(2)}) %collective-permute-start.9) | collective-permute-done | bytes 32800 | tf_op jit(solution)/shard_map/ppermute | solution.py:271
  30.9 0.8 %add.17 = f32[2,32,128]{2,1,0:T(8,128)S(1)} add(f32[2,32,128]{2,1,0:T(8,128)} %get-tuple-element.11, f32[2,32,128]{2,1,0:T(8,128)S(1)} %collective-permute-done.9) | non-fusion elementwise | flops 8192 | bytes 98304 | tf_op jit(solution)/shard_map/add | solution.py:271
  31.7 1.5 %collective-permute-start.10 = (f32[32,128]{1,0:T(8,128)S(1)}, f32[32,128]{1,0:T(8,128)S(1)}, u32[]{:S(2)}, u32[]{:S(2)}) collective-permute-start(f32[32,128]{1,0:T(8,128)S(1)} %slice_bitcast_fusion), channel_id=1, source_target_pairs={{0,2},{1,3},{2,0},{3,1},{4,6},{5,7},{6,4},{7,5},{8,10},{9,11},{10,... | collective-permute-start | bytes 49160 | tf_op jit(solution)/shard_map/ppermute | solution.py:273
  33.2 2.2 %collective-permute-done.10 = f32[32,128]{1,0:T(8,128)S(1)} collective-permute-done((f32[32,128]{1,0:T(8,128)S(1)}, f32[32,128]{1,0:T(8,128)S(1)}, u32[]{:S(2)}, u32[]{:S(2)}) %collective-permute-start.10) | collective-permute-done | bytes 16416 | tf_op jit(solution)/shard_map/ppermute | solution.py:273
  35.4 0.6 %fusion = f32[32,128]{1,0:T(8,128)} fusion(f32[32,128]{1,0:T(8,128)S(1)} %collective-permute-done.10, f32[2,32,128]{2,1,0:T(8,128)S(1)} %add.17), kind=kLoop, calls=%fused_computation.2 | loop fusion | flops 4096 | bytes 49152 | tf_op jit(solution)/shard_map/add | solution.py:273
  (28 shorter events, 1.0 us)
Async XLA Ops:
  0.0 0.7 %copy-start.8 = (s32[4,2]{0,1:T(2,128)S(1)}, s32[4,2]{0,1:T(2,128)}, u32[]{:S(2)}) copy-start(s32[4,2]{0,1:T(2,128)} %param.8) | copy-start | bytes 100
  0.7 0.7 %copy-start.9 = (s32[4,2]{0,1:T(2,128)S(1)}, s32[4,2]{0,1:T(2,128)}, u32[]{:S(2)}) copy-start(s32[4,2]{0,1:T(2,128)} %param.9) | copy-start | bytes 100
  3.7 1.5 %collective-permute-start = (bf16[4,8,128]{2,1,0:T(8,128)(2,1)}, bf16[4,8,128]{2,1,0:T(8,128)(2,1)S(1)}, u32[]{:S(2)}, u32[]{:S(2)}) collective-permute-start(bf16[4,8,128]{2,1,0:T(8,128)(2,1)} %get-tuple-element.10), channel_id=1, source_target_pairs={{0,1},{1,0},{2,3},{3,2},{4,5},{5,4},{6,7},{7,6},{8,9},{9,8},{10,11... | collective-permute-start | bytes 24584 | tf_op jit(solution)/shard_map/ppermute | solution.py:245
  6.5 6.9 %collective-permute-start.7 = (bf16[4,8,1152]{2,1,0:T(8,128)(2,1)}, bf16[4,8,1152]{2,1,0:T(8,128)(2,1)S(1)}, u32[]{:S(2)}, u32[]{:S(2)}) collective-permute-start(bf16[4,8,1152]{2,1,0:T(8,128)(2,1)} %add_dynamic-update-slice_fusion.refs_8_), channel_id=1, source_target_pairs={{5,1},{7,3},{1,5},{3,7},{13,9},{15,11},{9,13},{11,15},{21,17},{23,... | collective-permute-start | bytes 221192 | tf_op jit(solution)/shard_map/ppermute | solution.py:218
  7.1 9.2 %collective-permute-start.5 = (bf16[4,8,1152]{2,1,0:T(8,128)(2,1)}, bf16[4,8,1152]{2,1,0:T(8,128)(2,1)S(1)}, u32[]{:S(2)}, u32[]{:S(2)}) collective-permute-start(bf16[4,8,1152]{2,1,0:T(8,128)(2,1)} %add_dynamic-update-slice_fusion.refs_8_), channel_id=1, source_target_pairs={{8,0},{13,1},{10,2},{15,3},{12,4},{9,5},{14,6},{11,7},{0,8},{5,9},... | collective-permute-start | bytes 221192 | tf_op jit(solution)/shard_map/ppermute | solution.py:218
  10.1 6.9 %collective-permute-start.3 = (bf16[4,8,1152]{2,1,0:T(8,128)(2,1)}, bf16[4,8,1152]{2,1,0:T(8,128)(2,1)S(1)}, u32[]{:S(2)}, u32[]{:S(2)}) collective-permute-start(bf16[4,8,1152]{2,1,0:T(8,128)(2,1)} %add_dynamic-update-slice_fusion.refs_8_), channel_id=1, source_target_pairs={{24,0},{29,1},{26,2},{31,3},{28,4},{25,5},{30,6},{27,7},{16,8},{21... | collective-permute-start | bytes 221192 | tf_op jit(solution)/shard_map/ppermute | solution.py:218
  12.6 8.4 %collective-permute-start.1 = (bf16[4,8,1152]{2,1,0:T(8,128)(2,1)}, bf16[4,8,1152]{2,1,0:T(8,128)(2,1)S(1)}, u32[]{:S(2)}, u32[]{:S(2)}) collective-permute-start(bf16[4,8,1152]{2,1,0:T(8,128)(2,1)} %add_dynamic-update-slice_fusion.refs_8_), channel_id=1, source_target_pairs={{16,0},{21,1},{18,2},{23,3},{20,4},{17,5},{22,6},{19,7},{24,8},{29... | collective-permute-start | bytes 221192 | tf_op jit(solution)/shard_map/ppermute | solution.py:218
  13.4 9.6 %copy-start = (bf16[4,8,1152]{2,1,0:T(8,128)(2,1)}, bf16[4,8,1152]{2,1,0:T(8,128)(2,1)S(1)}, u32[]{:S(2)}) copy-start(bf16[4,8,1152]{2,1,0:T(8,128)(2,1)S(1)} %collective-permute-done.7.refs_6_) | copy-start | bytes 221188
  13.4 9.3 %collective-permute-start.8 = (bf16[4,8,1152]{2,1,0:T(8,128)(2,1)S(1)}, bf16[4,8,1152]{2,1,0:T(8,128)(2,1)S(1)}, u32[]{:S(2)}, u32[]{:S(2)}) collective-permute-start(bf16[4,8,1152]{2,1,0:T(8,128)(2,1)S(1)} %collective-permute-done.7.refs_6_), channel_id=1, source_target_pairs={{0,1},{1,0},{2,3},{3,2},{4,5},{5,4},{6,7},{7,6},{8,9},{9,8},{10,11... | collective-permute-start | bytes 221192 | tf_op jit(solution)/shard_map/ppermute | solution.py:219
  16.3 6.6 %copy-start.1 = (bf16[4,8,1152]{2,1,0:T(8,128)(2,1)}, bf16[4,8,1152]{2,1,0:T(8,128)(2,1)S(1)}, u32[]{:S(2)}) copy-start(bf16[4,8,1152]{2,1,0:T(8,128)(2,1)S(1)} %collective-permute-done.5.refs_4_) | copy-start | bytes 221188
  16.3 6.3 %collective-permute-start.6 = (bf16[4,8,1152]{2,1,0:T(8,128)(2,1)S(1)}, bf16[4,8,1152]{2,1,0:T(8,128)(2,1)S(1)}, u32[]{:S(2)}, u32[]{:S(2)}) collective-permute-start(bf16[4,8,1152]{2,1,0:T(8,128)(2,1)S(1)} %collective-permute-done.5.refs_4_), channel_id=1, source_target_pairs={{0,1},{1,0},{2,3},{3,2},{4,5},{5,4},{6,7},{7,6},{8,9},{9,8},{10,11... | collective-permute-start | bytes 221192 | tf_op jit(solution)/shard_map/ppermute | solution.py:219
  17.0 6.0 %copy-start.2 = (bf16[4,8,1152]{2,1,0:T(8,128)(2,1)}, bf16[4,8,1152]{2,1,0:T(8,128)(2,1)S(1)}, u32[]{:S(2)}) copy-start(bf16[4,8,1152]{2,1,0:T(8,128)(2,1)S(1)} %collective-permute-done.3.refs_2_) | copy-start | bytes 221188
  17.0 5.7 %collective-permute-start.4 = (bf16[4,8,1152]{2,1,0:T(8,128)(2,1)S(1)}, bf16[4,8,1152]{2,1,0:T(8,128)(2,1)S(1)}, u32[]{:S(2)}, u32[]{:S(2)}) collective-permute-start(bf16[4,8,1152]{2,1,0:T(8,128)(2,1)S(1)} %collective-permute-done.3.refs_2_), channel_id=1, source_target_pairs={{0,1},{1,0},{2,3},{3,2},{4,5},{5,4},{6,7},{7,6},{8,9},{9,8},{10,11... | collective-permute-start | bytes 221192 | tf_op jit(solution)/shard_map/ppermute | solution.py:219
  21.0 2.0 %copy-start.3 = (bf16[4,8,1152]{2,1,0:T(8,128)(2,1)}, bf16[4,8,1152]{2,1,0:T(8,128)(2,1)S(1)}, u32[]{:S(2)}) copy-start(bf16[4,8,1152]{2,1,0:T(8,128)(2,1)S(1)} %collective-permute-done.1.refs_0_) | copy-start | bytes 221188
  21.0 2.0 %collective-permute-start.2 = (bf16[4,8,1152]{2,1,0:T(8,128)(2,1)S(1)}, bf16[4,8,1152]{2,1,0:T(8,128)(2,1)S(1)}, u32[]{:S(2)}, u32[]{:S(2)}) collective-permute-start(bf16[4,8,1152]{2,1,0:T(8,128)(2,1)S(1)} %collective-permute-done.1.refs_0_), channel_id=1, source_target_pairs={{0,1},{1,0},{2,3},{3,2},{4,5},{5,4},{6,7},{7,6},{8,9},{9,8},{10,11... | collective-permute-start | bytes 221192 | tf_op jit(solution)/shard_map/ppermute | solution.py:219
  22.7 0.6 %copy-start.4 = (bf16[4,8,1152]{2,1,0:T(8,128)(2,1)}, bf16[4,8,1152]{2,1,0:T(8,128)(2,1)S(1)}, u32[]{:S(2)}) copy-start(bf16[4,8,1152]{2,1,0:T(8,128)(2,1)S(1)} %collective-permute-done.8.refs_7_) | copy-start | bytes 221188
  22.7 0.6 %copy-start.5 = (bf16[4,8,1152]{2,1,0:T(8,128)(2,1)}, bf16[4,8,1152]{2,1,0:T(8,128)(2,1)S(1)}, u32[]{:S(2)}) copy-start(bf16[4,8,1152]{2,1,0:T(8,128)(2,1)S(1)} %collective-permute-done.6.refs_5_) | copy-start | bytes 221188
  22.7 0.7 %copy-start.6 = (bf16[4,8,1152]{2,1,0:T(8,128)(2,1)}, bf16[4,8,1152]{2,1,0:T(8,128)(2,1)S(1)}, u32[]{:S(2)}) copy-start(bf16[4,8,1152]{2,1,0:T(8,128)(2,1)S(1)} %collective-permute-done.4.refs_3_) | copy-start | bytes 221188
  23.4 0.6 %copy-start.7 = (bf16[4,8,1152]{2,1,0:T(8,128)(2,1)}, bf16[4,8,1152]{2,1,0:T(8,128)(2,1)S(1)}, u32[]{:S(2)}) copy-start(bf16[4,8,1152]{2,1,0:T(8,128)(2,1)S(1)} %collective-permute-done.2.refs_1_) | copy-start | bytes 221188
  29.4 1.5 %collective-permute-start.9 = (f32[2,32,128]{2,1,0:T(8,128)}, f32[2,32,128]{2,1,0:T(8,128)S(1)}, u32[]{:S(2)}, u32[]{:S(2)}) collective-permute-start(f32[2,32,128]{2,1,0:T(8,128)} %get-tuple-element.12), channel_id=1, source_target_pairs={{0,1},{1,0},{2,3},{3,2},{4,5},{5,4},{6,7},{7,6},{8,9},{9,8},{10,11... | collective-permute-start | bytes 98312 | tf_op jit(solution)/shard_map/ppermute | solution.py:271
  31.7 3.7 %collective-permute-start.10 = (f32[32,128]{1,0:T(8,128)S(1)}, f32[32,128]{1,0:T(8,128)S(1)}, u32[]{:S(2)}, u32[]{:S(2)}) collective-permute-start(f32[32,128]{1,0:T(8,128)S(1)} %slice_bitcast_fusion), channel_id=1, source_target_pairs={{0,2},{1,3},{2,0},{3,1},{4,6},{5,7},{6,4},{7,5},{8,10},{9,11},{10,... | collective-permute-start | bytes 49160 | tf_op jit(solution)/shard_map/ppermute | solution.py:273

commit v2 on v1

--- a/solution.py
+++ b/solution.py
@@ -26,12 +26,12 @@
     return lax.broadcasted_iota(jnp.int32, shape, axis)
 
 
-def pack_kernel(half_ref, column_ref, live_ref, tc_ref, occ_ref, virt_ref, block_ref, small_ref):
+def pack_kernel(pair_ref, column_ref, live_ref, tc_ref, occ_ref, virt_ref, block_ref, small_ref):
     local_atoms, own_units, block_size, _ = occ_ref.shape
     wide_row = tc_ref.shape[2]
     unit_count = 2 * own_units
     _, column_at, lanes = small_layout(unit_count, block_size)
-    half = half_ref[0]
+    half = pair_ref[0] % 2
     row, lane = iota((block_size, lanes), 0), iota((block_size, lanes), 1)
     packed = jnp.zeros((local_atoms * block_size, lanes), F32)
     columns = [jnp.zeros((block_size, lanes), F32) for _ in range(local_atoms)]
@@ -40,7 +40,7 @@
         at = (unit // CHUNK) * (2 * CHUNK * block_size) + (unit % CHUNK) * block_size
         occ = jnp.concatenate(
             [
-                occ_ref[atom, slot].astype(F32) * live_ref[atom, slot].astype(F32)
+                occ_ref[atom, slot].astype(F32) * live_ref[slot, atom].astype(F32)
                 for atom in range(local_atoms)
             ],
             axis=0,
@@ -53,7 +53,7 @@
         packed += jnp.dot(occ, occ_place, preferred_element_type=F32)
         packed += jnp.dot(virt, virt_place, preferred_element_type=F32)
         for atom in range(local_atoms):
-            column = column_ref[atom, slot]
+            column = column_ref[slot, atom]
             high = column // BASE
             low = column - high * BASE
             columns[atom] += jnp.where(lane == column_at + unit, high.astype(F32), 0.0)
@@ -67,9 +67,7 @@
     small_ref[...] = packed
 
 
-def response_kernel(
-    wide_count, unit_count, starts_ref, place_ref, *refs
-):
+def response_kernel(wide_count, unit_count, offsets, wide_ref, pair_ref, *refs):
     block_refs = refs[: -7]
     keep_ref, send_ref, rows_ref, small_ref, index_ref, column_ref, sem = refs[-7:]
     block_size = block_refs[0].shape[1]
@@ -78,10 +76,13 @@
     chunk_count, column_at, lanes = small_layout(unit_count, block_size)
     atom_total = rows_ref.shape[0]
     local_atoms = atom_total // wide_count
-    side, half = place_ref[0], place_ref[1]
+    side, half, outer = wide_ref[0], pair_ref[0] % 2, pair_ref[0] // 2
 
     for number, block_ref in enumerate(block_refs):
-        first = starts_ref[number]
+        first = 0
+        if offsets[number] is not None:
+            even, odd = offsets[number]
+            first = (side ^ jnp.where(half == 0, even, odd)) * local_atoms
 
         def place_atom(atom, block_ref=block_ref, first=first):
             rows_ref[first + atom] = jnp.concatenate(
@@ -189,7 +190,6 @@
     parts = [total[at * row_count : (at + 1) * row_count] for at in range(4)]
     keep = [jnp.where(half == 0, parts[2 * at], parts[2 * at + 1]) for at in range(2)]
     send = [jnp.where(half == 0, parts[2 * at + 1], parts[2 * at]) for at in range(2)]
-    outer = place_ref[2]
     keep_ref[0] = jnp.where(outer == 0, keep[0], keep[1])
     keep_ref[1] = jnp.where(outer == 0, keep[1], keep[0])
     send_ref[0] = jnp.where(outer == 0, send[0], send[1])
@@ -200,13 +200,15 @@
 SMEM = pl.BlockSpec(memory_space=pltpu.SMEM)
 
 
+def scalar(value):
+    return value.astype(jnp.int32).reshape(1)
+
+
 def gather_over_wide(block, wide_count, pair_count):
-    here = lax.axis_index("wide")
     if wide_count != 8:
-        return [lax.all_gather(block, "wide", axis=0, tiled=True)], [jnp.int32(0)]
-    half = lax.axis_index("pair") % 2
+        return [lax.all_gather(block, "wide", axis=0, tiled=True)], (None,)
     partner = [(p, p ^ 1) for p in range(pair_count)]
-    blocks, owners = [], []
+    blocks, offsets = [], []
     for even, odd in ((4, 5), (6, 7), (2, 3), (0, 1)):
         route = [
             ((w ^ d) * pair_count + p, w * pair_count + p)
@@ -217,8 +219,8 @@
         ]
         fetched = lax.ppermute(block, ("wide", "pair"), route)
         blocks += [fetched, lax.ppermute(fetched, "pair", partner)]
-        owners += [here ^ jnp.where(half == 0, even, odd), here ^ jnp.where(half == 0, odd, even)]
-    return blocks + [block], owners + [here]
+        offsets += [(even, odd), (odd, even)]
+    return blocks + [block], tuple(offsets + [(0, 0)])
 
 
 def local(three_center, occ_green, virt_green, occ_column, partner_live):
@@ -228,33 +230,33 @@
     wide_count, pair_count = lax.axis_size("wide"), lax.axis_size("pair")
     unit_count = 2 * own_units
     _, column_at, lanes = small_layout(unit_count, block_size)
-    pair_at = lax.axis_index("pair")
-    half = pair_at % 2
+    wide_at = scalar(lax.axis_index("wide"))
+    pair_at = scalar(lax.axis_index("pair"))
     partner = [(p, p ^ 1) for p in range(pair_count)]
 
     block, small = pl.pallas_call(
         pack_kernel,
         out_shape=(
-            jax.ShapeDtypeStruct((local_atoms, block_size, wide_row + lanes), BF16),
-            jax.ShapeDtypeStruct((local_atoms, block_size, lanes), BF16),
+            pltpu.VMEM((local_atoms, block_size, wide_row + lanes), BF16),
+            pltpu.VMEM((local_atoms, block_size, lanes), BF16),
         ),
         in_specs=[SMEM, SMEM, SMEM, VMEM, VMEM, VMEM],
         out_specs=(VMEM, VMEM),
         name="pack",
-    )(half.reshape(1), occ_column, partner_live, three_center, occ_green, virt_green)
+    )(pair_at, occ_column.T, partner_live.T, three_center, occ_green, virt_green)
     merged = small + lax.ppermute(small, "pair", partner)
     block = lax.dynamic_update_slice(block, merged, (0, 0, wide_row))
-    blocks, owners = gather_over_wide(block, wide_count, pair_count)
-    starts = jnp.stack([owner * local_atoms for owner in owners]).astype(jnp.int32)
-    place = jnp.stack([lax.axis_index("wide"), half, pair_at // 2]).astype(jnp.int32)
+    blocks, offsets = gather_over_wide(block, wide_count, pair_count)
+    if wide_count == 8:
+        blocks = [pltpu.with_memory_space_constraint(block, pltpu.VMEM) for block in blocks]
 
     atom_total = wide_count * local_atoms
     own_atoms = atom_total // 2
     index_lanes = lanes - column_at // 128 * 128
     row_count = aux_count // pair_count
-    part = jax.ShapeDtypeStruct((2, row_count, aux_count), F32)
+    part = pltpu.VMEM((2, row_count, aux_count), F32)
     keep, send = pl.pallas_call(
-        functools.partial(response_kernel, wide_count, unit_count),
+        functools.partial(response_kernel, wide_count, unit_count, offsets),
         out_shape=(part, part),
         in_specs=[SMEM, SMEM] + [VMEM] * len(blocks),
         out_specs=(VMEM, VMEM),
@@ -267,7 +269,7 @@
         ],
         compiler_params=pltpu.CompilerParams(vmem_limit_bytes=56 * 2**20),
         name="response",
-    )(starts, place, *blocks)
+    )(wide_at, pair_at, *blocks)
     summed = keep + lax.ppermute(send, "pair", partner)
     other = [(p, p ^ 2) for p in range(pair_count)]
     return summed[0] + lax.ppermute(summed[1], "pair", other)

time: 36.4 us -> 28.2 us (0.77)
  local copies, waits for them, and re-layouts: 3.7 us -> 0.01 us
  other arithmetic: 3.27 us -> 0.63 us
  Pallas kernels: 7.08 us -> 4.66 us
  starting transfers between devices: 15 us -> 15.4 us
    unnamed x22 -> x0, local copies, waits for them, and re-layouts: 3.04 us -> none
    pallas_call x2, Pallas kernels: 7.08 us -> 4.66 us  [the longest x1 3.65 us: local(): pl.pallas_call(functools.partial(response_kernel, wide_count, unit_count,...]
    dynamic_update_slice x1, other arithmetic: 1.3 us -> 0.01 us  [local(): block = lax.dynamic_update_slice(block, merged, (0, 0, wide_row))]
    add x1, other arithmetic: 0.76 us -> 0.01 us  [local(): summed = keep + lax.ppermute(send, 'pair', partner)]
    another operation x1 -> x0, local copies, waits for them, and re-layouts: 0.66 us -> none  [local(): jnp.stack([owner * local_atoms for owner in owners]).astype(jnp.int32)]
    ppermute x4, waiting for transfers between devices: 0.28 us -> 0.91 us  [gather_over_wide(): blocks += [fetched, lax.ppermute(fetched, 'pair', partner)]]
    another operation x1 -> x0, other arithmetic: 0.6 us -> none  [local(): jnp.stack([lax.axis_index('wide'), half, pair_at // 2]).astype(jnp.int32)]
    ppermute x1, waiting for transfers between devices: 1.4 us -> 0.86 us  [local(): summed = keep + lax.ppermute(send, 'pair', partner)]
  transfers between devices with their start and end apart: 11 -> 11, of which waited for: 6 -> 6; matrix products, arithmetic and copies ran while one was open for 4% -> 0% of each run, Pallas kernels for 0% -> 0%
where the time goes in v2:
time: 28.2 us; the launch traced here: 28 us
  starting transfers between devices  15.4 us (55%)
  waiting for transfers between devices  7.27 us (26%)
  Pallas kernels  4.66 us (17%)
  other arithmetic  0.63 us (2%)
    ppermute x4, starting transfers between devices, gather_over_wide(): blocks += [fetched, lax.ppermute(fetched, 'pair', partner)]  6.71 us
    ppermute x4, starting transfers between devices, gather_over_wide(): fetched = lax.ppermute(block, ('wide', 'pair'), route)  6.23 us
    pallas_call x1, Pallas kernels, local(): pl.pallas_call(functools.partial(response_kernel, wide_count, unit_count,...  3.65 us
    ppermute x4, waiting for transfers between devices, gather_over_wide(): fetched = lax.ppermute(block, ('wide', 'pair'), route)  2.42 us
    ppermute x1, waiting for transfers between devices, local(): return summed[0] + lax.ppermute(summed[1], 'pair', other)  2.25 us
    ppermute x1, starting transfers between devices, local(): return summed[0] + lax.ppermute(summed[1], 'pair', other)  1.55 us
    pallas_call x1, Pallas kernels, local(): pl.pallas_call(pack_kernel, out_shape=(pltpu.VMEM((local_atoms, block_siz...  1.01 us
    ppermute x4, waiting for transfers between devices, gather_over_wide(): blocks += [fetched, lax.ppermute(fetched, 'pair', partner)]  0.91 us
  transfers between devices with their start and end apart: 11, of which 6 were waited for; matrix products, arithmetic and copies ran while one was open for 0% of the time, Pallas kernels for 0%

profile of v2, /device:TPU:0, one launch (start us, length us, event | category | flops | bytes accessed | tf_op | source)
XLA Modules:
  0.0 28.0 jit_solution(3310016967883625336)
XLA Ops:
  0.0 1.0 %pack.1 = (bf16[4,8,1152]{2,1,0:T(8,128)(2,1)S(1)}, bf16[4,8,128]{2,1,0:T(8,128)(2,1)S(1)}) custom-call(s32[1]{0:T(128)} %bitcast.1.pair_ref, s32[2,4]{1,0:T(2,128)} %bitcast.10, s32[2,4]{1,0:T(2,128)} %bitcast.11, bf16[4,8,1024]{2,1,0:T(8,128)(2,1)} %tc_ref.1, bf16[4,2,8,8]{3,2,1,0:T(8,128)(2,1)} %occ_ref.1, bf16[4,2,8,8]{3,2,1,0:T(8,128)(2,1)} %virt_ref.1), custom_call_target="tpu_custom_call" | custom-call | tf_op jit(solution)/shard_map/pack/pallas_call | solution.py:237
  1.0 0.5 %collective-permute-start = (bf16[4,8,128]{2,1,0:T(8,128)(2,1)S(1)}, bf16[4,8,128]{2,1,0:T(8,128)(2,1)S(1)}, u32[]{:S(2)}, u32[]{:S(2)}) collective-permute-start(bf16[4,8,128]{2,1,0:T(8,128)(2,1)S(1)} %get-tuple-element.10), channel_id=1, source_target_pairs={{0,1},{1,0},{2,3},{3,2},{4,5},{5,4},{6,7},{7,6},{8,9},{9,8},{10,11... | collective-permute-start | bytes 24584 | tf_op jit(solution)/shard_map/ppermute | solution.py:247
  1.5 0.8 %collective-permute-done = bf16[4,8,128]{2,1,0:T(8,128)(2,1)S(1)} collective-permute-done((bf16[4,8,128]{2,1,0:T(8,128)(2,1)S(1)}, bf16[4,8,128]{2,1,0:T(8,128)(2,1)S(1)}, u32[]{:S(2)}, u32[]{:S(2)}) %collective-permute-start) | collective-permute-done | bytes 8224 | tf_op jit(solution)/shard_map/ppermute | solution.py:247
  2.4 0.7 %collective-permute-start.7 = (bf16[4,8,1152]{2,1,0:T(8,128)(2,1)S(1)}, bf16[4,8,1152]{2,1,0:T(8,128)(2,1)S(1)}, u32[]{:S(2)}, u32[]{:S(2)}) collective-permute-start(bf16[4,8,1152]{2,1,0:T(8,128)(2,1)S(1)} %add_dynamic-update-slice_fusion.refs_8_), channel_id=1, source_target_pairs={{5,1},{7,3},{1,5},{3,7},{13,9},{15,11},{9,13},{11,15},{21,17},{23,... | collective-permute-start | bytes 221192 | tf_op jit(solution)/shard_map/ppermute | solution.py:220
  3.0 3.0 %collective-permute-start.5 = (bf16[4,8,1152]{2,1,0:T(8,128)(2,1)S(1)}, bf16[4,8,1152]{2,1,0:T(8,128)(2,1)S(1)}, u32[]{:S(2)}, u32[]{:S(2)}) collective-permute-start(bf16[4,8,1152]{2,1,0:T(8,128)(2,1)S(1)} %add_dynamic-update-slice_fusion.refs_8_), channel_id=1, source_target_pairs={{8,0},{13,1},{10,2},{15,3},{12,4},{9,5},{14,6},{11,7},{0,8},{5,9},... | collective-permute-start | bytes 221192 | tf_op jit(solution)/shard_map/ppermute | solution.py:220
  6.0 2.5 %collective-permute-start.3 = (bf16[4,8,1152]{2,1,0:T(8,128)(2,1)S(1)}, bf16[4,8,1152]{2,1,0:T(8,128)(2,1)S(1)}, u32[]{:S(2)}, u32[]{:S(2)}) collective-permute-start(bf16[4,8,1152]{2,1,0:T(8,128)(2,1)S(1)} %add_dynamic-update-slice_fusion.refs_8_), channel_id=1, source_target_pairs={{24,0},{29,1},{26,2},{31,3},{28,4},{25,5},{30,6},{27,7},{16,8},{21... | collective-permute-start | bytes 221192 | tf_op jit(solution)/shard_map/ppermute | solution.py:220
  8.5 0.1 collective-permute-start.1
  8.6 0.0 collective-permute-done.7.refs_6_
  8.6 3.0 %collective-permute-start.8 = (bf16[4,8,1152]{2,1,0:T(8,128)(2,1)S(1)}, bf16[4,8,1152]{2,1,0:T(8,128)(2,1)S(1)}, u32[]{:S(2)}, u32[]{:S(2)}) collective-permute-start(bf16[4,8,1152]{2,1,0:T(8,128)(2,1)S(1)} %collective-permute-done.7.refs_6_), channel_id=1, source_target_pairs={{0,1},{1,0},{2,3},{3,2},{4,5},{5,4},{6,7},{7,6},{8,9},{9,8},{10,11... | collective-permute-start | bytes 221192 | tf_op jit(solution)/shard_map/ppermute | solution.py:221
  11.6 0.0 collective-permute-done.5.refs_4_
  11.6 0.1 collective-permute-start.6
  11.7 1.0 %collective-permute-done.3.refs_2_ = bf16[4,8,1152]{2,1,0:T(8,128)(2,1)S(1)} collective-permute-done((bf16[4,8,1152]{2,1,0:T(8,128)(2,1)S(1)}, bf16[4,8,1152]{2,1,0:T(8,128)(2,1)S(1)}, u32[]{:S(2)}, u32[]{:S(2)}) %collective-permute-start.3) | collective-permute-done | bytes 73760 | tf_op jit(solution)/shard_map/ppermute | solution.py:220
  12.7 2.6 %collective-permute-start.4 = (bf16[4,8,1152]{2,1,0:T(8,128)(2,1)S(1)}, bf16[4,8,1152]{2,1,0:T(8,128)(2,1)S(1)}, u32[]{:S(2)}, u32[]{:S(2)}) collective-permute-start(bf16[4,8,1152]{2,1,0:T(8,128)(2,1)S(1)} %collective-permute-done.3.refs_2_), channel_id=1, source_target_pairs={{0,1},{1,0},{2,3},{3,2},{4,5},{5,4},{6,7},{7,6},{8,9},{9,8},{10,11... | collective-permute-start | bytes 221192 | tf_op jit(solution)/shard_map/ppermute | solution.py:221
  15.3 1.4 %collective-permute-done.1.refs_0_ = bf16[4,8,1152]{2,1,0:T(8,128)(2,1)S(1)} collective-permute-done((bf16[4,8,1152]{2,1,0:T(8,128)(2,1)S(1)}, bf16[4,8,1152]{2,1,0:T(8,128)(2,1)S(1)}, u32[]{:S(2)}, u32[]{:S(2)}) %collective-permute-start.1) | collective-permute-done | bytes 73760 | tf_op jit(solution)/shard_map/ppermute | solution.py:220
  16.7 1.1 %collective-permute-start.2 = (bf16[4,8,1152]{2,1,0:T(8,128)(2,1)S(1)}, bf16[4,8,1152]{2,1,0:T(8,128)(2,1)S(1)}, u32[]{:S(2)}, u32[]{:S(2)}) collective-permute-start(bf16[4,8,1152]{2,1,0:T(8,128)(2,1)S(1)} %collective-permute-done.1.refs_0_), channel_id=1, source_target_pairs={{0,1},{1,0},{2,3},{3,2},{4,5},{5,4},{6,7},{7,6},{8,9},{9,8},{10,11... | collective-permute-start | bytes 221192 | tf_op jit(solution)/shard_map/ppermute | solution.py:221
  17.7 0.0 collective-permute-done.8.refs_7_
  17.8 0.0 collective-permute-done.6.refs_5_
  17.8 0.9 %collective-permute-done.2.refs_1_ = bf16[4,8,1152]{2,1,0:T(8,128)(2,1)S(1)} collective-permute-done((bf16[4,8,1152]{2,1,0:T(8,128)(2,1)S(1)}, bf16[4,8,1152]{2,1,0:T(8,128)(2,1)S(1)}, u32[]{:S(2)}, u32[]{:S(2)}) %collective-permute-start.2) | collective-permute-done | bytes 73760 | tf_op jit(solution)/shard_map/ppermute | solution.py:221
  18.7 3.6 %response.1 = (f32[2,32,128]{2,1,0:T(8,128)S(1)}, f32[2,32,128]{2,1,0:T(8,128)S(1)}) custom-call(s32[1]{0:T(128)} %bitcast.wide_ref, s32[1]{0:T(128)} %bitcast.1.pair_ref, bf16[4,8,1152]{2,1,0:T(8,128)(2,1)S(1)} %collective-permute-done.1.refs_0_, bf16[4,8,1152]{2,1,0:T(8,128)(2,1)S(1)} %collective-permute-done.2.refs_1_, ...), custom_call_target="tpu_custom_call" | custom-call | tf_op jit(solution)/shard_map/response/pallas_call | solution.py:258
  22.3 0.4 %collective-permute-start.9 = (f32[2,32,128]{2,1,0:T(8,128)S(1)}, f32[2,32,128]{2,1,0:T(8,128)S(1)}, u32[]{:S(2)}, u32[]{:S(2)}) collective-permute-start(f32[2,32,128]{2,1,0:T(8,128)S(1)} %get-tuple-element.12), channel_id=1, source_target_pairs={{0,1},{1,0},{2,3},{3,2},{4,5},{5,4},{6,7},{7,6},{8,9},{9,8},{10,11... | collective-permute-start | bytes 98312 | tf_op jit(solution)/shard_map/ppermute | solution.py:273
  22.7 0.9 %collective-permute-done.9 = f32[2,32,128]{2,1,0:T(8,128)S(1)} collective-permute-done((f32[2,32,128]{2,1,0:T(8,128)S(1)}, f32[2,32,128]{2,1,0:T(8,128)S(1)}, u32[]{:S(2)}, u32[]{:S(2)}) %collective-permute-start.9) | collective-permute-done | bytes 32800 | tf_op jit(solution)/shard_map/ppermute | solution.py:273
  23.6 1.6 %collective-permute-start.10 = (f32[32,128]{1,0:T(8,128)S(1)}, f32[32,128]{1,0:T(8,128)S(1)}, u32[]{:S(2)}, u32[]{:S(2)}) collective-permute-start(f32[32,128]{1,0:T(8,128)S(1)} %slice_bitcast_fusion), channel_id=1, source_target_pairs={{0,2},{1,3},{2,0},{3,1},{4,6},{5,7},{6,4},{7,5},{8,10},{9,11},{10,... | collective-permute-start | bytes 49160 | tf_op jit(solution)/shard_map/ppermute | solution.py:275
  25.2 2.3 %collective-permute-done.10 = f32[32,128]{1,0:T(8,128)S(1)} collective-permute-done((f32[32,128]{1,0:T(8,128)S(1)}, f32[32,128]{1,0:T(8,128)S(1)}, u32[]{:S(2)}, u32[]{:S(2)}) %collective-permute-start.10) | collective-permute-done | bytes 16416 | tf_op jit(solution)/shard_map/ppermute | solution.py:275
  27.4 0.6 %fusion = f32[32,128]{1,0:T(8,128)} fusion(f32[32,128]{1,0:T(8,128)S(1)} %collective-permute-done.10, f32[2,32,128]{2,1,0:T(8,128)S(1)} %add.10), kind=kLoop, calls=%fused_computation.2 | loop fusion | flops 4096 | bytes 49152 | tf_op jit(solution)/shard_map/add | solution.py:275
  (4 shorter events, 0.0 us)
Async XLA Ops:
  1.0 1.3 %collective-permute-start = (bf16[4,8,128]{2,1,0:T(8,128)(2,1)S(1)}, bf16[4,8,128]{2,1,0:T(8,128)(2,1)S(1)}, u32[]{:S(2)}, u32[]{:S(2)}) collective-permute-start(bf16[4,8,128]{2,1,0:T(8,128)(2,1)S(1)} %get-tuple-element.10), channel_id=1, source_target_pairs={{0,1},{1,0},{2,3},{3,2},{4,5},{5,4},{6,7},{7,6},{8,9},{9,8},{10,11... | collective-permute-start | bytes 24584 | tf_op jit(solution)/shard_map/ppermute | solution.py:247
  2.4 6.2 %collective-permute-start.7 = (bf16[4,8,1152]{2,1,0:T(8,128)(2,1)S(1)}, bf16[4,8,1152]{2,1,0:T(8,128)(2,1)S(1)}, u32[]{:S(2)}, u32[]{:S(2)}) collective-permute-start(bf16[4,8,1152]{2,1,0:T(8,128)(2,1)S(1)} %add_dynamic-update-slice_fusion.refs_8_), channel_id=1, source_target_pairs={{5,1},{7,3},{1,5},{3,7},{13,9},{15,11},{9,13},{11,15},{21,17},{23,... | collective-permute-start | bytes 221192 | tf_op jit(solution)/shard_map/ppermute | solution.py:220
  3.0 8.6 %collective-permute-start.5 = (bf16[4,8,1152]{2,1,0:T(8,128)(2,1)S(1)}, bf16[4,8,1152]{2,1,0:T(8,128)(2,1)S(1)}, u32[]{:S(2)}, u32[]{:S(2)}) collective-permute-start(bf16[4,8,1152]{2,1,0:T(8,128)(2,1)S(1)} %add_dynamic-update-slice_fusion.refs_8_), channel_id=1, source_target_pairs={{8,0},{13,1},{10,2},{15,3},{12,4},{9,5},{14,6},{11,7},{0,8},{5,9},... | collective-permute-start | bytes 221192 | tf_op jit(solution)/shard_map/ppermute | solution.py:220
  6.0 6.7 %collective-permute-start.3 = (bf16[4,8,1152]{2,1,0:T(8,128)(2,1)S(1)}, bf16[4,8,1152]{2,1,0:T(8,128)(2,1)S(1)}, u32[]{:S(2)}, u32[]{:S(2)}) collective-permute-start(bf16[4,8,1152]{2,1,0:T(8,128)(2,1)S(1)} %add_dynamic-update-slice_fusion.refs_8_), channel_id=1, source_target_pairs={{24,0},{29,1},{26,2},{31,3},{28,4},{25,5},{30,6},{27,7},{16,8},{21... | collective-permute-start | bytes 221192 | tf_op jit(solution)/shard_map/ppermute | solution.py:220
  8.5 8.2 %collective-permute-start.1 = (bf16[4,8,1152]{2,1,0:T(8,128)(2,1)S(1)}, bf16[4,8,1152]{2,1,0:T(8,128)(2,1)S(1)}, u32[]{:S(2)}, u32[]{:S(2)}) collective-permute-start(bf16[4,8,1152]{2,1,0:T(8,128)(2,1)S(1)} %add_dynamic-update-slice_fusion.refs_8_), channel_id=1, source_target_pairs={{16,0},{21,1},{18,2},{23,3},{20,4},{17,5},{22,6},{19,7},{24,8},{29... | collective-permute-start | bytes 221192 | tf_op jit(solution)/shard_map/ppermute | solution.py:220
  8.6 9.1 %collective-permute-start.8 = (bf16[4,8,1152]{2,1,0:T(8,128)(2,1)S(1)}, bf16[4,8,1152]{2,1,0:T(8,128)(2,1)S(1)}, u32[]{:S(2)}, u32[]{:S(2)}) collective-permute-start(bf16[4,8,1152]{2,1,0:T(8,128)(2,1)S(1)} %collective-permute-done.7.refs_6_), channel_id=1, source_target_pairs={{0,1},{1,0},{2,3},{3,2},{4,5},{5,4},{6,7},{7,6},{8,9},{9,8},{10,11... | collective-permute-start | bytes 221192 | tf_op jit(solution)/shard_map/ppermute | solution.py:221
  11.6 6.1 %collective-permute-start.6 = (bf16[4,8,1152]{2,1,0:T(8,128)(2,1)S(1)}, bf16[4,8,1152]{2,1,0:T(8,128)(2,1)S(1)}, u32[]{:S(2)}, u32[]{:S(2)}) collective-permute-start(bf16[4,8,1152]{2,1,0:T(8,128)(2,1)S(1)} %collective-permute-done.5.refs_4_), channel_id=1, source_target_pairs={{0,1},{1,0},{2,3},{3,2},{4,5},{5,4},{6,7},{7,6},{8,9},{9,8},{10,11... | collective-permute-start | bytes 221192 | tf_op jit(solution)/shard_map/ppermute | solution.py:221
  12.7 5.1 %collective-permute-start.4 = (bf16[4,8,1152]{2,1,0:T(8,128)(2,1)S(1)}, bf16[4,8,1152]{2,1,0:T(8,128)(2,1)S(1)}, u32[]{:S(2)}, u32[]{:S(2)}) collective-permute-start(bf16[4,8,1152]{2,1,0:T(8,128)(2,1)S(1)} %collective-permute-done.3.refs_2_), channel_id=1, source_target_pairs={{0,1},{1,0},{2,3},{3,2},{4,5},{5,4},{6,7},{7,6},{8,9},{9,8},{10,11... | collective-permute-start | bytes 221192 | tf_op jit(solution)/shard_map/ppermute | solution.py:221
  16.7 2.0 %collective-permute-start.2 = (bf16[4,8,1152]{2,1,0:T(8,128)(2,1)S(1)}, bf16[4,8,1152]{2,1,0:T(8,128)(2,1)S(1)}, u32[]{:S(2)}, u32[]{:S(2)}) collective-permute-start(bf16[4,8,1152]{2,1,0:T(8,128)(2,1)S(1)} %collective-permute-done.1.refs_0_), channel_id=1, source_target_pairs={{0,1},{1,0},{2,3},{3,2},{4,5},{5,4},{6,7},{7,6},{8,9},{9,8},{10,11... | collective-permute-start | bytes 221192 | tf_op jit(solution)/shard_map/ppermute | solution.py:221
  22.3 1.3 %collective-permute-start.9 = (f32[2,32,128]{2,1,0:T(8,128)S(1)}, f32[2,32,128]{2,1,0:T(8,128)S(1)}, u32[]{:S(2)}, u32[]{:S(2)}) collective-permute-start(f32[2,32,128]{2,1,0:T(8,128)S(1)} %get-tuple-element.12), channel_id=1, source_target_pairs={{0,1},{1,0},{2,3},{3,2},{4,5},{5,4},{6,7},{7,6},{8,9},{9,8},{10,11... | collective-permute-start | bytes 98312 | tf_op jit(solution)/shard_map/ppermute | solution.py:273
  23.6 3.8 %collective-permute-start.10 = (f32[32,128]{1,0:T(8,128)S(1)}, f32[32,128]{1,0:T(8,128)S(1)}, u32[]{:S(2)}, u32[]{:S(2)}) collective-permute-start(f32[32,128]{1,0:T(8,128)S(1)} %slice_bitcast_fusion), channel_id=1, source_target_pairs={{0,2},{1,3},{2,0},{3,1},{4,6},{5,7},{6,4},{7,5},{8,10},{9,11},{10,... | collective-permute-start | bytes 49160 | tf_op jit(solution)/shard_map/ppermute | solution.py:275

commit v3 on v2

--- a/solution.py
+++ b/solution.py
@@ -68,8 +68,8 @@
 
 
 def response_kernel(wide_count, unit_count, offsets, wide_ref, pair_ref, *refs):
-    block_refs = refs[: -7]
-    keep_ref, send_ref, rows_ref, small_ref, index_ref, column_ref, sem = refs[-7:]
+    block_refs = refs[: -9]
+    keep_ref, send_ref, rows_ref, small_ref, index_ref, column_ref, sem, occupied_ref, both_ref = refs[-9:]
     block_size = block_refs[0].shape[1]
     square = block_size * block_size
     aux_count = rows_ref.shape[2]
@@ -145,9 +145,16 @@
             )
             wide = jnp.dot(smalls, spread, preferred_element_type=F32)
             for member in range(group):
-                values = wide[member * block_size : (member + 1) * block_size]
-                occ, virt = values[:, :wide_unit], values[:, wide_unit:]
+                occ = wide[member * block_size : (member + 1) * block_size, :wide_unit]
                 occ_weights = jnp.concatenate([occ * mask for mask in occ_mask], axis=0)
+                occupied_ref[:, member * wide_unit : (member + 1) * wide_unit] = lax.dot_general(
+                    rows_ref[atoms[member]],
+                    occ_weights.astype(BF16),
+                    (((0,), (0,)), ((), ())),
+                    preferred_element_type=F32,
+                ).astype(BF16)
+            for member in range(group):
+                virt = wide[member * block_size : (member + 1) * block_size, wide_unit:]
                 virt_weights = jnp.concatenate(
                     [
                         jnp.broadcast_to(virt[nu : nu + 1], virt.shape) * virt_mask[unit]
@@ -156,16 +163,12 @@
                     ],
                     axis=0,
                 )
-                occupied = lax.dot_general(
-                    rows_ref[atoms[member]],
-                    occ_weights.astype(BF16),
-                    (((0,), (0,)), ((), ())),
-                    preferred_element_type=F32,
+                both_ref[:, member * wide_unit : (member + 1) * wide_unit] = jnp.dot(
+                    occupied_ref[:, member * wide_unit : (member + 1) * wide_unit],
+                    virt_weights.astype(BF16), preferred_element_type=F32
                 ).astype(BF16)
-                both = jnp.dot(
-                    occupied, virt_weights.astype(BF16), preferred_element_type=F32
-                ).astype(BF16)
-                partner = []
+            partner = []
+            for member in range(group):
                 for unit in range(chunk * CHUNK, (chunk + 1) * CHUNK):
                     if unit < unit_count:
                         high = column_ref[step * group + member, 0, column_lane + unit]
@@ -175,9 +178,9 @@
                         partner.append(rows_ref[high * BASE + low])
                     else:
                         partner.append(jnp.zeros((square, aux_count), BF16))
-                total += jnp.dot(
-                    both, jnp.concatenate(partner, axis=0), preferred_element_type=F32
-                )
+            total += jnp.dot(
+                both_ref[...], jnp.concatenate(partner, axis=0), preferred_element_type=F32
+            )
         return total
 
     steps = own_atoms // group
@@ -209,7 +212,7 @@
         return [lax.all_gather(block, "wide", axis=0, tiled=True)], (None,)
     partner = [(p, p ^ 1) for p in range(pair_count)]
     blocks, offsets = [], []
-    for even, odd in ((4, 5), (6, 7), (2, 3), (0, 1)):
+    for even, odd in ((0, 1), (2, 3), (6, 7), (4, 5)):
         route = [
             ((w ^ d) * pair_count + p, w * pair_count + p)
             for w in range(wide_count)
@@ -252,6 +255,7 @@
 
     atom_total = wide_count * local_atoms
     own_atoms = atom_total // 2
+    group_lanes = max(1, min(own_atoms, 16 // -(-unit_count // CHUNK))) * CHUNK * block_size**2
     index_lanes = lanes - column_at // 128 * 128
     row_count = aux_count // pair_count
     part = pltpu.VMEM((2, row_count, aux_count), F32)
@@ -266,6 +270,8 @@
             pltpu.VMEM((own_atoms, 1, index_lanes), jnp.int32),
             pltpu.SMEM((own_atoms, 1, index_lanes), jnp.int32),
             pltpu.SemaphoreType.DMA,
+            pltpu.VMEM((aux_count, group_lanes), BF16),
+            pltpu.VMEM((aux_count, group_lanes), BF16),
         ],
         compiler_params=pltpu.CompilerParams(vmem_limit_bytes=56 * 2**20),
         name="response",

time: 28.2 us -> 23.4 us (0.83)
  starting transfers between devices: 15.4 us -> 12.3 us
  Pallas kernels: 4.66 us -> 2.96 us
    ppermute x4, starting transfers between devices: 6.71 us -> 3.34 us  [gather_over_wide(): blocks += [fetched, lax.ppermute(fetched, 'pair', partner)]]
    pallas_call x1, Pallas kernels: 3.65 us -> 1.95 us  [local(): pl.pallas_call(functools.partial(response_kernel, wide_count, unit_count,...]
  transfers between devices with their start and end apart: 11 -> 11, of which waited for: 6 -> 8; matrix products, arithmetic and copies ran while one was open for 0% -> 0% of each run, Pallas kernels for 0% -> 0%
where the time goes in v3:
time: 23.4 us; the launch traced here: 23.2 us
  starting transfers between devices  12.3 us (53%)
  waiting for transfers between devices  7.28 us (31%)
  Pallas kernels  2.96 us (13%)
  other arithmetic  0.63 us (3%)
    ppermute x4, starting transfers between devices, gather_over_wide(): fetched = lax.ppermute(block, ('wide', 'pair'), route)  6.21 us
    ppermute x4, starting transfers between devices, gather_over_wide(): blocks += [fetched, lax.ppermute(fetched, 'pair', partner)]  3.34 us
    ppermute x4, waiting for transfers between devices, gather_over_wide(): fetched = lax.ppermute(block, ('wide', 'pair'), route)  2.68 us
    ppermute x1, waiting for transfers between devices, local(): return summed[0] + lax.ppermute(summed[1], 'pair', other)  2.01 us
    pallas_call x1, Pallas kernels, local(): pl.pallas_call(functools.partial(response_kernel, wide_count, unit_count,...  1.95 us
    ppermute x1, starting transfers between devices, local(): return summed[0] + lax.ppermute(summed[1], 'pair', other)  1.8 us
    pallas_call x1, Pallas kernels, local(): pl.pallas_call(pack_kernel, out_shape=(pltpu.VMEM((local_atoms, block_siz...  1.01 us
    ppermute x4, waiting for transfers between devices, gather_over_wide(): blocks += [fetched, lax.ppermute(fetched, 'pair', partner)]  0.91 us
  transfers between devices with their start and end apart: 11, of which 8 were waited for; matrix products, arithmetic and copies ran while one was open for 0% of the time, Pallas kernels for 0%

profile of v3, /device:TPU:0, one launch (start us, length us, event | category | flops | bytes accessed | tf_op | source)
XLA Modules:
  0.0 23.2 jit_solution(14170636176058206021)
XLA Ops:
  0.0 1.0 %pack.1 = (bf16[4,8,1152]{2,1,0:T(8,128)(2,1)S(1)}, bf16[4,8,128]{2,1,0:T(8,128)(2,1)S(1)}) custom-call(s32[1]{0:T(128)} %bitcast.1.pair_ref, s32[2,4]{1,0:T(2,128)} %bitcast.10, s32[2,4]{1,0:T(2,128)} %bitcast.11, bf16[4,8,1024]{2,1,0:T(8,128)(2,1)} %tc_ref.1, bf16[4,2,8,8]{3,2,1,0:T(8,128)(2,1)} %occ_ref.1, bf16[4,2,8,8]{3,2,1,0:T(8,128)(2,1)} %virt_ref.1), custom_call_target="tpu_custom_call" | custom-call | tf_op jit(solution)/shard_map/pack/pallas_call | solution.py:240
  1.0 0.5 %collective-permute-start = (bf16[4,8,128]{2,1,0:T(8,128)(2,1)S(1)}, bf16[4,8,128]{2,1,0:T(8,128)(2,1)S(1)}, u32[]{:S(2)}, u32[]{:S(2)}) collective-permute-start(bf16[4,8,128]{2,1,0:T(8,128)(2,1)S(1)} %get-tuple-element.10), channel_id=1, source_target_pairs={{0,1},{1,0},{2,3},{3,2},{4,5},{5,4},{6,7},{7,6},{8,9},{9,8},{10,11... | collective-permute-start | bytes 24584 | tf_op jit(solution)/shard_map/ppermute | solution.py:250
  1.5 0.8 %collective-permute-done = bf16[4,8,128]{2,1,0:T(8,128)(2,1)S(1)} collective-permute-done((bf16[4,8,128]{2,1,0:T(8,128)(2,1)S(1)}, bf16[4,8,128]{2,1,0:T(8,128)(2,1)S(1)}, u32[]{:S(2)}, u32[]{:S(2)}) %collective-permute-start) | collective-permute-done | bytes 8224 | tf_op jit(solution)/shard_map/ppermute | solution.py:250
  2.4 4.0 %collective-permute-start.7 = (bf16[4,8,1152]{2,1,0:T(8,128)(2,1)S(1)}, bf16[4,8,1152]{2,1,0:T(8,128)(2,1)S(1)}, u32[]{:S(2)}, u32[]{:S(2)}) collective-permute-start(bf16[4,8,1152]{2,1,0:T(8,128)(2,1)S(1)} %add_dynamic-update-slice_fusion.refs_8_), channel_id=1, source_target_pairs={{16,0},{21,1},{18,2},{23,3},{20,4},{17,5},{22,6},{19,7},{24,8},{29... | collective-permute-start | bytes 221192 | tf_op jit(solution)/shard_map/ppermute | solution.py:223
  6.4 1.3 %collective-permute-start.5 = (bf16[4,8,1152]{2,1,0:T(8,128)(2,1)S(1)}, bf16[4,8,1152]{2,1,0:T(8,128)(2,1)S(1)}, u32[]{:S(2)}, u32[]{:S(2)}) collective-permute-start(bf16[4,8,1152]{2,1,0:T(8,128)(2,1)S(1)} %add_dynamic-update-slice_fusion.refs_8_), channel_id=1, source_target_pairs={{24,0},{29,1},{26,2},{31,3},{28,4},{25,5},{30,6},{27,7},{16,8},{21... | collective-permute-start | bytes 221192 | tf_op jit(solution)/shard_map/ppermute | solution.py:223
  7.7 0.2 collective-permute-start.3
  7.9 0.7 %collective-permute-start.1 = (bf16[4,8,1152]{2,1,0:T(8,128)(2,1)S(1)}, bf16[4,8,1152]{2,1,0:T(8,128)(2,1)S(1)}, u32[]{:S(2)}, u32[]{:S(2)}) collective-permute-start(bf16[4,8,1152]{2,1,0:T(8,128)(2,1)S(1)} %add_dynamic-update-slice_fusion.refs_8_), channel_id=1, source_target_pairs={{5,1},{7,3},{1,5},{3,7},{13,9},{15,11},{9,13},{11,15},{21,17},{23,... | collective-permute-start | bytes 221192 | tf_op jit(solution)/shard_map/ppermute | solution.py:223
  8.6 0.5 %collective-permute-done.7.refs_6_ = bf16[4,8,1152]{2,1,0:T(8,128)(2,1)S(1)} collective-permute-done((bf16[4,8,1152]{2,1,0:T(8,128)(2,1)S(1)}, bf16[4,8,1152]{2,1,0:T(8,128)(2,1)S(1)}, u32[]{:S(2)}, u32[]{:S(2)}) %collective-permute-start.7) | collective-permute-done | bytes 73760 | tf_op jit(solution)/shard_map/ppermute | solution.py:223
  9.1 2.5 %collective-permute-start.8 = (bf16[4,8,1152]{2,1,0:T(8,128)(2,1)S(1)}, bf16[4,8,1152]{2,1,0:T(8,128)(2,1)S(1)}, u32[]{:S(2)}, u32[]{:S(2)}) collective-permute-start(bf16[4,8,1152]{2,1,0:T(8,128)(2,1)S(1)} %collective-permute-done.7.refs_6_), channel_id=1, source_target_pairs={{0,1},{1,0},{2,3},{3,2},{4,5},{5,4},{6,7},{7,6},{8,9},{9,8},{10,11... | collective-permute-start | bytes 221192 | tf_op jit(solution)/shard_map/ppermute | solution.py:224
  11.6 1.7 %collective-permute-done.5.refs_4_ = bf16[4,8,1152]{2,1,0:T(8,128)(2,1)S(1)} collective-permute-done((bf16[4,8,1152]{2,1,0:T(8,128)(2,1)S(1)}, bf16[4,8,1152]{2,1,0:T(8,128)(2,1)S(1)}, u32[]{:S(2)}, u32[]{:S(2)}) %collective-permute-start.5) | collective-permute-done | bytes 73760 | tf_op jit(solution)/shard_map/ppermute | solution.py:223
  13.3 0.4 %collective-permute-start.6 = (bf16[4,8,1152]{2,1,0:T(8,128)(2,1)S(1)}, bf16[4,8,1152]{2,1,0:T(8,128)(2,1)S(1)}, u32[]{:S(2)}, u32[]{:S(2)}) collective-permute-start(bf16[4,8,1152]{2,1,0:T(8,128)(2,1)S(1)} %collective-permute-done.5.refs_4_), channel_id=1, source_target_pairs={{0,1},{1,0},{2,3},{3,2},{4,5},{5,4},{6,7},{7,6},{8,9},{9,8},{10,11... | collective-permute-start | bytes 221192 | tf_op jit(solution)/shard_map/ppermute | solution.py:224
  13.7 0.4 %collective-permute-done.3.refs_2_ = bf16[4,8,1152]{2,1,0:T(8,128)(2,1)S(1)} collective-permute-done((bf16[4,8,1152]{2,1,0:T(8,128)(2,1)S(1)}, bf16[4,8,1152]{2,1,0:T(8,128)(2,1)S(1)}, u32[]{:S(2)}, u32[]{:S(2)}) %collective-permute-start.3) | collective-permute-done | bytes 73760 | tf_op jit(solution)/shard_map/ppermute | solution.py:223
  14.1 0.2 collective-permute-start.4
  14.3 0.0 collective-permute-done.1.refs_0_
  14.3 0.4 %collective-permute-start.2 = (bf16[4,8,1152]{2,1,0:T(8,128)(2,1)S(1)}, bf16[4,8,1152]{2,1,0:T(8,128)(2,1)S(1)}, u32[]{:S(2)}, u32[]{:S(2)}) collective-permute-start(bf16[4,8,1152]{2,1,0:T(8,128)(2,1)S(1)} %collective-permute-done.1.refs_0_), channel_id=1, source_target_pairs={{0,1},{1,0},{2,3},{3,2},{4,5},{5,4},{6,7},{7,6},{8,9},{9,8},{10,11... | collective-permute-start | bytes 221192 | tf_op jit(solution)/shard_map/ppermute | solution.py:224
  14.6 0.0 collective-permute-done.8.refs_7_
  14.6 0.7 %collective-permute-done.4.refs_3_ = bf16[4,8,1152]{2,1,0:T(8,128)(2,1)S(1)} collective-permute-done((bf16[4,8,1152]{2,1,0:T(8,128)(2,1)S(1)}, bf16[4,8,1152]{2,1,0:T(8,128)(2,1)S(1)}, u32[]{:S(2)}, u32[]{:S(2)}) %collective-permute-start.4) | collective-permute-done | bytes 73760 | tf_op jit(solution)/shard_map/ppermute | solution.py:224
  15.4 0.2 collective-permute-done.2.refs_1_
  15.5 1.9 %response.1 = (f32[2,32,128]{2,1,0:T(8,128)S(1)}, f32[2,32,128]{2,1,0:T(8,128)S(1)}) custom-call(s32[1]{0:T(128)} %bitcast.wide_ref, s32[1]{0:T(128)} %bitcast.1.pair_ref, bf16[4,8,1152]{2,1,0:T(8,128)(2,1)S(1)} %collective-permute-done.1.refs_0_, bf16[4,8,1152]{2,1,0:T(8,128)(2,1)S(1)} %collective-permute-done.2.refs_1_, ...), custom_call_target="tpu_custom_call" | custom-call | tf_op jit(solution)/shard_map/response/pallas_call | solution.py:262
  17.5 0.4 %collective-permute-start.9 = (f32[2,32,128]{2,1,0:T(8,128)S(1)}, f32[2,32,128]{2,1,0:T(8,128)S(1)}, u32[]{:S(2)}, u32[]{:S(2)}) collective-permute-start(f32[2,32,128]{2,1,0:T(8,128)S(1)} %get-tuple-element.12), channel_id=1, source_target_pairs={{0,1},{1,0},{2,3},{3,2},{4,5},{5,4},{6,7},{7,6},{8,9},{9,8},{10,11... | collective-permute-start | bytes 98312 | tf_op jit(solution)/shard_map/ppermute | solution.py:279
  17.9 0.9 %collective-permute-done.9 = f32[2,32,128]{2,1,0:T(8,128)S(1)} collective-permute-done((f32[2,32,128]{2,1,0:T(8,128)S(1)}, f32[2,32,128]{2,1,0:T(8,128)S(1)}, u32[]{:S(2)}, u32[]{:S(2)}) %collective-permute-start.9) | collective-permute-done | bytes 32800 | tf_op jit(solution)/shard_map/ppermute | solution.py:279
  18.8 1.8 %collective-permute-start.10 = (f32[32,128]{1,0:T(8,128)S(1)}, f32[32,128]{1,0:T(8,128)S(1)}, u32[]{:S(2)}, u32[]{:S(2)}) collective-permute-start(f32[32,128]{1,0:T(8,128)S(1)} %slice_bitcast_fusion), channel_id=1, source_target_pairs={{0,2},{1,3},{2,0},{3,1},{4,6},{5,7},{6,4},{7,5},{8,10},{9,11},{10,... | collective-permute-start | bytes 49160 | tf_op jit(solution)/shard_map/ppermute | solution.py:281
  20.6 2.0 %collective-permute-done.10 = f32[32,128]{1,0:T(8,128)S(1)} collective-permute-done((f32[32,128]{1,0:T(8,128)S(1)}, f32[32,128]{1,0:T(8,128)S(1)}, u32[]{:S(2)}, u32[]{:S(2)}) %collective-permute-start.10) | collective-permute-done | bytes 16416 | tf_op jit(solution)/shard_map/ppermute | solution.py:281
  22.6 0.6 %fusion = f32[32,128]{1,0:T(8,128)} fusion(f32[32,128]{1,0:T(8,128)S(1)} %collective-permute-done.10, f32[2,32,128]{2,1,0:T(8,128)S(1)} %add.10), kind=kLoop, calls=%fused_computation.2 | loop fusion | flops 4096 | bytes 49152 | tf_op jit(solution)/shard_map/add | solution.py:281
  (4 shorter events, 0.0 us)
Async XLA Ops:
  1.0 1.3 %collective-permute-start = (bf16[4,8,128]{2,1,0:T(8,128)(2,1)S(1)}, bf16[4,8,128]{2,1,0:T(8,128)(2,1)S(1)}, u32[]{:S(2)}, u32[]{:S(2)}) collective-permute-start(bf16[4,8,128]{2,1,0:T(8,128)(2,1)S(1)} %get-tuple-element.10), channel_id=1, source_target_pairs={{0,1},{1,0},{2,3},{3,2},{4,5},{5,4},{6,7},{7,6},{8,9},{9,8},{10,11... | collective-permute-start | bytes 24584 | tf_op jit(solution)/shard_map/ppermute | solution.py:250
  2.4 6.8 %collective-permute-start.7 = (bf16[4,8,1152]{2,1,0:T(8,128)(2,1)S(1)}, bf16[4,8,1152]{2,1,0:T(8,128)(2,1)S(1)}, u32[]{:S(2)}, u32[]{:S(2)}) collective-permute-start(bf16[4,8,1152]{2,1,0:T(8,128)(2,1)S(1)} %add_dynamic-update-slice_fusion.refs_8_), channel_id=1, source_target_pairs={{16,0},{21,1},{18,2},{23,3},{20,4},{17,5},{22,6},{19,7},{24,8},{29... | collective-permute-start | bytes 221192 | tf_op jit(solution)/shard_map/ppermute | solution.py:223
  6.4 7.0 %collective-permute-start.5 = (bf16[4,8,1152]{2,1,0:T(8,128)(2,1)S(1)}, bf16[4,8,1152]{2,1,0:T(8,128)(2,1)S(1)}, u32[]{:S(2)}, u32[]{:S(2)}) collective-permute-start(bf16[4,8,1152]{2,1,0:T(8,128)(2,1)S(1)} %add_dynamic-update-slice_fusion.refs_8_), channel_id=1, source_target_pairs={{24,0},{29,1},{26,2},{31,3},{28,4},{25,5},{30,6},{27,7},{16,8},{21... | collective-permute-start | bytes 221192 | tf_op jit(solution)/shard_map/ppermute | solution.py:223
  7.7 6.4 %collective-permute-start.3 = (bf16[4,8,1152]{2,1,0:T(8,128)(2,1)S(1)}, bf16[4,8,1152]{2,1,0:T(8,128)(2,1)S(1)}, u32[]{:S(2)}, u32[]{:S(2)}) collective-permute-start(bf16[4,8,1152]{2,1,0:T(8,128)(2,1)S(1)} %add_dynamic-update-slice_fusion.refs_8_), channel_id=1, source_target_pairs={{8,0},{13,1},{10,2},{15,3},{12,4},{9,5},{14,6},{11,7},{0,8},{5,9},... | collective-permute-start | bytes 221192 | tf_op jit(solution)/shard_map/ppermute | solution.py:223
  7.9 6.3 %collective-permute-start.1 = (bf16[4,8,1152]{2,1,0:T(8,128)(2,1)S(1)}, bf16[4,8,1152]{2,1,0:T(8,128)(2,1)S(1)}, u32[]{:S(2)}, u32[]{:S(2)}) collective-permute-start(bf16[4,8,1152]{2,1,0:T(8,128)(2,1)S(1)} %add_dynamic-update-slice_fusion.refs_8_), channel_id=1, source_target_pairs={{5,1},{7,3},{1,5},{3,7},{13,9},{15,11},{9,13},{11,15},{21,17},{23,... | collective-permute-start | bytes 221192 | tf_op jit(solution)/shard_map/ppermute | solution.py:223
  9.1 5.5 %collective-permute-start.8 = (bf16[4,8,1152]{2,1,0:T(8,128)(2,1)S(1)}, bf16[4,8,1152]{2,1,0:T(8,128)(2,1)S(1)}, u32[]{:S(2)}, u32[]{:S(2)}) collective-permute-start(bf16[4,8,1152]{2,1,0:T(8,128)(2,1)S(1)} %collective-permute-done.7.refs_6_), channel_id=1, source_target_pairs={{0,1},{1,0},{2,3},{3,2},{4,5},{5,4},{6,7},{7,6},{8,9},{9,8},{10,11... | collective-permute-start | bytes 221192 | tf_op jit(solution)/shard_map/ppermute | solution.py:224
  13.3 1.3 %collective-permute-start.6 = (bf16[4,8,1152]{2,1,0:T(8,128)(2,1)S(1)}, bf16[4,8,1152]{2,1,0:T(8,128)(2,1)S(1)}, u32[]{:S(2)}, u32[]{:S(2)}) collective-permute-start(bf16[4,8,1152]{2,1,0:T(8,128)(2,1)S(1)} %collective-permute-done.5.refs_4_), channel_id=1, source_target_pairs={{0,1},{1,0},{2,3},{3,2},{4,5},{5,4},{6,7},{7,6},{8,9},{9,8},{10,11... | collective-permute-start | bytes 221192 | tf_op jit(solution)/shard_map/ppermute | solution.py:224
  14.1 1.3 %collective-permute-start.4 = (bf16[4,8,1152]{2,1,0:T(8,128)(2,1)S(1)}, bf16[4,8,1152]{2,1,0:T(8,128)(2,1)S(1)}, u32[]{:S(2)}, u32[]{:S(2)}) collective-permute-start(bf16[4,8,1152]{2,1,0:T(8,128)(2,1)S(1)} %collective-permute-done.3.refs_2_), channel_id=1, source_target_pairs={{0,1},{1,0},{2,3},{3,2},{4,5},{5,4},{6,7},{7,6},{8,9},{9,8},{10,11... | collective-permute-start | bytes 221192 | tf_op jit(solution)/shard_map/ppermute | solution.py:224
  14.3 1.3 %collective-permute-start.2 = (bf16[4,8,1152]{2,1,0:T(8,128)(2,1)S(1)}, bf16[4,8,1152]{2,1,0:T(8,128)(2,1)S(1)}, u32[]{:S(2)}, u32[]{:S(2)}) collective-permute-start(bf16[4,8,1152]{2,1,0:T(8,128)(2,1)S(1)} %collective-permute-done.1.refs_0_), channel_id=1, source_target_pairs={{0,1},{1,0},{2,3},{3,2},{4,5},{5,4},{6,7},{7,6},{8,9},{9,8},{10,11... | collective-permute-start | bytes 221192 | tf_op jit(solution)/shard_map/ppermute | solution.py:224
  17.5 1.3 %collective-permute-start.9 = (f32[2,32,128]{2,1,0:T(8,128)S(1)}, f32[2,32,128]{2,1,0:T(8,128)S(1)}, u32[]{:S(2)}, u32[]{:S(2)}) collective-permute-start(f32[2,32,128]{2,1,0:T(8,128)S(1)} %get-tuple-element.12), channel_id=1, source_target_pairs={{0,1},{1,0},{2,3},{3,2},{4,5},{5,4},{6,7},{7,6},{8,9},{9,8},{10,11... | collective-permute-start | bytes 98312 | tf_op jit(solution)/shard_map/ppermute | solution.py:279
  18.8 3.8 %collective-permute-start.10 = (f32[32,128]{1,0:T(8,128)S(1)}, f32[32,128]{1,0:T(8,128)S(1)}, u32[]{:S(2)}, u32[]{:S(2)}) collective-permute-start(f32[32,128]{1,0:T(8,128)S(1)} %slice_bitcast_fusion), channel_id=1, source_target_pairs={{0,2},{1,3},{2,0},{3,1},{4,6},{5,7},{6,4},{7,5},{8,10},{9,11},{10,... | collective-permute-start | bytes 49160 | tf_op jit(solution)/shard_map/ppermute | solution.py:281

commit v4 on v2

v4 whole, which is shorter than its diff:
```python
import functools

import jax
import jax.numpy as jnp
from jax import lax
from jax.experimental import pallas as pl
from jax.experimental.pallas import tpu as pltpu
from jax.sharding import PartitionSpec as P

CHUNK = 4
BASE = 256
F32, BF16 = jnp.float32, jnp.bfloat16


def ceil_to(value, step):
    return -(-value // step) * step


def small_layout(unit_count, block_size):
    chunk_count = -(-unit_count // CHUNK)
    column_at = chunk_count * 2 * CHUNK * block_size
    return chunk_count, column_at, ceil_to(column_at + 2 * unit_count, 128)


def iota(shape, axis):
    return lax.broadcasted_iota(jnp.int32, shape, axis)


def pack_kernel(pair_ref, column_ref, live_ref, tc_ref, occ_ref, virt_ref, block_ref, small_ref):
    local_atoms, own_units, block_size, _ = occ_ref.shape
    wide_row = tc_ref.shape[2]
    unit_count = 2 * own_units
    _, column_at, lanes = small_layout(unit_count, block_size)
    half = pair_ref[0] % 2
    row, lane = iota((block_size, lanes), 0), iota((block_size, lanes), 1)
    packed = jnp.zeros((local_atoms * block_size, lanes), F32)
    columns = [jnp.zeros((block_size, lanes), F32) for _ in range(local_atoms)]
    for slot in range(own_units):
        unit = half * own_units + slot
        at = (unit // CHUNK) * (2 * CHUNK * block_size) + (unit % CHUNK) * block_size
        occ = jnp.concatenate(
            [
                occ_ref[atom, slot].astype(F32) * live_ref[slot, atom].astype(F32)
                for atom in range(local_atoms)
            ],
            axis=0,
        ).astype(BF16)
        virt = jnp.concatenate(
            [virt_ref[atom, slot].astype(F32) for atom in range(local_atoms)], axis=0
        ).astype(BF16)
        occ_place = (lane == at + row).astype(BF16)
        virt_place = (lane == at + CHUNK * block_size + row).astype(BF16)
        packed += jnp.dot(occ, occ_place, preferred_element_type=F32)
        packed += jnp.dot(virt, virt_place, preferred_element_type=F32)
        for atom in range(local_atoms):
            column = column_ref[slot, atom]
            high = column // BASE
            low = column - high * BASE
            columns[atom] += jnp.where(lane == column_at + unit, high.astype(F32), 0.0)
            columns[atom] += jnp.where(
                lane == column_at + unit_count + unit, low.astype(F32), 0.0
            )
    packed = (packed + jnp.concatenate(columns, axis=0)).astype(BF16)
    packed = packed.reshape(local_atoms, block_size, lanes)
    block_ref[:, :, :wide_row] = tc_ref[...]
    block_ref[:, :, wide_row:] = packed
    small_ref[...] = packed


def in_rows(block, aux_count):
    parts = range(block.shape[0])
    return jnp.concatenate([block[:, at * aux_count : (at + 1) * aux_count] for at in parts], axis=0)


def digits_of(small, column_at):
    digits = small[:, column_at // 128 * 128 :].astype(F32)
    return digits[0:1, :].astype(jnp.int32)


def weight_parts(block_size, lane_at):
    square = block_size * block_size
    wide_unit = CHUNK * square
    row, lane = iota((128, 2 * wide_unit), 0), iota((128, 2 * wide_unit), 1)
    inner = lane % wide_unit
    unit, upper, lower = inner // square, (inner // block_size) % block_size, inner % block_size
    within = jnp.where(lane >= wide_unit, upper + CHUNK * block_size, lower)
    spread = (row == unit * block_size + within + lane_at).astype(BF16)
    row, lane = iota((block_size, wide_unit), 0), iota((block_size, wide_unit), 1)
    unit, upper, lower = lane // square, (lane // block_size) % block_size, lane % block_size
    occ_mask = [(upper == at).astype(F32) for at in range(block_size)]
    virt_mask = [((unit == at) & (lower == row)).astype(F32) for at in range(CHUNK)]
    return spread, occ_mask, virt_mask


def contract(rows, smalls, parts, occupied_ref, both_ref):
    spread, occ_mask, virt_mask = parts
    block_size, wide_unit = occ_mask[0].shape
    wide = jnp.dot(jnp.concatenate(smalls, axis=0), spread, preferred_element_type=F32)
    for member in range(len(rows)):
        occ = wide[member * block_size : (member + 1) * block_size, :wide_unit]
        weights = jnp.concatenate([occ * mask for mask in occ_mask], axis=0)
        occupied_ref[:, member * wide_unit : (member + 1) * wide_unit] = lax.dot_general(
            rows[member],
            weights.astype(BF16),
            (((0,), (0,)), ((), ())),
            preferred_element_type=F32,
        ).astype(BF16)
    for member in range(len(rows)):
        virt = wide[member * block_size : (member + 1) * block_size, wide_unit:]
        weights = jnp.concatenate(
            [
                jnp.broadcast_to(virt[nu : nu + 1], virt.shape) * mask
                for mask in virt_mask
                for nu in range(block_size)
            ],
            axis=0,
        )
        at = slice(member * wide_unit, (member + 1) * wide_unit)
        both_ref[:, at] = jnp.dot(
            occupied_ref[:, at], weights.astype(BF16), preferred_element_type=F32
        ).astype(BF16)


def partner_rows(rows_ref, columns, unit_count, chunk):
    found = []
    for unit in range(chunk * CHUNK, (chunk + 1) * CHUNK):
        if unit < unit_count:
            found.append(rows_ref[columns(unit) * BASE + columns(unit_count + unit)])
        else:
            found.append(jnp.zeros(rows_ref.shape[1:], BF16))
    return found


def write_rows(total, pair_at, keep_ref, send_ref):
    half, outer = pair_at % 2, pair_at // 2
    row_count = keep_ref.shape[1]
    parts = [total[at * row_count : (at + 1) * row_count] for at in range(4)]
    keep = [jnp.where(half == 0, parts[2 * at], parts[2 * at + 1]) for at in range(2)]
    send = [jnp.where(half == 0, parts[2 * at + 1], parts[2 * at]) for at in range(2)]
    for ref, both in ((keep_ref, keep), (send_ref, send)):
        ref[0] = jnp.where(outer == 0, both[0], both[1])
        ref[1] = jnp.where(outer == 0, both[1], both[0])


def contract_kernel(unit_count, wide_ref, pair_ref, own_ref, *refs):
    count = len(PAIRS)
    block_refs = refs[:count]
    both_ref, rows_ref, index_ref, occupied_ref, small_ref = refs[count:]
    local_atoms, block_size, _ = own_ref.shape
    aux_count = both_ref.shape[0]
    _, column_at, lanes = small_layout(unit_count, block_size)
    side, half = wide_ref[0], pair_ref[0] % 2
    for slot, (even, odd) in enumerate(PAIRS):
        place = (side ^ jnp.where(half == 0, even, odd)) // 2 * local_atoms
        for atom in range(local_atoms):
            block = block_refs[slot][atom]
            if even == 0:
                block = jnp.where(half == 0, own_ref[atom], block)
            rows_ref[place + atom] = in_rows(block, aux_count)
            small_ref[place + atom] = block[:, block_size * aux_count :]
    atoms = range(count * local_atoms)
    smalls = [small_ref[atom] for atom in atoms]
    row, lane = iota((lanes, 128), 0), iota((lanes, 128), 1)
    join = jnp.where(row == column_at + lane, float(BASE), 0.0)
    join += jnp.where(row == column_at + unit_count + lane, 1.0, 0.0)
    joined = jnp.dot(
        jnp.concatenate(smalls, axis=0), join.astype(BF16), preferred_element_type=F32
    ).astype(jnp.int32)
    contract(
        [rows_ref[atom] for atom in atoms], smalls, weight_parts(block_size, 0), occupied_ref, both_ref
    )
    for atom in atoms:
        for unit in range(unit_count):
            index_ref[atom, unit] = joined[atom * block_size, unit]


def respond_kernel(unit_count, wide_ref, pair_ref, index_ref, own_ref, both_ref, near_ref, *refs):
    count = len(PAIRS)
    far_refs = refs[:count]
    keep_ref, send_ref, rows_ref = refs[count:]
    local_atoms, block_size, _ = own_ref.shape
    aux_count = rows_ref.shape[2]
    side, half = wide_ref[0], pair_ref[0] % 2
    for slot, (even, odd) in enumerate(PAIRS):
        owner = side ^ jnp.where(half == 0, odd, even)
        for atom in range(local_atoms):
            rows_ref[owner * local_atoms + atom] = in_rows(far_refs[slot][atom], aux_count)
    for atom in range(local_atoms):
        rows_ref[side * local_atoms + atom] = in_rows(own_ref[atom], aux_count)
    for place in range(count):
        owner = place * 2 + (side ^ half) % 2
        for atom in range(local_atoms):
            rows_ref[owner * local_atoms + atom] = near_ref[place * local_atoms + atom]
    found = []
    for atom in range(count * local_atoms):
        for unit in range(CHUNK):
            if unit < unit_count:
                found.append(rows_ref[index_ref[atom, unit]])
            else:
                found.append(jnp.zeros(rows_ref.shape[1:], BF16))
    total = jnp.dot(both_ref[...], jnp.concatenate(found, axis=0), preferred_element_type=F32)
    write_rows(total, pair_ref[0], keep_ref, send_ref)


def whole_kernel(wide_count, unit_count, pair_ref, block_ref, *refs):
    keep_ref, send_ref, rows_ref, index_ref, column_ref, occupied_ref, both_ref, sem = refs
    atom_total, block_size, _ = block_ref.shape
    aux_count = rows_ref.shape[2]
    local_atoms = atom_total // wide_count
    chunk_count, column_at, _ = small_layout(unit_count, block_size)
    column_lane = column_at % 128
    half = pair_ref[0] % 2
    group = both_ref.shape[1] // (CHUNK * block_size * block_size)

    def atom_of(position):
        return (position // local_atoms * 2 + half) * local_atoms + position % local_atoms

    @pl.loop(0, atom_total)
    def _(atom):
        rows_ref[atom] = in_rows(block_ref[atom], aux_count)
        index_ref[atom] = digits_of(block_ref[atom, :, block_size * aux_count :], column_at)

    copy = pltpu.make_async_copy(index_ref, column_ref, sem)
    copy.start()
    copy.wait()

    def work(step, total):
        atoms = [atom_of(step * group + member) for member in range(group)]
        for chunk in range(chunk_count):
            lane_at = chunk * 2 * CHUNK * block_size
            tile = block_size * aux_count + lane_at // 128 * 128
            parts = weight_parts(block_size, lane_at % 128)
            smalls = [block_ref[atom, :, tile : tile + 128] for atom in atoms]
            contract([rows_ref[atom] for atom in atoms], smalls, parts, occupied_ref, both_ref)
            found = []
            for atom in atoms:
                found += partner_rows(
                    rows_ref, lambda lane: column_ref[atom, 0, column_lane + lane], unit_count, chunk
                )
            total += jnp.dot(
                both_ref[...], jnp.concatenate(found, axis=0), preferred_element_type=F32
            )
        return total

    total = jnp.zeros((aux_count, aux_count), F32)
    total = lax.fori_loop(0, atom_total // 2 // group, work, total)
    write_rows(total, pair_ref[0], keep_ref, send_ref)


VMEM = pl.BlockSpec(memory_space=pltpu.VMEM)
SMEM = pl.BlockSpec(memory_space=pltpu.SMEM)


def scalar(value):
    return value.astype(jnp.int32).reshape(1)


PAIRS = ((4, 5), (6, 7), (2, 3), (0, 1))


def respond_direct(block, wide_at, pair_at, unit_count, wide_count, pair_count, aux_count):
    local_atoms, block_size, width = block.shape
    square = block_size * block_size
    partner = [(p, p ^ 1) for p in range(pair_count)]
    fetched, far = [], []
    for even, odd in PAIRS:
        route = [
            ((w ^ d) * pair_count + p, w * pair_count + p)
            for w in range(wide_count)
            for p in range(pair_count)
            for d in (odd if p % 2 else even,)
            if d
        ]
        fetched.append(lax.ppermute(block, ("wide", "pair"), route))
        far.append(lax.ppermute(fetched[-1], "pair", partner))
    near_atoms = len(PAIRS) * local_atoms
    both, near, index = pl.pallas_call(
        functools.partial(contract_kernel, unit_count),
        out_shape=(
            pltpu.VMEM((aux_count, near_atoms * CHUNK * square), BF16),
            pltpu.VMEM((near_atoms, square, aux_count), BF16),
            pltpu.SMEM((near_atoms, unit_count), jnp.int32),
        ),
        in_specs=[SMEM, SMEM] + [VMEM] * (1 + len(PAIRS)),
        out_specs=(VMEM, VMEM, SMEM),
        scratch_shapes=[
            pltpu.VMEM((aux_count, near_atoms * CHUNK * square), BF16),
            pltpu.VMEM((near_atoms, block_size, width - block_size * aux_count), BF16),
        ],
        name="contract",
    )(wide_at, pair_at, *[in_vmem(value) for value in [block] + fetched])
    part = pltpu.VMEM((2, aux_count // pair_count, aux_count), F32)
    return pl.pallas_call(
        functools.partial(respond_kernel, unit_count),
        out_shape=(part, part),
        in_specs=[SMEM, SMEM, SMEM] + [VMEM] * (3 + len(PAIRS)),
        out_specs=(VMEM, VMEM),
        scratch_shapes=[pltpu.VMEM((wide_count * local_atoms, square, aux_count), BF16)],
        name="respond",
    )(
        wide_at,
        pair_at,
        pltpu.with_memory_space_constraint(index, pltpu.SMEM),
        *[in_vmem(value) for value in [block, both, near] + far],
    )


def respond_whole(block, pair_at, unit_count, wide_count, pair_count, aux_count):
    local_atoms, block_size, width = block.shape
    square = block_size * block_size
    chunk_count, column_at, _ = small_layout(unit_count, block_size)
    index_lanes = width - block_size * aux_count - column_at // 128 * 128
    atom_total = wide_count * local_atoms
    group = max(1, min(local_atoms, 16 // chunk_count))
    group_lanes = group * CHUNK * square
    part = pltpu.VMEM((2, aux_count // pair_count, aux_count), F32)
    return pl.pallas_call(
        functools.partial(whole_kernel, wide_count, unit_count),
        out_shape=(part, part),
        in_specs=[SMEM, VMEM],
        out_specs=(VMEM, VMEM),
        scratch_shapes=[
            pltpu.VMEM((atom_total, square, aux_count), BF16),
            pltpu.VMEM((atom_total, 1, index_lanes), jnp.int32),
            pltpu.SMEM((atom_total, 1, index_lanes), jnp.int32),
            pltpu.VMEM((aux_count, group_lanes), BF16),
            pltpu.VMEM((aux_count, group_lanes), BF16),
            pltpu.SemaphoreType.DMA,
        ],
        compiler_params=pltpu.CompilerParams(vmem_limit_bytes=56 * 2**20),
        name="whole",
    )(pair_at, lax.all_gather(block, "wide", axis=0, tiled=True))


def in_vmem(value):
    return pltpu.with_memory_space_constraint(value, pltpu.VMEM)


def local(three_center, occ_green, virt_green, occ_column, partner_live):
    local_atoms, block_size, wide_row = three_center.shape
    own_units = occ_green.shape[1]
    aux_count = wide_row // block_size
    wide_count, pair_count = lax.axis_size("wide"), lax.axis_size("pair")
    unit_count = 2 * own_units
    _, _, lanes = small_layout(unit_count, block_size)
    wide_at = scalar(lax.axis_index("wide"))
    pair_at = scalar(lax.axis_index("pair"))
    partner = [(p, p ^ 1) for p in range(pair_count)]

    block, small = pl.pallas_call(
        pack_kernel,
        out_shape=(
            pltpu.VMEM((local_atoms, block_size, wide_row + lanes), BF16),
            pltpu.VMEM((local_atoms, block_size, lanes), BF16),
        ),
        in_specs=[SMEM, SMEM, SMEM, VMEM, VMEM, VMEM],
        out_specs=(VMEM, VMEM),
        name="pack",
    )(pair_at, occ_column.T, partner_live.T, three_center, occ_green, virt_green)
    merged = small + lax.ppermute(small, "pair", partner)
    block = lax.dynamic_update_slice(block, merged, (0, 0, wide_row))
    if wide_count == 8 and unit_count <= CHUNK:
        keep, send = respond_direct(
            block, wide_at, pair_at, unit_count, wide_count, pair_count, aux_count
        )
    else:
        keep, send = respond_whole(block, pair_at, unit_count, wide_count, pair_count, aux_count)
    summed = keep + lax.ppermute(send, "pair", partner)
    other = [(p, p ^ 2) for p in range(pair_count)]
    return summed[0] + lax.ppermute(summed[1], "pair", other)


def solution(mesh):
    placed = (
        P("wide", None, None),
        P("wide", "pair", None, None),
        P("wide", "pair", None, None),
        P("wide", "pair"),
        P("wide", "pair"),
    )
    return jax.shard_map(
        local, mesh=mesh, in_specs=placed, out_specs=P("pair", None), check_vma=False
    )
```

time: 28.2 us -> 22 us (0.78)
  starting transfers between devices: 15.4 us -> 12.2 us
  Pallas kernels: 4.66 us -> 2.47 us
  waiting for transfers between devices: 7.27 us -> 6.46 us
    ppermute x8, starting transfers between devices: 12.9 us -> 9.56 us  [the longest x4 6.21 us: respond_direct(): fetched.append(lax.ppermute(block, ('wide', 'pair'), route))]
    pallas_call x1 -> x2, Pallas kernels: 3.65 us -> 1.46 us  [the longest x1 0.94 us: respond_direct(): pl.pallas_call(functools.partial(contract_kernel, unit_count), out_shape=...]
    ppermute x8, waiting for transfers between devices: 3.33 us -> 2.69 us  [the longest x4 2.68 us: respond_direct(): fetched.append(lax.ppermute(block, ('wide', 'pair'), route))]
  transfers between devices with their start and end apart: 11 -> 11, of which waited for: 6 -> 6; matrix products, arithmetic and copies ran while one was open for 0% -> 0% of each run, Pallas kernels for 0% -> 4%
where the time goes in v4:
time: 22 us; the launch traced here: 21.8 us
  starting transfers between devices  12.2 us (55%)
  waiting for transfers between devices  6.46 us (29%)
  Pallas kernels  2.47 us (11%)
  other arithmetic  0.63 us (3%)
    ppermute x4, starting transfers between devices, respond_direct(): fetched.append(lax.ppermute(block, ('wide', 'pair'), route))  6.21 us
    ppermute x4, starting transfers between devices, respond_direct(): far.append(lax.ppermute(fetched[-1], 'pair', partner))  3.34 us
    ppermute x4, waiting for transfers between devices, respond_direct(): fetched.append(lax.ppermute(block, ('wide', 'pair'), route))  2.68 us
    ppermute x1, waiting for transfers between devices, local(): return summed[0] + lax.ppermute(summed[1], 'pair', other)  2.01 us
    ppermute x1, starting transfers between devices, local(): return summed[0] + lax.ppermute(summed[1], 'pair', other)  1.8 us
    pallas_call x1, Pallas kernels, local(): pl.pallas_call(pack_kernel, out_shape=(pltpu.VMEM((local_atoms, block_siz...  1.01 us
    pallas_call x1, Pallas kernels, respond_direct(): pl.pallas_call(functools.partial(contract_kernel, unit_count), out_shape=...  0.94 us
    ppermute x1, waiting for transfers between devices, local(): summed = keep + lax.ppermute(send, 'pair', partner)  0.94 us
  transfers between devices with their start and end apart: 11, of which 6 were waited for; matrix products, arithmetic and copies ran while one was open for 0% of the time, Pallas kernels for 4%

profile of v4, /device:TPU:0, one launch (start us, length us, event | category | flops | bytes accessed | tf_op | source)
XLA Modules:
  0.0 21.8 jit_solution(14795057681174938303)
XLA Ops:
  0.0 1.0 %pack.1 = (bf16[4,8,1152]{2,1,0:T(8,128)(2,1)S(1)}, bf16[4,8,128]{2,1,0:T(8,128)(2,1)S(1)}) custom-call(s32[1]{0:T(128)} %bitcast.1.pair_ref, s32[2,4]{1,0:T(2,128)} %bitcast.10, s32[2,4]{1,0:T(2,128)} %bitcast.11, bf16[4,8,1024]{2,1,0:T(8,128)(2,1)} %tc_ref.1, bf16[4,2,8,8]{3,2,1,0:T(8,128)(2,1)} %occ_ref.1, bf16[4,2,8,8]{3,2,1,0:T(8,128)(2,1)} %virt_ref.1), custom_call_target="tpu_custom_call" | custom-call | tf_op jit(solution)/shard_map/pack/pallas_call | solution.py:350
  1.0 0.5 %collective-permute-start = (bf16[4,8,128]{2,1,0:T(8,128)(2,1)S(1)}, bf16[4,8,128]{2,1,0:T(8,128)(2,1)S(1)}, u32[]{:S(2)}, u32[]{:S(2)}) collective-permute-start(bf16[4,8,128]{2,1,0:T(8,128)(2,1)S(1)} %get-tuple-element.13), channel_id=1, source_target_pairs={{0,1},{1,0},{2,3},{3,2},{4,5},{5,4},{6,7},{7,6},{8,9},{9,8},{10,11... | collective-permute-start | bytes 24584 | tf_op jit(solution)/shard_map/ppermute | solution.py:360
  1.5 0.8 %collective-permute-done = bf16[4,8,128]{2,1,0:T(8,128)(2,1)S(1)} collective-permute-done((bf16[4,8,128]{2,1,0:T(8,128)(2,1)S(1)}, bf16[4,8,128]{2,1,0:T(8,128)(2,1)S(1)}, u32[]{:S(2)}, u32[]{:S(2)}) %collective-permute-start) | collective-permute-done | bytes 8224 | tf_op jit(solution)/shard_map/ppermute | solution.py:360
  2.4 4.0 %collective-permute-start.1 = (bf16[4,8,1152]{2,1,0:T(8,128)(2,1)S(1)}, bf16[4,8,1152]{2,1,0:T(8,128)(2,1)S(1)}, u32[]{:S(2)}, u32[]{:S(2)}) collective-permute-start(bf16[4,8,1152]{2,1,0:T(8,128)(2,1)S(1)} %add_dynamic-update-slice_fusion.own_ref), channel_id=1, source_target_pairs={{16,0},{21,1},{18,2},{23,3},{20,4},{17,5},{22,6},{19,7},{24,8},{29... | collective-permute-start | bytes 221192 | tf_op jit(solution)/shard_map/ppermute | solution.py:274
  6.4 1.3 %collective-permute-start.2 = (bf16[4,8,1152]{2,1,0:T(8,128)(2,1)S(1)}, bf16[4,8,1152]{2,1,0:T(8,128)(2,1)S(1)}, u32[]{:S(2)}, u32[]{:S(2)}) collective-permute-start(bf16[4,8,1152]{2,1,0:T(8,128)(2,1)S(1)} %add_dynamic-update-slice_fusion.own_ref), channel_id=1, source_target_pairs={{24,0},{29,1},{26,2},{31,3},{28,4},{25,5},{30,6},{27,7},{16,8},{21... | collective-permute-start | bytes 221192 | tf_op jit(solution)/shard_map/ppermute | solution.py:274
  7.7 0.2 %collective-permute-start.3 = (bf16[4,8,1152]{2,1,0:T(8,128)(2,1)S(1)}, bf16[4,8,1152]{2,1,0:T(8,128)(2,1)S(1)}, u32[]{:S(2)}, u32[]{:S(2)}) collective-permute-start(bf16[4,8,1152]{2,1,0:T(8,128)(2,1)S(1)} %add_dynamic-update-slice_fusion.own_ref), channel_id=1, source_target_pairs={{8,0},{13,1},{10,2},{15,3},{12,4},{9,5},{14,6},{11,7},{0,8},{5,9},... | collective-permute-start | bytes 221192 | tf_op jit(solution)/shard_map/ppermute | solution.py:274
  7.9 0.7 %collective-permute-start.4 = (bf16[4,8,1152]{2,1,0:T(8,128)(2,1)S(1)}, bf16[4,8,1152]{2,1,0:T(8,128)(2,1)S(1)}, u32[]{:S(2)}, u32[]{:S(2)}) collective-permute-start(bf16[4,8,1152]{2,1,0:T(8,128)(2,1)S(1)} %add_dynamic-update-slice_fusion.own_ref), channel_id=1, source_target_pairs={{5,1},{7,3},{1,5},{3,7},{13,9},{15,11},{9,13},{11,15},{21,17},{23,... | collective-permute-start | bytes 221192 | tf_op jit(solution)/shard_map/ppermute | solution.py:274
  8.6 0.5 %collective-permute-done.1.refs_0_ = bf16[4,8,1152]{2,1,0:T(8,128)(2,1)S(1)} collective-permute-done((bf16[4,8,1152]{2,1,0:T(8,128)(2,1)S(1)}, bf16[4,8,1152]{2,1,0:T(8,128)(2,1)S(1)}, u32[]{:S(2)}, u32[]{:S(2)}) %collective-permute-start.1) | collective-permute-done | bytes 73760 | tf_op jit(solution)/shard_map/ppermute | solution.py:274
  9.1 2.5 %collective-permute-start.5 = (bf16[4,8,1152]{2,1,0:T(8,128)(2,1)S(1)}, bf16[4,8,1152]{2,1,0:T(8,128)(2,1)S(1)}, u32[]{:S(2)}, u32[]{:S(2)}) collective-permute-start(bf16[4,8,1152]{2,1,0:T(8,128)(2,1)S(1)} %collective-permute-done.1.refs_0_), channel_id=1, source_target_pairs={{0,1},{1,0},{2,3},{3,2},{4,5},{5,4},{6,7},{7,6},{8,9},{9,8},{10,11... | collective-permute-start | bytes 221192 | tf_op jit(solution)/shard_map/ppermute | solution.py:275
  11.6 1.7 %collective-permute-done.2.refs_1_ = bf16[4,8,1152]{2,1,0:T(8,128)(2,1)S(1)} collective-permute-done((bf16[4,8,1152]{2,1,0:T(8,128)(2,1)S(1)}, bf16[4,8,1152]{2,1,0:T(8,128)(2,1)S(1)}, u32[]{:S(2)}, u32[]{:S(2)}) %collective-permute-start.2) | collective-permute-done | bytes 73760 | tf_op jit(solution)/shard_map/ppermute | solution.py:274
  13.3 0.4 %collective-permute-start.6 = (bf16[4,8,1152]{2,1,0:T(8,128)(2,1)S(1)}, bf16[4,8,1152]{2,1,0:T(8,128)(2,1)S(1)}, u32[]{:S(2)}, u32[]{:S(2)}) collective-permute-start(bf16[4,8,1152]{2,1,0:T(8,128)(2,1)S(1)} %collective-permute-done.2.refs_1_), channel_id=1, source_target_pairs={{0,1},{1,0},{2,3},{3,2},{4,5},{5,4},{6,7},{7,6},{8,9},{9,8},{10,11... | collective-permute-start | bytes 221192 | tf_op jit(solution)/shard_map/ppermute | solution.py:275
  13.7 0.4 %collective-permute-done.3.refs_2_ = bf16[4,8,1152]{2,1,0:T(8,128)(2,1)S(1)} collective-permute-done((bf16[4,8,1152]{2,1,0:T(8,128)(2,1)S(1)}, bf16[4,8,1152]{2,1,0:T(8,128)(2,1)S(1)}, u32[]{:S(2)}, u32[]{:S(2)}) %collective-permute-start.3) | collective-permute-done | bytes 73760 | tf_op jit(solution)/shard_map/ppermute | solution.py:274
  14.1 0.2 collective-permute-start.7
  14.3 0.0 collective-permute-done.4.refs_3_
  14.3 0.4 %collective-permute-start.8 = (bf16[4,8,1152]{2,1,0:T(8,128)(2,1)S(1)}, bf16[4,8,1152]{2,1,0:T(8,128)(2,1)S(1)}, u32[]{:S(2)}, u32[]{:S(2)}) collective-permute-start(bf16[4,8,1152]{2,1,0:T(8,128)(2,1)S(1)} %collective-permute-done.4.refs_3_), channel_id=1, source_target_pairs={{0,1},{1,0},{2,3},{3,2},{4,5},{5,4},{6,7},{7,6},{8,9},{9,8},{10,11... | collective-permute-start | bytes 221192 | tf_op jit(solution)/shard_map/ppermute | solution.py:275
  14.6 0.9 %contract.1 = (bf16[128,4096]{1,0:T(8,128)(2,1)S(1)}, bf16[16,64,128]{2,1,0:T(8,128)(2,1)S(1)}, s32[16,4]{1,0:T(8,128)S(4)}) custom-call(s32[1]{0:T(128)} %bitcast.wide_ref, s32[1]{0:T(128)} %bitcast.1.pair_ref, bf16[4,8,1152]{2,1,0:T(8,128)(2,1)S(1)} %add_dynamic-update-slice_fusion.own_ref, bf16[4,8,1152]{2,1,0:T(8,128)(2,1)S(1)} %collective-permute-done.1.refs_0_, ...), custom_call_target="tpu_custom_call" | custom-call | tf_op jit(solution)/shard_map/contract/pallas_call | solution.py:277
  15.6 0.0 collective-permute-done.6.refs_1_
  15.6 0.0 collective-permute-done.7.refs_2_
  15.6 0.5 %respond.1 = (f32[2,32,128]{2,1,0:T(8,128)S(1)}, f32[2,32,128]{2,1,0:T(8,128)S(1)}) custom-call(s32[1]{0:T(128)} %bitcast.wide_ref, s32[1]{0:T(128)} %bitcast.1.pair_ref, s32[16,4]{1,0:T(8,128)S(4)} %get-tuple-element.14.index_ref, bf16[4,8,1152]{2,1,0:T(8,128)(2,1)S(1)} %add_dynamic-update-slice_fusion.own_ref, ...), custom_call_target="tpu_custom_call" | custom-call | tf_op jit(solution)/shard_map/respond/pallas_call | solution.py:293
  16.1 0.3 %collective-permute-start.9 = (f32[2,32,128]{2,1,0:T(8,128)S(1)}, f32[2,32,128]{2,1,0:T(8,128)S(1)}, u32[]{:S(2)}, u32[]{:S(2)}) collective-permute-start(f32[2,32,128]{2,1,0:T(8,128)S(1)} %get-tuple-element.18), channel_id=1, source_target_pairs={{0,1},{1,0},{2,3},{3,2},{4,5},{5,4},{6,7},{7,6},{8,9},{9,8},{10,11... | collective-permute-start | bytes 98312 | tf_op jit(solution)/shard_map/ppermute | solution.py:368
  16.5 0.9 %collective-permute-done.9 = f32[2,32,128]{2,1,0:T(8,128)S(1)} collective-permute-done((f32[2,32,128]{2,1,0:T(8,128)S(1)}, f32[2,32,128]{2,1,0:T(8,128)S(1)}, u32[]{:S(2)}, u32[]{:S(2)}) %collective-permute-start.9) | collective-permute-done | bytes 32800 | tf_op jit(solution)/shard_map/ppermute | solution.py:368
  17.4 1.8 %collective-permute-start.10 = (f32[32,128]{1,0:T(8,128)S(1)}, f32[32,128]{1,0:T(8,128)S(1)}, u32[]{:S(2)}, u32[]{:S(2)}) collective-permute-start(f32[32,128]{1,0:T(8,128)S(1)} %slice_bitcast_fusion), channel_id=1, source_target_pairs={{0,2},{1,3},{2,0},{3,1},{4,6},{5,7},{6,4},{7,5},{8,10},{9,11},{10,... | collective-permute-start | bytes 49160 | tf_op jit(solution)/shard_map/ppermute | solution.py:370
  19.2 2.0 %collective-permute-done.10 = f32[32,128]{1,0:T(8,128)S(1)} collective-permute-done((f32[32,128]{1,0:T(8,128)S(1)}, f32[32,128]{1,0:T(8,128)S(1)}, u32[]{:S(2)}, u32[]{:S(2)}) %collective-permute-start.10) | collective-permute-done | bytes 16416 | tf_op jit(solution)/shard_map/ppermute | solution.py:370
  21.2 0.6 %fusion = f32[32,128]{1,0:T(8,128)} fusion(f32[32,128]{1,0:T(8,128)S(1)} %collective-permute-done.10, f32[2,32,128]{2,1,0:T(8,128)S(1)} %add.10), kind=kLoop, calls=%fused_computation.2 | loop fusion | flops 4096 | bytes 49152 | tf_op jit(solution)/shard_map/add | solution.py:370
  (5 shorter events, 0.0 us)
Async XLA Ops:
  1.0 1.3 %collective-permute-start = (bf16[4,8,128]{2,1,0:T(8,128)(2,1)S(1)}, bf16[4,8,128]{2,1,0:T(8,128)(2,1)S(1)}, u32[]{:S(2)}, u32[]{:S(2)}) collective-permute-start(bf16[4,8,128]{2,1,0:T(8,128)(2,1)S(1)} %get-tuple-element.13), channel_id=1, source_target_pairs={{0,1},{1,0},{2,3},{3,2},{4,5},{5,4},{6,7},{7,6},{8,9},{9,8},{10,11... | collective-permute-start | bytes 24584 | tf_op jit(solution)/shard_map/ppermute | solution.py:360
  2.4 6.8 %collective-permute-start.1 = (bf16[4,8,1152]{2,1,0:T(8,128)(2,1)S(1)}, bf16[4,8,1152]{2,1,0:T(8,128)(2,1)S(1)}, u32[]{:S(2)}, u32[]{:S(2)}) collective-permute-start(bf16[4,8,1152]{2,1,0:T(8,128)(2,1)S(1)} %add_dynamic-update-slice_fusion.own_ref), channel_id=1, source_target_pairs={{16,0},{21,1},{18,2},{23,3},{20,4},{17,5},{22,6},{19,7},{24,8},{29... | collective-permute-start | bytes 221192 | tf_op jit(solution)/shard_map/ppermute | solution.py:274
  6.4 7.0 %collective-permute-start.2 = (bf16[4,8,1152]{2,1,0:T(8,128)(2,1)S(1)}, bf16[4,8,1152]{2,1,0:T(8,128)(2,1)S(1)}, u32[]{:S(2)}, u32[]{:S(2)}) collective-permute-start(bf16[4,8,1152]{2,1,0:T(8,128)(2,1)S(1)} %add_dynamic-update-slice_fusion.own_ref), channel_id=1, source_target_pairs={{24,0},{29,1},{26,2},{31,3},{28,4},{25,5},{30,6},{27,7},{16,8},{21... | collective-permute-start | bytes 221192 | tf_op jit(solution)/shard_map/ppermute | solution.py:274
  7.7 6.4 %collective-permute-start.3 = (bf16[4,8,1152]{2,1,0:T(8,128)(2,1)S(1)}, bf16[4,8,1152]{2,1,0:T(8,128)(2,1)S(1)}, u32[]{:S(2)}, u32[]{:S(2)}) collective-permute-start(bf16[4,8,1152]{2,1,0:T(8,128)(2,1)S(1)} %add_dynamic-update-slice_fusion.own_ref), channel_id=1, source_target_pairs={{8,0},{13,1},{10,2},{15,3},{12,4},{9,5},{14,6},{11,7},{0,8},{5,9},... | collective-permute-start | bytes 221192 | tf_op jit(solution)/shard_map/ppermute | solution.py:274
  7.9 6.3 %collective-permute-start.4 = (bf16[4,8,1152]{2,1,0:T(8,128)(2,1)S(1)}, bf16[4,8,1152]{2,1,0:T(8,128)(2,1)S(1)}, u32[]{:S(2)}, u32[]{:S(2)}) collective-permute-start(bf16[4,8,1152]{2,1,0:T(8,128)(2,1)S(1)} %add_dynamic-update-slice_fusion.own_ref), channel_id=1, source_target_pairs={{5,1},{7,3},{1,5},{3,7},{13,9},{15,11},{9,13},{11,15},{21,17},{23,... | collective-permute-start | bytes 221192 | tf_op jit(solution)/shard_map/ppermute | solution.py:274
  9.1 6.4 %collective-permute-start.5 = (bf16[4,8,1152]{2,1,0:T(8,128)(2,1)S(1)}, bf16[4,8,1152]{2,1,0:T(8,128)(2,1)S(1)}, u32[]{:S(2)}, u32[]{:S(2)}) collective-permute-start(bf16[4,8,1152]{2,1,0:T(8,128)(2,1)S(1)} %collective-permute-done.1.refs_0_), channel_id=1, source_target_pairs={{0,1},{1,0},{2,3},{3,2},{4,5},{5,4},{6,7},{7,6},{8,9},{9,8},{10,11... | collective-permute-start | bytes 221192 | tf_op jit(solution)/shard_map/ppermute | solution.py:275
  13.3 2.2 %collective-permute-start.6 = (bf16[4,8,1152]{2,1,0:T(8,128)(2,1)S(1)}, bf16[4,8,1152]{2,1,0:T(8,128)(2,1)S(1)}, u32[]{:S(2)}, u32[]{:S(2)}) collective-permute-start(bf16[4,8,1152]{2,1,0:T(8,128)(2,1)S(1)} %collective-permute-done.2.refs_1_), channel_id=1, source_target_pairs={{0,1},{1,0},{2,3},{3,2},{4,5},{5,4},{6,7},{7,6},{8,9},{9,8},{10,11... | collective-permute-start | bytes 221192 | tf_op jit(solution)/shard_map/ppermute | solution.py:275
  14.1 1.5 %collective-permute-start.7 = (bf16[4,8,1152]{2,1,0:T(8,128)(2,1)S(1)}, bf16[4,8,1152]{2,1,0:T(8,128)(2,1)S(1)}, u32[]{:S(2)}, u32[]{:S(2)}) collective-permute-start(bf16[4,8,1152]{2,1,0:T(8,128)(2,1)S(1)} %collective-permute-done.3.refs_2_), channel_id=1, source_target_pairs={{0,1},{1,0},{2,3},{3,2},{4,5},{5,4},{6,7},{7,6},{8,9},{9,8},{10,11... | collective-permute-start | bytes 221192 | tf_op jit(solution)/shard_map/ppermute | solution.py:275
  14.3 1.3 %collective-permute-start.8 = (bf16[4,8,1152]{2,1,0:T(8,128)(2,1)S(1)}, bf16[4,8,1152]{2,1,0:T(8,128)(2,1)S(1)}, u32[]{:S(2)}, u32[]{:S(2)}) collective-permute-start(bf16[4,8,1152]{2,1,0:T(8,128)(2,1)S(1)} %collective-permute-done.4.refs_3_), channel_id=1, source_target_pairs={{0,1},{1,0},{2,3},{3,2},{4,5},{5,4},{6,7},{7,6},{8,9},{9,8},{10,11... | collective-permute-start | bytes 221192 | tf_op jit(solution)/shard_map/ppermute | solution.py:275
  16.1 1.3 %collective-permute-start.9 = (f32[2,32,128]{2,1,0:T(8,128)S(1)}, f32[2,32,128]{2,1,0:T(8,128)S(1)}, u32[]{:S(2)}, u32[]{:S(2)}) collective-permute-start(f32[2,32,128]{2,1,0:T(8,128)S(1)} %get-tuple-element.18), channel_id=1, source_target_pairs={{0,1},{1,0},{2,3},{3,2},{4,5},{5,4},{6,7},{7,6},{8,9},{9,8},{10,11... | collective-permute-start | bytes 98312 | tf_op jit(solution)/shard_map/ppermute | solution.py:368
  17.4 3.8 %collective-permute-start.10 = (f32[32,128]{1,0:T(8,128)S(1)}, f32[32,128]{1,0:T(8,128)S(1)}, u32[]{:S(2)}, u32[]{:S(2)}) collective-permute-start(f32[32,128]{1,0:T(8,128)S(1)} %slice_bitcast_fusion), channel_id=1, source_target_pairs={{0,2},{1,3},{2,0},{3,1},{4,6},{5,7},{6,4},{7,5},{8,10},{9,11},{10,... | collective-permute-start | bytes 49160 | tf_op jit(solution)/shard_map/ppermute | solution.py:370

commit v5 on v4

v5 whole, which is shorter than its diff:
```python
import jax
import jax.numpy as jnp
from jax import lax
from jax.experimental import pallas as pl
from jax.experimental.pallas import tpu as pltpu
from jax.sharding import PartitionSpec as P

CHUNK = 4
BASE = 256
PAIRS = ((4, 5), (6, 7), (0, 1), (2, 3))
F32, BF16 = jnp.float32, jnp.bfloat16
VMEM = pl.BlockSpec(memory_space=pltpu.VMEM)
SMEM = pl.BlockSpec(memory_space=pltpu.SMEM)


def ceil_to(value, step):
    return -(-value // step) * step


def iota(shape, axis):
    return lax.broadcasted_iota(jnp.int32, shape, axis)


def scalar(value):
    return value.astype(jnp.int32).reshape(1)


def in_vmem(value):
    return pltpu.with_memory_space_constraint(value, pltpu.VMEM)


def small_layout(unit_count, block_size):
    chunk_count = -(-unit_count // CHUNK)
    column_at = ceil_to(chunk_count * 2 * CHUNK * block_size, 128)
    return chunk_count, column_at, ceil_to(column_at + 2 * unit_count, 128)


def pack_kernel(unit_count, pair_ref, column_ref, live_ref, tc_ref, occ_ref, virt_ref, block_ref, small_ref):
    local_atoms, own_units, block_size, _ = occ_ref.shape
    wide_row = tc_ref.shape[2]
    _, column_at, lanes = small_layout(unit_count, block_size)
    row, lane = iota((block_size, lanes), 0), iota((block_size, lanes), 1)
    packed = jnp.zeros((local_atoms * block_size, lanes), F32)
    columns = [jnp.zeros((block_size, lanes), F32) for _ in range(local_atoms)]
    for slot in range(own_units):
        unit = pair_ref[0] * own_units + slot
        at = (unit // CHUNK) * (2 * CHUNK * block_size) + (unit % CHUNK) * block_size
        occ = jnp.concatenate(
            [
                occ_ref[atom, slot].astype(F32) * live_ref[slot, atom].astype(F32)
                for atom in range(local_atoms)
            ],
            axis=0,
        ).astype(BF16)
        virt = jnp.concatenate(
            [virt_ref[atom, slot].astype(F32) for atom in range(local_atoms)], axis=0
        ).astype(BF16)
        occ_place = (lane == at + row).astype(BF16)
        virt_place = (lane == at + CHUNK * block_size + row).astype(BF16)
        packed += jnp.dot(occ, occ_place, preferred_element_type=F32)
        packed += jnp.dot(virt, virt_place, preferred_element_type=F32)
        for atom in range(local_atoms):
            column = column_ref[slot, atom]
            high = column // BASE
            low = column - high * BASE
            columns[atom] += jnp.where(lane == column_at + unit, high.astype(F32), 0.0)
            columns[atom] += jnp.where(
                lane == column_at + unit_count + unit, low.astype(F32), 0.0
            )
    packed = (packed + jnp.concatenate(columns, axis=0)).astype(BF16)
    packed = packed.reshape(local_atoms, block_size, lanes)
    block_ref[:, :, :wide_row] = tc_ref[...]
    block_ref[:, :, wide_row:] = packed
    small_ref[...] = packed


def in_rows(block, aux_count):
    parts = range(block.shape[0])
    return jnp.concatenate([block[:, at * aux_count : (at + 1) * aux_count] for at in parts], axis=0)


def own_rows(rows, outer, row_count):
    found = rows[:, :row_count]
    for at in range(1, rows.shape[1] // row_count):
        found = jnp.where(outer == at, rows[:, at * row_count : (at + 1) * row_count], found)
    return found


def turned(rows):
    found = []
    for at in range(0, len(rows), 2):
        both = jnp.concatenate(rows[at : at + 2], axis=1).T
        found += jnp.split(both, len(rows[at : at + 2]), axis=0)
    return found


def weight_parts(block_size, lane_at):
    square = block_size * block_size
    wide_unit = CHUNK * square
    row, lane = iota((128, 2 * wide_unit), 0), iota((128, 2 * wide_unit), 1)
    inner = lane % wide_unit
    unit, upper, lower = inner // square, (inner // block_size) % block_size, inner % block_size
    within = jnp.where(lane >= wide_unit, upper + CHUNK * block_size, lower)
    spread = (row == unit * block_size + within + lane_at).astype(BF16)
    row, lane = iota((block_size, wide_unit), 0), iota((block_size, wide_unit), 1)
    unit, upper, lower = lane // square, (lane // block_size) % block_size, lane % block_size
    occ_mask = [(upper == at).astype(F32) for at in range(block_size)]
    virt_mask = [((unit == at) & (lower == row)).astype(F32) for at in range(CHUNK)]
    return spread, occ_mask, virt_mask


def contract(rows, smalls, parts, occupied_ref, both_ref, first):
    spread, occ_mask, virt_mask = parts
    block_size, wide_unit = occ_mask[0].shape
    wide = jnp.dot(jnp.concatenate(smalls, axis=0), spread, preferred_element_type=F32)
    for member in range(len(rows)):
        occ = wide[member * block_size : (member + 1) * block_size, :wide_unit]
        weights = jnp.concatenate([occ * mask for mask in occ_mask], axis=0)
        at = slice(first + member * wide_unit, first + (member + 1) * wide_unit)
        occupied_ref[:, at] = jnp.dot(
            rows[member], weights.astype(BF16), preferred_element_type=F32
        ).astype(BF16)
    for member in range(len(rows)):
        virt = wide[member * block_size : (member + 1) * block_size, wide_unit:]
        half = wide_unit // 2
        for part in range(2):
            some = virt[:, part * half : (part + 1) * half]
            weights = jnp.concatenate(
                [
                    jnp.broadcast_to(some[nu : nu + 1], some.shape) * mask[:, :half]
                    for mask in virt_mask[: CHUNK // 2]
                    for nu in range(block_size)
                ],
                axis=0,
            )
            at = first + member * wide_unit + part * half
            both_ref[:, at : at + half] = jnp.dot(
                occupied_ref[:, at : at + half], weights.astype(BF16), preferred_element_type=F32
            ).astype(BF16)


def join_columns(digits, unit_count):
    row, lane = (iota((digits.shape[1], ceil_to(unit_count, 128)), axis) for axis in range(2))
    join = jnp.where(row == lane, float(BASE), 0.0) + jnp.where(row == unit_count + lane, 1.0, 0.0)
    join = jnp.where(lane < unit_count, join, 0.0).astype(BF16)
    return jnp.dot(digits, join, preferred_element_type=F32).astype(jnp.int32)


def write_rows(total, half, keep_ref, send_ref):
    row_count = keep_ref.shape[0]
    keep_ref[...] = jnp.where(half == 0, total[:row_count], total[row_count:])
    send_ref[...] = jnp.where(half == 0, total[row_count:], total[:row_count])


def kernel_of(function, *sizes):
    def kernel(*refs):
        function(*sizes, *refs)

    return kernel


def contract_kernel(unit_count, wide_ref, pair_ref, own_ref, early_ref, *refs):
    count = len(PAIRS)
    block_refs = refs[:count]
    both_ref, rows_ref, index_ref, occupied_ref, small_ref = refs[count:]
    local_atoms, block_size, _ = own_ref.shape
    aux_count, row_count = rows_ref.shape[2], both_ref.shape[0]
    chunk_count, column_at, lanes = small_layout(unit_count, block_size)
    side, half, outer = wide_ref[0], pair_ref[0] % 2, pair_ref[0] // 2
    for slot, (even, odd) in enumerate(PAIRS):
        place = (side ^ jnp.where(half == 0, even, odd)) // 2 * local_atoms
        for atom in range(local_atoms):
            block = block_refs[slot][atom]
            if even == 0:
                block = jnp.where(half == 0, own_ref[atom], block)
            rows_ref[place + atom] = in_rows(block, aux_count)
            small = block[:, block_size * aux_count :]
            small_ref[place + atom] = early_ref[atom] if slot == 0 else small
    atoms = range(count * local_atoms)
    rows = turned([own_rows(rows_ref[atom], outer, row_count) for atom in atoms])
    for chunk in range(chunk_count):
        lane_at = chunk * 2 * CHUNK * block_size
        tile = lane_at // 128 * 128
        smalls = [small_ref[atom, :, tile : tile + 128] for atom in atoms]
        first = chunk * len(atoms) * CHUNK * block_size * block_size
        contract(
            rows, smalls, weight_parts(block_size, lane_at - tile), occupied_ref, both_ref, first
        )
    digits = jnp.concatenate([small_ref[atom, :, column_at:] for atom in atoms], axis=0)
    joined = join_columns(digits, unit_count)
    for atom in atoms:
        for unit in range(unit_count):
            index_ref[atom, unit] = joined[atom * block_size, unit]


def respond_kernel(unit_count, wide_ref, pair_ref, index_ref, own_ref, both_ref, near_ref, *refs):
    count = len(PAIRS)
    far_refs = refs[:count]
    keep_ref, send_ref, rows_ref = refs[count:]
    local_atoms, block_size, _ = own_ref.shape
    aux_count = rows_ref.shape[2]
    chunk_count, _, _ = small_layout(unit_count, block_size)
    side, half = wide_ref[0], pair_ref[0] % 2
    for slot, (even, odd) in enumerate(PAIRS):
        owner = side ^ jnp.where(half == 0, odd, even)
        for atom in range(local_atoms):
            rows_ref[owner * local_atoms + atom] = in_rows(far_refs[slot][atom], aux_count)
    for atom in range(local_atoms):
        rows_ref[side * local_atoms + atom] = in_rows(own_ref[atom], aux_count)
    for place in range(count):
        owner = place * 2 + (side ^ half) % 2
        for atom in range(local_atoms):
            rows_ref[owner * local_atoms + atom] = near_ref[place * local_atoms + atom]
    found = []
    for chunk in range(chunk_count):
        for atom in range(count * local_atoms):
            for unit in range(chunk * CHUNK, (chunk + 1) * CHUNK):
                if unit < unit_count:
                    found.append(rows_ref[index_ref[atom, unit]])
                else:
                    found.append(jnp.zeros(rows_ref.shape[1:], BF16))
    total = jnp.dot(both_ref[...], jnp.concatenate(found, axis=0), preferred_element_type=F32)
    write_rows(total, half, keep_ref, send_ref)


def whole_kernel(wide_count, unit_count, pair_ref, block_ref, *refs):
    keep_ref, send_ref, rows_ref, occupied_ref, both_ref = refs
    atom_total, block_size, _ = block_ref.shape
    aux_count = rows_ref.shape[2]
    row_count = both_ref.shape[0]
    local_atoms = atom_total // wide_count
    chunk_count, column_at, _ = small_layout(unit_count, block_size)
    half, outer = pair_ref[0] % 2, pair_ref[0] // 2
    group = both_ref.shape[1] // (CHUNK * block_size * block_size)

    @pl.loop(0, atom_total)
    def _(atom):
        rows_ref[atom] = in_rows(block_ref[atom], aux_count)

    def work(step, total):
        positions = [step * group + member for member in range(group)]
        atoms = [(at // local_atoms * 2 + half) * local_atoms + at % local_atoms for at in positions]
        rows = turned([own_rows(rows_ref[atom], outer, row_count) for atom in atoms])
        column_tile = block_size * aux_count + column_at
        digits = jnp.concatenate([block_ref[atom, :, column_tile:] for atom in atoms], axis=0)
        joined = join_columns(digits, unit_count)
        for chunk in range(chunk_count):
            lane_at = chunk * 2 * CHUNK * block_size
            tile = block_size * aux_count + lane_at // 128 * 128
            smalls = [block_ref[atom, :, tile : tile + 128] for atom in atoms]
            contract(rows, smalls, weight_parts(block_size, lane_at % 128), occupied_ref, both_ref, 0)
            found = []
            for member in range(group):
                for unit in range(chunk * CHUNK, (chunk + 1) * CHUNK):
                    if unit < unit_count:
                        found.append(rows_ref[joined[member * block_size, unit]])
                    else:
                        found.append(jnp.zeros(rows_ref.shape[1:], BF16))
            total += jnp.dot(
                both_ref[...], jnp.concatenate(found, axis=0), preferred_element_type=F32
            )
        return total

    total = jnp.zeros((row_count, aux_count), F32)
    total = lax.fori_loop(0, atom_total // 2 // group, work, total)
    write_rows(total, half, keep_ref, send_ref)


def respond_direct(early, full, early_small, wide_at, pair_at, unit_count, sizes):
    wide_count, pair_count, aux_count = sizes
    local_atoms, block_size, _ = full.shape
    square = block_size * block_size
    partner = [(p, p ^ 1) for p in range(pair_count)]
    across = [(p, p ^ 2) for p in range(pair_count)]
    fetched, far = [], []
    for slot, (even, odd) in enumerate(PAIRS):
        route = [
            ((w ^ d) * pair_count + p, w * pair_count + p)
            for w in range(wide_count)
            for p in range(pair_count)
            for d in (odd if p % 2 else even,)
            if d
        ]
        fetched.append(lax.ppermute(full if slot else early, ("wide", "pair"), route))
        far.append(lax.ppermute(fetched[-1], "pair", partner))
    small = fetched[0][:, :, block_size * aux_count :]
    small = small + lax.ppermute(small, "pair", across)
    chunk_count, _, lanes = small_layout(unit_count, block_size)
    near_atoms = len(PAIRS) * local_atoms
    row_count = aux_count * 2 // pair_count
    width = near_atoms * chunk_count * CHUNK * square
    both, near, index = pl.pallas_call(
        kernel_of(contract_kernel, unit_count),
        out_shape=(
            pltpu.VMEM((row_count, width), BF16),
            pltpu.VMEM((near_atoms, square, aux_count), BF16),
            pltpu.SMEM((near_atoms, unit_count), jnp.int32),
        ),
        in_specs=[SMEM, SMEM] + [VMEM] * (2 + len(PAIRS)),
        out_specs=(VMEM, VMEM, SMEM),
        scratch_shapes=[
            pltpu.VMEM((row_count, width), BF16),
            pltpu.VMEM((near_atoms, block_size, lanes), BF16),
        ],
        name="contract",
    )(wide_at, pair_at, *[in_vmem(value) for value in [full, small] + fetched])
    part = pltpu.VMEM((row_count // 2, aux_count), F32)
    return pl.pallas_call(
        kernel_of(respond_kernel, unit_count),
        out_shape=(part, part),
        in_specs=[SMEM, SMEM, SMEM] + [VMEM] * (3 + len(PAIRS)),
        out_specs=(VMEM, VMEM),
        scratch_shapes=[pltpu.VMEM((wide_count * local_atoms, square, aux_count), BF16)],
        name="respond",
    )(
        wide_at,
        pair_at,
        pltpu.with_memory_space_constraint(index, pltpu.SMEM),
        *[in_vmem(value) for value in [full, both, near] + far],
    )


def respond_whole(block, pair_at, unit_count, sizes):
    wide_count, pair_count, aux_count = sizes
    local_atoms, block_size, _ = block.shape
    square = block_size * block_size
    chunk_count, _, _ = small_layout(unit_count, block_size)
    group = max(1, min(local_atoms, 16 // chunk_count))
    row_count = aux_count * 2 // pair_count
    part = pltpu.VMEM((row_count // 2, aux_count), F32)
    return pl.pallas_call(
        kernel_of(whole_kernel, wide_count, unit_count),
        out_shape=(part, part),
        in_specs=[SMEM, VMEM],
        out_specs=(VMEM, VMEM),
        scratch_shapes=[
            pltpu.VMEM((wide_count * local_atoms, square, aux_count), BF16),
            pltpu.VMEM((row_count, group * CHUNK * square), BF16),
            pltpu.VMEM((row_count, group * CHUNK * square), BF16),
        ],
        compiler_params=pltpu.CompilerParams(vmem_limit_bytes=56 * 2**20),
        name="whole",
    )(pair_at, lax.all_gather(block, "wide", axis=0, tiled=True))


def local(three_center, occ_green, virt_green, occ_column, partner_live):
    local_atoms, block_size, wide_row = three_center.shape
    aux_count = wide_row // block_size
    wide_count, pair_count = lax.axis_size("wide"), lax.axis_size("pair")
    sizes = wide_count, pair_count, aux_count
    unit_count = pair_count * occ_green.shape[1]
    _, _, lanes = small_layout(unit_count, block_size)
    wide_at = scalar(lax.axis_index("wide"))
    pair_at = scalar(lax.axis_index("pair"))
    partner = [(p, p ^ 1) for p in range(pair_count)]
    across = [(p, p ^ 2) for p in range(pair_count)]

    block, small = pl.pallas_call(
        kernel_of(pack_kernel, unit_count),
        out_shape=(
            pltpu.VMEM((local_atoms, block_size, wide_row + lanes), BF16),
            pltpu.VMEM((local_atoms, block_size, lanes), BF16),
        ),
        in_specs=[SMEM, SMEM, SMEM, VMEM, VMEM, VMEM],
        out_specs=(VMEM, VMEM),
        name="pack",
    )(pair_at, occ_column.T, partner_live.T, three_center, occ_green, virt_green)
    two = small + lax.ppermute(small, "pair", partner)
    four = two + lax.ppermute(two, "pair", across)
    early = lax.dynamic_update_slice(block, two, (0, 0, wide_row))
    full = lax.dynamic_update_slice(block, four, (0, 0, wide_row))
    if wide_count == 8 and unit_count <= 2 * CHUNK:
        keep, send = respond_direct(early, full, two, wide_at, pair_at, unit_count, sizes)
    else:
        keep, send = respond_whole(full, pair_at, unit_count, sizes)
    return keep + lax.ppermute(send, "pair", partner)


def solution(mesh):
    placed = (
        P("wide", None, None),
        P("wide", "pair", None, None),
        P("wide", "pair", None, None),
        P("wide", "pair"),
        P("wide", "pair"),
    )
    return jax.shard_map(
        local, mesh=mesh, in_specs=placed, out_specs=P("pair", None), check_vma=False
    )
```

time: 22 us -> 21.5 us (0.977)
  waiting for transfers between devices: 6.46 us -> 3.92 us
  starting transfers between devices: 12.2 us -> 13.3 us
  Pallas kernels: 2.47 us -> 3.3 us
    ppermute x7 -> x8, waiting for transfers between devices: 6.45 us -> 3.91 us  [the longest x4 1.94 us: respond_direct(): lax.ppermute(full if slot else early, ('wide', 'pair'), route)]
    ppermute x7 -> x8, starting transfers between devices: 8.86 us -> 11.3 us  [the longest x4 7.01 us: respond_direct(): lax.ppermute(full if slot else early, ('wide', 'pair'), route)]
    ppermute x4, starting transfers between devices: 3.34 us -> 2.02 us  [respond_direct(): far.append(lax.ppermute(fetched[-1], 'pair', partner))]
    pallas_call x3, Pallas kernels: 2.47 us -> 3.3 us  [the longest x1 1.74 us: respond_direct(): pl.pallas_call(kernel_of(contract_kernel, unit_count), out_shape=(pltpu.V...]
  transfers between devices with their start and end apart: 11 -> 12, of which waited for: 6 -> 5; matrix products, arithmetic and copies ran while one was open for 0% -> 0% of each run, Pallas kernels for 4% -> 8%
where the time goes in v5:
time: 21.5 us; the launch traced here: 21.3 us
  starting transfers between devices  13.3 us (62%)
  waiting for transfers between devices  3.92 us (18%)
  Pallas kernels  3.3 us (15%)
  other arithmetic  0.63 us (3%)
    ppermute x4, starting transfers between devices, respond_direct(): lax.ppermute(full if slot else early, ('wide', 'pair'), route)  7.01 us
    ppermute x1, starting transfers between devices, local(): four = two + lax.ppermute(two, 'pair', across)  2.9 us
    ppermute x4, starting transfers between devices, respond_direct(): far.append(lax.ppermute(fetched[-1], 'pair', partner))  2.02 us
    ppermute x4, waiting for transfers between devices, respond_direct(): lax.ppermute(full if slot else early, ('wide', 'pair'), route)  1.94 us
    pallas_call x1, Pallas kernels, respond_direct(): pl.pallas_call(kernel_of(contract_kernel, unit_count), out_shape=(pltpu.V...  1.74 us
    ppermute x1, waiting for transfers between devices, local(): return keep + lax.ppermute(send, 'pair', partner)  1.07 us
    pallas_call x1, Pallas kernels, local(): pl.pallas_call(kernel_of(pack_kernel, unit_count), out_shape=(pltpu.VMEM(...  1.02 us
    ppermute x1, waiting for transfers between devices, local(): two = small + lax.ppermute(small, 'pair', partner)  0.83 us
  transfers between devices with their start and end apart: 12, of which 5 were waited for; matrix products, arithmetic and copies ran while one was open for 0% of the time, Pallas kernels for 8%

profile of v5, /device:TPU:0, one launch (start us, length us, event | category | flops | bytes accessed | tf_op | source)
XLA Modules:
  0.0 21.3 jit_solution(13395716921259752325)
XLA Ops:
  0.0 1.0 %pack.1 = (bf16[4,8,1280]{2,1,0:T(8,128)(2,1)S(1)}, bf16[4,8,256]{2,1,0:T(8,128)(2,1)S(1)}) custom-call(s32[1]{0:T(128)} %bitcast.1.refs_0_.refs_1_, s32[2,4]{1,0:T(2,128)} %bitcast.4, s32[2,4]{1,0:T(2,128)} %bitcast.5, bf16[4,8,1024]{2,1,0:T(8,128)(2,1)} %refs_3_.1, bf16[4,2,8,8]{3,2,1,0:T(8,128)(2,1)} %refs_4_.1, bf16[4,2,8,8]{3,2,1,0:T(8,128)(2,1)} %refs_5_.1), custom_call_target="tpu_custom_call" | custom-call | tf_op jit(solution)/shard_map/pack/pallas_call | solution.py:358
  1.0 0.5 %collective-permute-start = (bf16[4,8,256]{2,1,0:T(8,128)(2,1)S(1)}, bf16[4,8,256]{2,1,0:T(8,128)(2,1)S(1)}, u32[]{:S(2)}, u32[]{:S(2)}) collective-permute-start(bf16[4,8,256]{2,1,0:T(8,128)(2,1)S(1)} %get-tuple-element.13), channel_id=1, source_target_pairs={{0,1},{1,0},{2,3},{3,2},{4,5},{5,4},{6,7},{7,6},{8,9},{9,8},{10,11... | collective-permute-start | bytes 49160 | tf_op jit(solution)/shard_map/ppermute | solution.py:368
  1.5 0.8 %collective-permute-done = bf16[4,8,256]{2,1,0:T(8,128)(2,1)S(1)} collective-permute-done((bf16[4,8,256]{2,1,0:T(8,128)(2,1)S(1)}, bf16[4,8,256]{2,1,0:T(8,128)(2,1)S(1)}, u32[]{:S(2)}, u32[]{:S(2)}) %collective-permute-start) | collective-permute-done | bytes 16416 | tf_op jit(solution)/shard_map/ppermute | solution.py:368
  2.4 2.9 %collective-permute-start.1 = (bf16[4,8,256]{2,1,0:T(8,128)(2,1)S(1)}, bf16[4,8,256]{2,1,0:T(8,128)(2,1)S(1)}, u32[]{:S(2)}, u32[]{:S(2)}) collective-permute-start(bf16[4,8,256]{2,1,0:T(8,128)(2,1)S(1)} %get-tuple-element.20), channel_id=1, source_target_pairs={{0,2},{1,3},{2,0},{3,1},{4,6},{5,7},{6,4},{7,5},{8,10},{9,11},{10,... | collective-permute-start | bytes 49160 | tf_op jit(solution)/shard_map/ppermute | solution.py:369
  5.3 2.6 %collective-permute-start.2 = (bf16[4,8,1280]{2,1,0:T(8,128)(2,1)S(1)}, bf16[4,8,1280]{2,1,0:T(8,128)(2,1)S(1)}, u32[]{:S(2)}, u32[]{:S(2)}) collective-permute-start(bf16[4,8,1280]{2,1,0:T(8,128)(2,1)S(1)} %get-tuple-element.19), channel_id=1, source_target_pairs={{16,0},{21,1},{18,2},{23,3},{20,4},{17,5},{22,6},{19,7},{24,8},{29... | collective-permute-start | bytes 245768 | tf_op jit(solution)/shard_map/ppermute | solution.py:284
  7.9 1.6 %collective-permute-start.6 = (bf16[4,8,1280]{2,1,0:T(8,128)(2,1)S(1)}, bf16[4,8,1280]{2,1,0:T(8,128)(2,1)S(1)}, u32[]{:S(2)}, u32[]{:S(2)}) collective-permute-start(bf16[4,8,1280]{2,1,0:T(8,128)(2,1)S(1)} %add_dynamic-update-slice_fusion.refs_2_.refs_3_), channel_id=1, source_target_pairs={{8,0},{13,1},{10,2},{15,3},{12,4},{9,5},{14,6},{11,7},{0,8},{5,9},... | collective-permute-start | bytes 245768 | tf_op jit(solution)/shard_map/ppermute | solution.py:284
  9.5 2.1 %collective-permute-start.4 = (bf16[4,8,1280]{2,1,0:T(8,128)(2,1)S(1)}, bf16[4,8,1280]{2,1,0:T(8,128)(2,1)S(1)}, u32[]{:S(2)}, u32[]{:S(2)}) collective-permute-start(bf16[4,8,1280]{2,1,0:T(8,128)(2,1)S(1)} %add_dynamic-update-slice_fusion.refs_2_.refs_3_), channel_id=1, source_target_pairs={{24,0},{29,1},{26,2},{31,3},{28,4},{25,5},{30,6},{27,7},{16,8},{21... | collective-permute-start | bytes 245768 | tf_op jit(solution)/shard_map/ppermute | solution.py:284
  11.7 0.7 %collective-permute-start.5 = (bf16[4,8,1280]{2,1,0:T(8,128)(2,1)S(1)}, bf16[4,8,1280]{2,1,0:T(8,128)(2,1)S(1)}, u32[]{:S(2)}, u32[]{:S(2)}) collective-permute-start(bf16[4,8,1280]{2,1,0:T(8,128)(2,1)S(1)} %add_dynamic-update-slice_fusion.refs_2_.refs_3_), channel_id=1, source_target_pairs={{5,1},{7,3},{1,5},{3,7},{13,9},{15,11},{9,13},{11,15},{21,17},{23,... | collective-permute-start | bytes 245768 | tf_op jit(solution)/shard_map/ppermute | solution.py:284
  12.3 0.9 %collective-permute-done.2.refs_4_ = bf16[4,8,1280]{2,1,0:T(8,128)(2,1)S(1)} collective-permute-done((bf16[4,8,1280]{2,1,0:T(8,128)(2,1)S(1)}, bf16[4,8,1280]{2,1,0:T(8,128)(2,1)S(1)}, u32[]{:S(2)}, u32[]{:S(2)}) %collective-permute-start.2) | collective-permute-done | bytes 81952 | tf_op jit(solution)/shard_map/ppermute | solution.py:284
  13.2 0.7 %collective-permute-start.3 = (bf16[4,8,256]{2,1,0:T(8,128)(2,1)S(1)}, bf16[4,8,256]{2,1,0:T(8,128)(2,1)S(1)}, u32[]{:S(2)}, u32[]{:S(2)}) collective-permute-start(bf16[4,8,256]{2,1,0:T(8,128)(2,1)S(1)} %slice.4), channel_id=1, source_target_pairs={{0,2},{1,3},{2,0},{3,1},{4,6},{5,7},{6,4},{7,5},{8,10},{9,11},{10,... | collective-permute-start | bytes 49160 | tf_op jit(solution)/shard_map/ppermute | solution.py:287
  13.9 1.5 %collective-permute-start.7 = (bf16[4,8,1280]{2,1,0:T(8,128)(2,1)S(1)}, bf16[4,8,1280]{2,1,0:T(8,128)(2,1)S(1)}, u32[]{:S(2)}, u32[]{:S(2)}) collective-permute-start(bf16[4,8,1280]{2,1,0:T(8,128)(2,1)S(1)} %collective-permute-done.2.refs_4_), channel_id=1, source_target_pairs={{0,1},{1,0},{2,3},{3,2},{4,5},{5,4},{6,7},{7,6},{8,9},{9,8},{10,11... | collective-permute-start | bytes 245768 | tf_op jit(solution)/shard_map/ppermute | solution.py:285
  15.4 0.0 collective-permute-done.6.refs_7_
  15.4 0.0 collective-permute-start.10
  15.4 1.1 %collective-permute-done.4.refs_5_ = bf16[4,8,1280]{2,1,0:T(8,128)(2,1)S(1)} collective-permute-done((bf16[4,8,1280]{2,1,0:T(8,128)(2,1)S(1)}, bf16[4,8,1280]{2,1,0:T(8,128)(2,1)S(1)}, u32[]{:S(2)}, u32[]{:S(2)}) %collective-permute-start.4) | collective-permute-done | bytes 81952 | tf_op jit(solution)/shard_map/ppermute | solution.py:284
  16.5 0.5 %collective-permute-start.9 = (bf16[4,8,1280]{2,1,0:T(8,128)(2,1)S(1)}, bf16[4,8,1280]{2,1,0:T(8,128)(2,1)S(1)}, u32[]{:S(2)}, u32[]{:S(2)}) collective-permute-start(bf16[4,8,1280]{2,1,0:T(8,128)(2,1)S(1)} %collective-permute-done.5.refs_6_), channel_id=1, source_target_pairs={{0,1},{1,0},{2,3},{3,2},{4,5},{5,4},{6,7},{7,6},{8,9},{9,8},{10,11... | collective-permute-start | bytes 245768 | tf_op jit(solution)/shard_map/ppermute | solution.py:285
  17.0 0.1 collective-permute-done.3
  17.1 1.7 %contract.1 = (bf16[64,8192]{1,0:T(8,128)(2,1)S(1)}, bf16[16,64,128]{2,1,0:T(8,128)(2,1)S(1)}, s32[16,8]{1,0:T(8,128)S(4)}) custom-call(s32[1]{0:T(128)} %bitcast.refs_0_, s32[1]{0:T(128)} %bitcast.1.refs_0_.refs_1_, bf16[4,8,1280]{2,1,0:T(8,128)(2,1)S(1)} %add_dynamic-update-slice_fusion.refs_2_.refs_3_, bf16[4,8,256]{2,1,0:T(8,128)(2,1)S(1)} %slice_add_fusion.refs_3_, ...), custom_call_target="tpu_custom_call" | custom-call | tf_op jit(solution)/shard_map/contract/pallas_call | solution.py:292
  18.8 0.0 collective-permute-done.7.refs_6_
  18.8 0.0 collective-permute-done.8.refs_7_
  18.8 0.0 collective-permute-done.9.refs_8_
  18.9 0.5 %respond.1 = (f32[32,128]{1,0:T(8,128)S(1)}, f32[32,128]{1,0:T(8,128)S(1)}) custom-call(s32[1]{0:T(128)} %bitcast.refs_0_, s32[1]{0:T(128)} %bitcast.1.refs_0_.refs_1_, s32[16,8]{1,0:T(8,128)S(4)} %get-tuple-element.14.refs_2_, bf16[4,8,1280]{2,1,0:T(8,128)(2,1)S(1)} %add_dynamic-update-slice_fusion.refs_2_.refs_3_, ...), custom_call_target="tpu_custom_call" | custom-call | tf_op jit(solution)/shard_map/respond/pallas_call | solution.py:308
  19.4 0.2 collective-permute-start.11
  19.6 1.1 %collective-permute-done.11 = f32[32,128]{1,0:T(8,128)S(1)} collective-permute-done((f32[32,128]{1,0:T(8,128)S(1)}, f32[32,128]{1,0:T(8,128)S(1)}, u32[]{:S(2)}, u32[]{:S(2)}) %collective-permute-start.11) | collective-permute-done | bytes 16416 | tf_op jit(solution)/shard_map/ppermute | solution.py:376
  20.7 0.6 %add.15 = f32[32,128]{1,0:T(8,128)} add(f32[32,128]{1,0:T(8,128)S(1)} %get-tuple-element.17, f32[32,128]{1,0:T(8,128)S(1)} %collective-permute-done.11) | non-fusion elementwise | flops 4096 | bytes 49152 | tf_op jit(solution)/shard_map/add | solution.py:376
  (9 shorter events, 0.0 us)
Async XLA Ops:
  1.0 1.4 %collective-permute-start = (bf16[4,8,256]{2,1,0:T(8,128)(2,1)S(1)}, bf16[4,8,256]{2,1,0:T(8,128)(2,1)S(1)}, u32[]{:S(2)}, u32[]{:S(2)}) collective-permute-start(bf16[4,8,256]{2,1,0:T(8,128)(2,1)S(1)} %get-tuple-element.13), channel_id=1, source_target_pairs={{0,1},{1,0},{2,3},{3,2},{4,5},{5,4},{6,7},{7,6},{8,9},{9,8},{10,11... | collective-permute-start | bytes 49160 | tf_op jit(solution)/shard_map/ppermute | solution.py:368
  2.4 5.5 %collective-permute-start.1 = (bf16[4,8,256]{2,1,0:T(8,128)(2,1)S(1)}, bf16[4,8,256]{2,1,0:T(8,128)(2,1)S(1)}, u32[]{:S(2)}, u32[]{:S(2)}) collective-permute-start(bf16[4,8,256]{2,1,0:T(8,128)(2,1)S(1)} %get-tuple-element.20), channel_id=1, source_target_pairs={{0,2},{1,3},{2,0},{3,1},{4,6},{5,7},{6,4},{7,5},{8,10},{9,11},{10,... | collective-permute-start | bytes 49160 | tf_op jit(solution)/shard_map/ppermute | solution.py:369
  5.3 7.9 %collective-permute-start.2 = (bf16[4,8,1280]{2,1,0:T(8,128)(2,1)S(1)}, bf16[4,8,1280]{2,1,0:T(8,128)(2,1)S(1)}, u32[]{:S(2)}, u32[]{:S(2)}) collective-permute-start(bf16[4,8,1280]{2,1,0:T(8,128)(2,1)S(1)} %get-tuple-element.19), channel_id=1, source_target_pairs={{16,0},{21,1},{18,2},{23,3},{20,4},{17,5},{22,6},{19,7},{24,8},{29... | collective-permute-start | bytes 245768 | tf_op jit(solution)/shard_map/ppermute | solution.py:284
  7.9 7.5 %collective-permute-start.6 = (bf16[4,8,1280]{2,1,0:T(8,128)(2,1)S(1)}, bf16[4,8,1280]{2,1,0:T(8,128)(2,1)S(1)}, u32[]{:S(2)}, u32[]{:S(2)}) collective-permute-start(bf16[4,8,1280]{2,1,0:T(8,128)(2,1)S(1)} %add_dynamic-update-slice_fusion.refs_2_.refs_3_), channel_id=1, source_target_pairs={{8,0},{13,1},{10,2},{15,3},{12,4},{9,5},{14,6},{11,7},{0,8},{5,9},... | collective-permute-start | bytes 245768 | tf_op jit(solution)/shard_map/ppermute | solution.py:284
  9.5 7.0 %collective-permute-start.4 = (bf16[4,8,1280]{2,1,0:T(8,128)(2,1)S(1)}, bf16[4,8,1280]{2,1,0:T(8,128)(2,1)S(1)}, u32[]{:S(2)}, u32[]{:S(2)}) collective-permute-start(bf16[4,8,1280]{2,1,0:T(8,128)(2,1)S(1)} %add_dynamic-update-slice_fusion.refs_2_.refs_3_), channel_id=1, source_target_pairs={{24,0},{29,1},{26,2},{31,3},{28,4},{25,5},{30,6},{27,7},{16,8},{21... | collective-permute-start | bytes 245768 | tf_op jit(solution)/shard_map/ppermute | solution.py:284
  11.7 4.8 %collective-permute-start.5 = (bf16[4,8,1280]{2,1,0:T(8,128)(2,1)S(1)}, bf16[4,8,1280]{2,1,0:T(8,128)(2,1)S(1)}, u32[]{:S(2)}, u32[]{:S(2)}) collective-permute-start(bf16[4,8,1280]{2,1,0:T(8,128)(2,1)S(1)} %add_dynamic-update-slice_fusion.refs_2_.refs_3_), channel_id=1, source_target_pairs={{5,1},{7,3},{1,5},{3,7},{13,9},{15,11},{9,13},{11,15},{21,17},{23,... | collective-permute-start | bytes 245768 | tf_op jit(solution)/shard_map/ppermute | solution.py:284
  13.2 3.9 %collective-permute-start.3 = (bf16[4,8,256]{2,1,0:T(8,128)(2,1)S(1)}, bf16[4,8,256]{2,1,0:T(8,128)(2,1)S(1)}, u32[]{:S(2)}, u32[]{:S(2)}) collective-permute-start(bf16[4,8,256]{2,1,0:T(8,128)(2,1)S(1)} %slice.4), channel_id=1, source_target_pairs={{0,2},{1,3},{2,0},{3,1},{4,6},{5,7},{6,4},{7,5},{8,10},{9,11},{10,... | collective-permute-start | bytes 49160 | tf_op jit(solution)/shard_map/ppermute | solution.py:287
  13.9 4.9 %collective-permute-start.7 = (bf16[4,8,1280]{2,1,0:T(8,128)(2,1)S(1)}, bf16[4,8,1280]{2,1,0:T(8,128)(2,1)S(1)}, u32[]{:S(2)}, u32[]{:S(2)}) collective-permute-start(bf16[4,8,1280]{2,1,0:T(8,128)(2,1)S(1)} %collective-permute-done.2.refs_4_), channel_id=1, source_target_pairs={{0,1},{1,0},{2,3},{3,2},{4,5},{5,4},{6,7},{7,6},{8,9},{9,8},{10,11... | collective-permute-start | bytes 245768 | tf_op jit(solution)/shard_map/ppermute | solution.py:285
  15.4 3.4 %collective-permute-start.10 = (bf16[4,8,1280]{2,1,0:T(8,128)(2,1)S(1)}, bf16[4,8,1280]{2,1,0:T(8,128)(2,1)S(1)}, u32[]{:S(2)}, u32[]{:S(2)}) collective-permute-start(bf16[4,8,1280]{2,1,0:T(8,128)(2,1)S(1)} %collective-permute-done.6.refs_7_), channel_id=1, source_target_pairs={{0,1},{1,0},{2,3},{3,2},{4,5},{5,4},{6,7},{7,6},{8,9},{9,8},{10,11... | collective-permute-start | bytes 245768 | tf_op jit(solution)/shard_map/ppermute | solution.py:285
  16.5 2.4 %collective-permute-start.8 = (bf16[4,8,1280]{2,1,0:T(8,128)(2,1)S(1)}, bf16[4,8,1280]{2,1,0:T(8,128)(2,1)S(1)}, u32[]{:S(2)}, u32[]{:S(2)}) collective-permute-start(bf16[4,8,1280]{2,1,0:T(8,128)(2,1)S(1)} %collective-permute-done.4.refs_5_), channel_id=1, source_target_pairs={{0,1},{1,0},{2,3},{3,2},{4,5},{5,4},{6,7},{7,6},{8,9},{9,8},{10,11... | collective-permute-start | bytes 245768 | tf_op jit(solution)/shard_map/ppermute | solution.py:285
  16.5 2.4 %collective-permute-start.9 = (bf16[4,8,1280]{2,1,0:T(8,128)(2,1)S(1)}, bf16[4,8,1280]{2,1,0:T(8,128)(2,1)S(1)}, u32[]{:S(2)}, u32[]{:S(2)}) collective-permute-start(bf16[4,8,1280]{2,1,0:T(8,128)(2,1)S(1)} %collective-permute-done.5.refs_6_), channel_id=1, source_target_pairs={{0,1},{1,0},{2,3},{3,2},{4,5},{5,4},{6,7},{7,6},{8,9},{9,8},{10,11... | collective-permute-start | bytes 245768 | tf_op jit(solution)/shard_map/ppermute | solution.py:285
  19.4 1.2 %collective-permute-start.11 = (f32[32,128]{1,0:T(8,128)S(1)}, f32[32,128]{1,0:T(8,128)S(1)}, u32[]{:S(2)}, u32[]{:S(2)}) collective-permute-start(f32[32,128]{1,0:T(8,128)S(1)} %get-tuple-element.18), channel_id=1, source_target_pairs={{0,1},{1,0},{2,3},{3,2},{4,5},{5,4},{6,7},{7,6},{8,9},{9,8},{10,11... | collective-permute-start | bytes 49160 | tf_op jit(solution)/shard_map/ppermute | solution.py:376

commit v6 on v5

--- a/solution.py
+++ b/solution.py
@@ -89,54 +89,37 @@
 def turned(rows):
     found = []
     for at in range(0, len(rows), 2):
-        both = jnp.concatenate(rows[at : at + 2], axis=1).T
+        both = jnp.concatenate(rows[at : at + 2], axis=1)
+        both = jnp.concatenate([both, both], axis=0).T
         found += jnp.split(both, len(rows[at : at + 2]), axis=0)
     return found
 
 
-def weight_parts(block_size, lane_at):
+def spread_small(block_size, lane_at):
     square = block_size * block_size
     wide_unit = CHUNK * square
     row, lane = iota((128, 2 * wide_unit), 0), iota((128, 2 * wide_unit), 1)
     inner = lane % wide_unit
-    unit, upper, lower = inner // square, (inner // block_size) % block_size, inner % block_size
-    within = jnp.where(lane >= wide_unit, upper + CHUNK * block_size, lower)
-    spread = (row == unit * block_size + within + lane_at).astype(BF16)
-    row, lane = iota((block_size, wide_unit), 0), iota((block_size, wide_unit), 1)
-    unit, upper, lower = lane // square, (lane // block_size) % block_size, lane % block_size
-    occ_mask = [(upper == at).astype(F32) for at in range(block_size)]
-    virt_mask = [((unit == at) & (lower == row)).astype(F32) for at in range(CHUNK)]
-    return spread, occ_mask, virt_mask
-
-
-def contract(rows, smalls, parts, occupied_ref, both_ref, first):
-    spread, occ_mask, virt_mask = parts
-    block_size, wide_unit = occ_mask[0].shape
+    unit, sigma, lam = inner // square, (inner // block_size) % block_size, inner % block_size
+    within = jnp.where(lane >= wide_unit, sigma + CHUNK * block_size, lam)
+    return (row == unit * block_size + within + lane_at).astype(BF16)
+
+
+def contract(rows, smalls, spread, both_ref, first):
+    block_size, wide_unit = smalls[0].shape[0], spread.shape[1] // 2
     wide = jnp.dot(jnp.concatenate(smalls, axis=0), spread, preferred_element_type=F32)
     for member in range(len(rows)):
-        occ = wide[member * block_size : (member + 1) * block_size, :wide_unit]
-        weights = jnp.concatenate([occ * mask for mask in occ_mask], axis=0)
+        values = wide[member * block_size : (member + 1) * block_size]
+        occ, virt = values[:, :wide_unit], values[:, wide_unit:]
+        weights = jnp.concatenate(
+            [jnp.broadcast_to(virt[nu : nu + 1], occ.shape) * occ for nu in range(block_size)], axis=0
+        )
+        high = weights.astype(BF16)
+        low = (weights - high.astype(F32)).astype(BF16)
         at = slice(first + member * wide_unit, first + (member + 1) * wide_unit)
-        occupied_ref[:, at] = jnp.dot(
-            rows[member], weights.astype(BF16), preferred_element_type=F32
+        both_ref[:, at] = jnp.dot(
+            rows[member], jnp.concatenate([high, low], axis=0), preferred_element_type=F32
         ).astype(BF16)
-    for member in range(len(rows)):
-        virt = wide[member * block_size : (member + 1) * block_size, wide_unit:]
-        half = wide_unit // 2
-        for part in range(2):
-            some = virt[:, part * half : (part + 1) * half]
-            weights = jnp.concatenate(
-                [
-                    jnp.broadcast_to(some[nu : nu + 1], some.shape) * mask[:, :half]
-                    for mask in virt_mask[: CHUNK // 2]
-                    for nu in range(block_size)
-                ],
-                axis=0,
-            )
-            at = first + member * wide_unit + part * half
-            both_ref[:, at : at + half] = jnp.dot(
-                occupied_ref[:, at : at + half], weights.astype(BF16), preferred_element_type=F32
-            ).astype(BF16)
 
 
 def join_columns(digits, unit_count):
@@ -162,7 +145,7 @@
 def contract_kernel(unit_count, wide_ref, pair_ref, own_ref, early_ref, *refs):
     count = len(PAIRS)
     block_refs = refs[:count]
-    both_ref, rows_ref, index_ref, occupied_ref, small_ref = refs[count:]
+    both_ref, rows_ref, index_ref, small_ref = refs[count:]
     local_atoms, block_size, _ = own_ref.shape
     aux_count, row_count = rows_ref.shape[2], both_ref.shape[0]
     chunk_count, column_at, lanes = small_layout(unit_count, block_size)
@@ -183,9 +166,7 @@
         tile = lane_at // 128 * 128
         smalls = [small_ref[atom, :, tile : tile + 128] for atom in atoms]
         first = chunk * len(atoms) * CHUNK * block_size * block_size
-        contract(
-            rows, smalls, weight_parts(block_size, lane_at - tile), occupied_ref, both_ref, first
-        )
+        contract(rows, smalls, spread_small(block_size, lane_at - tile), both_ref, first)
     digits = jnp.concatenate([small_ref[atom, :, column_at:] for atom in atoms], axis=0)
     joined = join_columns(digits, unit_count)
     for atom in atoms:
@@ -224,7 +205,7 @@
 
 
 def whole_kernel(wide_count, unit_count, pair_ref, block_ref, *refs):
-    keep_ref, send_ref, rows_ref, occupied_ref, both_ref = refs
+    keep_ref, send_ref, rows_ref, both_ref = refs
     atom_total, block_size, _ = block_ref.shape
     aux_count = rows_ref.shape[2]
     row_count = both_ref.shape[0]
@@ -248,7 +229,7 @@
             lane_at = chunk * 2 * CHUNK * block_size
             tile = block_size * aux_count + lane_at // 128 * 128
             smalls = [block_ref[atom, :, tile : tile + 128] for atom in atoms]
-            contract(rows, smalls, weight_parts(block_size, lane_at % 128), occupied_ref, both_ref, 0)
+            contract(rows, smalls, spread_small(block_size, lane_at % 128), both_ref, 0)
             found = []
             for member in range(group):
                 for unit in range(chunk * CHUNK, (chunk + 1) * CHUNK):
@@ -298,10 +279,7 @@
         ),
         in_specs=[SMEM, SMEM] + [VMEM] * (2 + len(PAIRS)),
         out_specs=(VMEM, VMEM, SMEM),
-        scratch_shapes=[
-            pltpu.VMEM((row_count, width), BF16),
-            pltpu.VMEM((near_atoms, block_size, lanes), BF16),
-        ],
+        scratch_shapes=[pltpu.VMEM((near_atoms, block_size, lanes), BF16)],
         name="contract",
     )(wide_at, pair_at, *[in_vmem(value) for value in [full, small] + fetched])
     part = pltpu.VMEM((row_count // 2, aux_count), F32)
@@ -335,7 +313,6 @@
         out_specs=(VMEM, VMEM),
         scratch_shapes=[
             pltpu.VMEM((wide_count * local_atoms, square, aux_count), BF16),
-            pltpu.VMEM((row_count, group * CHUNK * square), BF16),
             pltpu.VMEM((row_count, group * CHUNK * square), BF16),
         ],
         compiler_params=pltpu.CompilerParams(vmem_limit_bytes=56 * 2**20),

time: 21.5 us -> 21 us (0.977)
  Pallas kernels: 3.3 us -> 2.87 us
    pallas_call x1, Pallas kernels: 1.74 us -> 1.3 us  [respond_direct(): pl.pallas_call(kernel_of(contract_kernel, unit_count), out_shape=(pltpu.V...]
  transfers between devices with their start and end apart: 12 -> 12, of which waited for: 5 -> 5; matrix products, arithmetic and copies ran while one was open for 0% -> 0% of each run, Pallas kernels for 8% -> 6%
where the time goes in v6:
time: 21 us; the launch traced here: 20.8 us
  starting transfers between devices  13.3 us (63%)
  waiting for transfers between devices  3.92 us (19%)
  Pallas kernels  2.87 us (14%)
  other arithmetic  0.63 us (3%)
    ppermute x4, starting transfers between devices, respond_direct(): lax.ppermute(full if slot else early, ('wide', 'pair'), route)  7.01 us
    ppermute x1, starting transfers between devices, local(): four = two + lax.ppermute(two, 'pair', across)  2.9 us
    ppermute x4, starting transfers between devices, respond_direct(): far.append(lax.ppermute(fetched[-1], 'pair', partner))  2.02 us
    ppermute x4, waiting for transfers between devices, respond_direct(): lax.ppermute(full if slot else early, ('wide', 'pair'), route)  1.94 us
    pallas_call x1, Pallas kernels, respond_direct(): pl.pallas_call(kernel_of(contract_kernel, unit_count), out_shape=(pltpu.V...  1.3 us
    ppermute x1, waiting for transfers between devices, local(): return keep + lax.ppermute(send, 'pair', partner)  1.07 us
    pallas_call x1, Pallas kernels, local(): pl.pallas_call(kernel_of(pack_kernel, unit_count), out_shape=(pltpu.VMEM(...  1.02 us
    ppermute x1, waiting for transfers between devices, local(): two = small + lax.ppermute(small, 'pair', partner)  0.83 us
  transfers between devices with their start and end apart: 12, of which 5 were waited for; matrix products, arithmetic and copies ran while one was open for 0% of the time, Pallas kernels for 6%

profile of v6, /device:TPU:0, one launch (start us, length us, event | category | flops | bytes accessed | tf_op | source)
XLA Modules:
  0.0 20.8 jit_solution(16247978296495495176)
XLA Ops:
  0.0 1.0 %pack.1 = (bf16[4,8,1280]{2,1,0:T(8,128)(2,1)S(1)}, bf16[4,8,256]{2,1,0:T(8,128)(2,1)S(1)}) custom-call(s32[1]{0:T(128)} %bitcast.1.refs_0_.refs_1_, s32[2,4]{1,0:T(2,128)} %bitcast.4, s32[2,4]{1,0:T(2,128)} %bitcast.5, bf16[4,8,1024]{2,1,0:T(8,128)(2,1)} %refs_3_.1, bf16[4,2,8,8]{3,2,1,0:T(8,128)(2,1)} %refs_4_.1, bf16[4,2,8,8]{3,2,1,0:T(8,128)(2,1)} %refs_5_.1), custom_call_target="tpu_custom_call" | custom-call | tf_op jit(solution)/shard_map/pack/pallas_call | solution.py:335
  1.0 0.5 %collective-permute-start = (bf16[4,8,256]{2,1,0:T(8,128)(2,1)S(1)}, bf16[4,8,256]{2,1,0:T(8,128)(2,1)S(1)}, u32[]{:S(2)}, u32[]{:S(2)}) collective-permute-start(bf16[4,8,256]{2,1,0:T(8,128)(2,1)S(1)} %get-tuple-element.13), channel_id=1, source_target_pairs={{0,1},{1,0},{2,3},{3,2},{4,5},{5,4},{6,7},{7,6},{8,9},{9,8},{10,11... | collective-permute-start | bytes 49160 | tf_op jit(solution)/shard_map/ppermute | solution.py:345
  1.5 0.8 %collective-permute-done = bf16[4,8,256]{2,1,0:T(8,128)(2,1)S(1)} collective-permute-done((bf16[4,8,256]{2,1,0:T(8,128)(2,1)S(1)}, bf16[4,8,256]{2,1,0:T(8,128)(2,1)S(1)}, u32[]{:S(2)}, u32[]{:S(2)}) %collective-permute-start) | collective-permute-done | bytes 16416 | tf_op jit(solution)/shard_map/ppermute | solution.py:345
  2.4 2.9 %collective-permute-start.1 = (bf16[4,8,256]{2,1,0:T(8,128)(2,1)S(1)}, bf16[4,8,256]{2,1,0:T(8,128)(2,1)S(1)}, u32[]{:S(2)}, u32[]{:S(2)}) collective-permute-start(bf16[4,8,256]{2,1,0:T(8,128)(2,1)S(1)} %get-tuple-element.20), channel_id=1, source_target_pairs={{0,2},{1,3},{2,0},{3,1},{4,6},{5,7},{6,4},{7,5},{8,10},{9,11},{10,... | collective-permute-start | bytes 49160 | tf_op jit(solution)/shard_map/ppermute | solution.py:346
  5.3 2.6 %collective-permute-start.2 = (bf16[4,8,1280]{2,1,0:T(8,128)(2,1)S(1)}, bf16[4,8,1280]{2,1,0:T(8,128)(2,1)S(1)}, u32[]{:S(2)}, u32[]{:S(2)}) collective-permute-start(bf16[4,8,1280]{2,1,0:T(8,128)(2,1)S(1)} %get-tuple-element.19), channel_id=1, source_target_pairs={{16,0},{21,1},{18,2},{23,3},{20,4},{17,5},{22,6},{19,7},{24,8},{29... | collective-permute-start | bytes 245768 | tf_op jit(solution)/shard_map/ppermute | solution.py:265
  7.9 0.0 collective-permute-done.1
  7.9 1.6 %collective-permute-start.6 = (bf16[4,8,1280]{2,1,0:T(8,128)(2,1)S(1)}, bf16[4,8,1280]{2,1,0:T(8,128)(2,1)S(1)}, u32[]{:S(2)}, u32[]{:S(2)}) collective-permute-start(bf16[4,8,1280]{2,1,0:T(8,128)(2,1)S(1)} %add_dynamic-update-slice_fusion.refs_2_.refs_3_), channel_id=1, source_target_pairs={{8,0},{13,1},{10,2},{15,3},{12,4},{9,5},{14,6},{11,7},{0,8},{5,9},... | collective-permute-start | bytes 245768 | tf_op jit(solution)/shard_map/ppermute | solution.py:265
  9.5 2.1 %collective-permute-start.4 = (bf16[4,8,1280]{2,1,0:T(8,128)(2,1)S(1)}, bf16[4,8,1280]{2,1,0:T(8,128)(2,1)S(1)}, u32[]{:S(2)}, u32[]{:S(2)}) collective-permute-start(bf16[4,8,1280]{2,1,0:T(8,128)(2,1)S(1)} %add_dynamic-update-slice_fusion.refs_2_.refs_3_), channel_id=1, source_target_pairs={{24,0},{29,1},{26,2},{31,3},{28,4},{25,5},{30,6},{27,7},{16,8},{21... | collective-permute-start | bytes 245768 | tf_op jit(solution)/shard_map/ppermute | solution.py:265
  11.7 0.7 %collective-permute-start.5 = (bf16[4,8,1280]{2,1,0:T(8,128)(2,1)S(1)}, bf16[4,8,1280]{2,1,0:T(8,128)(2,1)S(1)}, u32[]{:S(2)}, u32[]{:S(2)}) collective-permute-start(bf16[4,8,1280]{2,1,0:T(8,128)(2,1)S(1)} %add_dynamic-update-slice_fusion.refs_2_.refs_3_), channel_id=1, source_target_pairs={{5,1},{7,3},{1,5},{3,7},{13,9},{15,11},{9,13},{11,15},{21,17},{23,... | collective-permute-start | bytes 245768 | tf_op jit(solution)/shard_map/ppermute | solution.py:265
  12.3 0.9 %collective-permute-done.2.refs_4_ = bf16[4,8,1280]{2,1,0:T(8,128)(2,1)S(1)} collective-permute-done((bf16[4,8,1280]{2,1,0:T(8,128)(2,1)S(1)}, bf16[4,8,1280]{2,1,0:T(8,128)(2,1)S(1)}, u32[]{:S(2)}, u32[]{:S(2)}) %collective-permute-start.2) | collective-permute-done | bytes 81952 | tf_op jit(solution)/shard_map/ppermute | solution.py:265
  13.2 0.7 %collective-permute-start.3 = (bf16[4,8,256]{2,1,0:T(8,128)(2,1)S(1)}, bf16[4,8,256]{2,1,0:T(8,128)(2,1)S(1)}, u32[]{:S(2)}, u32[]{:S(2)}) collective-permute-start(bf16[4,8,256]{2,1,0:T(8,128)(2,1)S(1)} %slice.4), channel_id=1, source_target_pairs={{0,2},{1,3},{2,0},{3,1},{4,6},{5,7},{6,4},{7,5},{8,10},{9,11},{10,... | collective-permute-start | bytes 49160 | tf_op jit(solution)/shard_map/ppermute | solution.py:268
  13.9 1.5 %collective-permute-start.7 = (bf16[4,8,1280]{2,1,0:T(8,128)(2,1)S(1)}, bf16[4,8,1280]{2,1,0:T(8,128)(2,1)S(1)}, u32[]{:S(2)}, u32[]{:S(2)}) collective-permute-start(bf16[4,8,1280]{2,1,0:T(8,128)(2,1)S(1)} %collective-permute-done.2.refs_4_), channel_id=1, source_target_pairs={{0,1},{1,0},{2,3},{3,2},{4,5},{5,4},{6,7},{7,6},{8,9},{9,8},{10,11... | collective-permute-start | bytes 245768 | tf_op jit(solution)/shard_map/ppermute | solution.py:266
  15.4 0.0 collective-permute-done.6.refs_7_
  15.4 0.0 collective-permute-start.10
  15.4 1.1 %collective-permute-done.4.refs_5_ = bf16[4,8,1280]{2,1,0:T(8,128)(2,1)S(1)} collective-permute-done((bf16[4,8,1280]{2,1,0:T(8,128)(2,1)S(1)}, bf16[4,8,1280]{2,1,0:T(8,128)(2,1)S(1)}, u32[]{:S(2)}, u32[]{:S(2)}) %collective-permute-start.4) | collective-permute-done | bytes 81952 | tf_op jit(solution)/shard_map/ppermute | solution.py:265
  16.5 0.0 collective-permute-start.8
  16.5 0.5 %collective-permute-start.9 = (bf16[4,8,1280]{2,1,0:T(8,128)(2,1)S(1)}, bf16[4,8,1280]{2,1,0:T(8,128)(2,1)S(1)}, u32[]{:S(2)}, u32[]{:S(2)}) collective-permute-start(bf16[4,8,1280]{2,1,0:T(8,128)(2,1)S(1)} %collective-permute-done.5.refs_6_), channel_id=1, source_target_pairs={{0,1},{1,0},{2,3},{3,2},{4,5},{5,4},{6,7},{7,6},{8,9},{9,8},{10,11... | collective-permute-start | bytes 245768 | tf_op jit(solution)/shard_map/ppermute | solution.py:266
  17.0 0.1 collective-permute-done.3
  17.1 1.3 %contract.1 = (bf16[64,8192]{1,0:T(8,128)(2,1)S(1)}, bf16[16,64,128]{2,1,0:T(8,128)(2,1)S(1)}, s32[16,8]{1,0:T(8,128)S(4)}) custom-call(s32[1]{0:T(128)} %bitcast.refs_0_, s32[1]{0:T(128)} %bitcast.1.refs_0_.refs_1_, bf16[4,8,1280]{2,1,0:T(8,128)(2,1)S(1)} %add_dynamic-update-slice_fusion.refs_2_.refs_3_, bf16[4,8,256]{2,1,0:T(8,128)(2,1)S(1)} %slice_add_fusion.refs_3_, ...), custom_call_target="tpu_custom_call" | custom-call | tf_op jit(solution)/shard_map/contract/pallas_call | solution.py:273
  18.4 0.0 collective-permute-done.10.refs_9_
  18.4 0.6 %respond.1 = (f32[32,128]{1,0:T(8,128)S(1)}, f32[32,128]{1,0:T(8,128)S(1)}) custom-call(s32[1]{0:T(128)} %bitcast.refs_0_, s32[1]{0:T(128)} %bitcast.1.refs_0_.refs_1_, s32[16,8]{1,0:T(8,128)S(4)} %get-tuple-element.14.refs_2_, bf16[4,8,1280]{2,1,0:T(8,128)(2,1)S(1)} %add_dynamic-update-slice_fusion.refs_2_.refs_3_, ...), custom_call_target="tpu_custom_call" | custom-call | tf_op jit(solution)/shard_map/respond/pallas_call | solution.py:286
  19.0 0.2 collective-permute-start.11
  19.2 1.1 %collective-permute-done.11 = f32[32,128]{1,0:T(8,128)S(1)} collective-permute-done((f32[32,128]{1,0:T(8,128)S(1)}, f32[32,128]{1,0:T(8,128)S(1)}, u32[]{:S(2)}, u32[]{:S(2)}) %collective-permute-start.11) | collective-permute-done | bytes 16416 | tf_op jit(solution)/shard_map/ppermute | solution.py:353
  20.2 0.6 %add.15 = f32[32,128]{1,0:T(8,128)} add(f32[32,128]{1,0:T(8,128)S(1)} %get-tuple-element.17, f32[32,128]{1,0:T(8,128)S(1)} %collective-permute-done.11) | non-fusion elementwise | flops 4096 | bytes 49152 | tf_op jit(solution)/shard_map/add | solution.py:353
  (9 shorter events, 0.0 us)
Async XLA Ops:
  1.0 1.4 %collective-permute-start = (bf16[4,8,256]{2,1,0:T(8,128)(2,1)S(1)}, bf16[4,8,256]{2,1,0:T(8,128)(2,1)S(1)}, u32[]{:S(2)}, u32[]{:S(2)}) collective-permute-start(bf16[4,8,256]{2,1,0:T(8,128)(2,1)S(1)} %get-tuple-element.13), channel_id=1, source_target_pairs={{0,1},{1,0},{2,3},{3,2},{4,5},{5,4},{6,7},{7,6},{8,9},{9,8},{10,11... | collective-permute-start | bytes 49160 | tf_op jit(solution)/shard_map/ppermute | solution.py:345
  2.4 5.5 %collective-permute-start.1 = (bf16[4,8,256]{2,1,0:T(8,128)(2,1)S(1)}, bf16[4,8,256]{2,1,0:T(8,128)(2,1)S(1)}, u32[]{:S(2)}, u32[]{:S(2)}) collective-permute-start(bf16[4,8,256]{2,1,0:T(8,128)(2,1)S(1)} %get-tuple-element.20), channel_id=1, source_target_pairs={{0,2},{1,3},{2,0},{3,1},{4,6},{5,7},{6,4},{7,5},{8,10},{9,11},{10,... | collective-permute-start | bytes 49160 | tf_op jit(solution)/shard_map/ppermute | solution.py:346
  5.3 7.9 %collective-permute-start.2 = (bf16[4,8,1280]{2,1,0:T(8,128)(2,1)S(1)}, bf16[4,8,1280]{2,1,0:T(8,128)(2,1)S(1)}, u32[]{:S(2)}, u32[]{:S(2)}) collective-permute-start(bf16[4,8,1280]{2,1,0:T(8,128)(2,1)S(1)} %get-tuple-element.19), channel_id=1, source_target_pairs={{16,0},{21,1},{18,2},{23,3},{20,4},{17,5},{22,6},{19,7},{24,8},{29... | collective-permute-start | bytes 245768 | tf_op jit(solution)/shard_map/ppermute | solution.py:265
  7.9 7.5 %collective-permute-start.6 = (bf16[4,8,1280]{2,1,0:T(8,128)(2,1)S(1)}, bf16[4,8,1280]{2,1,0:T(8,128)(2,1)S(1)}, u32[]{:S(2)}, u32[]{:S(2)}) collective-permute-start(bf16[4,8,1280]{2,1,0:T(8,128)(2,1)S(1)} %add_dynamic-update-slice_fusion.refs_2_.refs_3_), channel_id=1, source_target_pairs={{8,0},{13,1},{10,2},{15,3},{12,4},{9,5},{14,6},{11,7},{0,8},{5,9},... | collective-permute-start | bytes 245768 | tf_op jit(solution)/shard_map/ppermute | solution.py:265
  9.5 7.0 %collective-permute-start.4 = (bf16[4,8,1280]{2,1,0:T(8,128)(2,1)S(1)}, bf16[4,8,1280]{2,1,0:T(8,128)(2,1)S(1)}, u32[]{:S(2)}, u32[]{:S(2)}) collective-permute-start(bf16[4,8,1280]{2,1,0:T(8,128)(2,1)S(1)} %add_dynamic-update-slice_fusion.refs_2_.refs_3_), channel_id=1, source_target_pairs={{24,0},{29,1},{26,2},{31,3},{28,4},{25,5},{30,6},{27,7},{16,8},{21... | collective-permute-start | bytes 245768 | tf_op jit(solution)/shard_map/ppermute | solution.py:265
  11.7 4.8 %collective-permute-start.5 = (bf16[4,8,1280]{2,1,0:T(8,128)(2,1)S(1)}, bf16[4,8,1280]{2,1,0:T(8,128)(2,1)S(1)}, u32[]{:S(2)}, u32[]{:S(2)}) collective-permute-start(bf16[4,8,1280]{2,1,0:T(8,128)(2,1)S(1)} %add_dynamic-update-slice_fusion.refs_2_.refs_3_), channel_id=1, source_target_pairs={{5,1},{7,3},{1,5},{3,7},{13,9},{15,11},{9,13},{11,15},{21,17},{23,... | collective-permute-start | bytes 245768 | tf_op jit(solution)/shard_map/ppermute | solution.py:265
  13.2 3.9 %collective-permute-start.3 = (bf16[4,8,256]{2,1,0:T(8,128)(2,1)S(1)}, bf16[4,8,256]{2,1,0:T(8,128)(2,1)S(1)}, u32[]{:S(2)}, u32[]{:S(2)}) collective-permute-start(bf16[4,8,256]{2,1,0:T(8,128)(2,1)S(1)} %slice.4), channel_id=1, source_target_pairs={{0,2},{1,3},{2,0},{3,1},{4,6},{5,7},{6,4},{7,5},{8,10},{9,11},{10,... | collective-permute-start | bytes 49160 | tf_op jit(solution)/shard_map/ppermute | solution.py:268
  13.9 4.5 %collective-permute-start.7 = (bf16[4,8,1280]{2,1,0:T(8,128)(2,1)S(1)}, bf16[4,8,1280]{2,1,0:T(8,128)(2,1)S(1)}, u32[]{:S(2)}, u32[]{:S(2)}) collective-permute-start(bf16[4,8,1280]{2,1,0:T(8,128)(2,1)S(1)} %collective-permute-done.2.refs_4_), channel_id=1, source_target_pairs={{0,1},{1,0},{2,3},{3,2},{4,5},{5,4},{6,7},{7,6},{8,9},{9,8},{10,11... | collective-permute-start | bytes 245768 | tf_op jit(solution)/shard_map/ppermute | solution.py:266
  15.4 3.0 %collective-permute-start.10 = (bf16[4,8,1280]{2,1,0:T(8,128)(2,1)S(1)}, bf16[4,8,1280]{2,1,0:T(8,128)(2,1)S(1)}, u32[]{:S(2)}, u32[]{:S(2)}) collective-permute-start(bf16[4,8,1280]{2,1,0:T(8,128)(2,1)S(1)} %collective-permute-done.6.refs_7_), channel_id=1, source_target_pairs={{0,1},{1,0},{2,3},{3,2},{4,5},{5,4},{6,7},{7,6},{8,9},{9,8},{10,11... | collective-permute-start | bytes 245768 | tf_op jit(solution)/shard_map/ppermute | solution.py:266
  16.5 1.9 %collective-permute-start.8 = (bf16[4,8,1280]{2,1,0:T(8,128)(2,1)S(1)}, bf16[4,8,1280]{2,1,0:T(8,128)(2,1)S(1)}, u32[]{:S(2)}, u32[]{:S(2)}) collective-permute-start(bf16[4,8,1280]{2,1,0:T(8,128)(2,1)S(1)} %collective-permute-done.4.refs_5_), channel_id=1, source_target_pairs={{0,1},{1,0},{2,3},{3,2},{4,5},{5,4},{6,7},{7,6},{8,9},{9,8},{10,11... | collective-permute-start | bytes 245768 | tf_op jit(solution)/shard_map/ppermute | solution.py:266
  16.5 1.9 %collective-permute-start.9 = (bf16[4,8,1280]{2,1,0:T(8,128)(2,1)S(1)}, bf16[4,8,1280]{2,1,0:T(8,128)(2,1)S(1)}, u32[]{:S(2)}, u32[]{:S(2)}) collective-permute-start(bf16[4,8,1280]{2,1,0:T(8,128)(2,1)S(1)} %collective-permute-done.5.refs_6_), channel_id=1, source_target_pairs={{0,1},{1,0},{2,3},{3,2},{4,5},{5,4},{6,7},{7,6},{8,9},{9,8},{10,11... | collective-permute-start | bytes 245768 | tf_op jit(solution)/shard_map/ppermute | solution.py:266
  19.0 1.2 %collective-permute-start.11 = (f32[32,128]{1,0:T(8,128)S(1)}, f32[32,128]{1,0:T(8,128)S(1)}, u32[]{:S(2)}, u32[]{:S(2)}) collective-permute-start(f32[32,128]{1,0:T(8,128)S(1)} %get-tuple-element.18), channel_id=1, source_target_pairs={{0,1},{1,0},{2,3},{3,2},{4,5},{5,4},{6,7},{7,6},{8,9},{9,8},{10,11... | collective-permute-start | bytes 49160 | tf_op jit(solution)/shard_map/ppermute | solution.py:353

commit v7 on v6

--- a/solution.py
+++ b/solution.py
@@ -7,7 +7,7 @@
 
 CHUNK = 4
 BASE = 256
-PAIRS = ((4, 5), (6, 7), (0, 1), (2, 3))
+PAIRS = ((6, 7), (4, 5), (0, 1), (2, 3))
 F32, BF16 = jnp.float32, jnp.bfloat16
 VMEM = pl.BlockSpec(memory_space=pltpu.VMEM)
 SMEM = pl.BlockSpec(memory_space=pltpu.SMEM)

time: 21 us -> 20.9 us (level)
  waiting for transfers between devices: 3.92 us -> 2.01 us
  starting transfers between devices: 13.3 us -> 15 us
    ppermute x4, waiting for transfers between devices: 1.94 us -> 0.32 us  [respond_direct(): lax.ppermute(full if slot else early, ('wide', 'pair'), route)]
    ppermute x1, starting transfers between devices: 0.71 us -> 1.56 us  [respond_direct(): small = small + lax.ppermute(small, 'pair', across)]
    ppermute x1, starting transfers between devices: 0.17 us -> 0.56 us  [local(): return keep + lax.ppermute(send, 'pair', partner)]
    ppermute x4, starting transfers between devices: 2.02 us -> 2.39 us  [respond_direct(): far.append(lax.ppermute(fetched[-1], 'pair', partner))]
    ppermute x1, waiting for transfers between devices: 1.07 us -> 0.84 us  [local(): return keep + lax.ppermute(send, 'pair', partner)]
  transfers between devices with their start and end apart: 12 -> 12, of which waited for: 5 -> 3; matrix products, arithmetic and copies ran while one was open for 0% -> 0% of each run, Pallas kernels for 6% -> 6%
where the time goes in v7:
time: 20.9 us; the launch traced here: 20.7 us
  starting transfers between devices  15 us (72%)
  Pallas kernels  2.88 us (14%)
  waiting for transfers between devices  2.01 us (10%)
  other arithmetic  0.63 us (3%)
    ppermute x4, starting transfers between devices, respond_direct(): lax.ppermute(full if slot else early, ('wide', 'pair'), route)  7.13 us
    ppermute x1, starting transfers between devices, local(): four = two + lax.ppermute(two, 'pair', across)  2.9 us
    ppermute x4, starting transfers between devices, respond_direct(): far.append(lax.ppermute(fetched[-1], 'pair', partner))  2.39 us
    ppermute x1, starting transfers between devices, respond_direct(): small = small + lax.ppermute(small, 'pair', across)  1.56 us
    pallas_call x1, Pallas kernels, respond_direct(): pl.pallas_call(kernel_of(contract_kernel, unit_count), out_shape=(pltpu.V...  1.31 us
    pallas_call x1, Pallas kernels, local(): pl.pallas_call(kernel_of(pack_kernel, unit_count), out_shape=(pltpu.VMEM(...  1.02 us
    ppermute x1, waiting for transfers between devices, local(): return keep + lax.ppermute(send, 'pair', partner)  0.84 us
    ppermute x1, waiting for transfers between devices, local(): two = small + lax.ppermute(small, 'pair', partner)  0.83 us
  transfers between devices with their start and end apart: 12, of which 3 were waited for; matrix products, arithmetic and copies ran while one was open for 0% of the time, Pallas kernels for 6%

profile of v7, /device:TPU:0, one launch (start us, length us, event | category | flops | bytes accessed | tf_op | source)
XLA Modules:
  0.0 20.7 jit_solution(8743529579580031584)
XLA Ops:
  0.0 1.0 %pack.1 = (bf16[4,8,1280]{2,1,0:T(8,128)(2,1)S(1)}, bf16[4,8,256]{2,1,0:T(8,128)(2,1)S(1)}) custom-call(s32[1]{0:T(128)} %bitcast.1.refs_0_.refs_1_, s32[2,4]{1,0:T(2,128)} %bitcast.4, s32[2,4]{1,0:T(2,128)} %bitcast.5, bf16[4,8,1024]{2,1,0:T(8,128)(2,1)} %refs_3_.1, bf16[4,2,8,8]{3,2,1,0:T(8,128)(2,1)} %refs_4_.1, bf16[4,2,8,8]{3,2,1,0:T(8,128)(2,1)} %refs_5_.1), custom_call_target="tpu_custom_call" | custom-call | tf_op jit(solution)/shard_map/pack/pallas_call | solution.py:335
  1.0 0.5 %collective-permute-start = (bf16[4,8,256]{2,1,0:T(8,128)(2,1)S(1)}, bf16[4,8,256]{2,1,0:T(8,128)(2,1)S(1)}, u32[]{:S(2)}, u32[]{:S(2)}) collective-permute-start(bf16[4,8,256]{2,1,0:T(8,128)(2,1)S(1)} %get-tuple-element.13), channel_id=1, source_target_pairs={{0,1},{1,0},{2,3},{3,2},{4,5},{5,4},{6,7},{7,6},{8,9},{9,8},{10,11... | collective-permute-start | bytes 49160 | tf_op jit(solution)/shard_map/ppermute | solution.py:345
  1.5 0.8 %collective-permute-done = bf16[4,8,256]{2,1,0:T(8,128)(2,1)S(1)} collective-permute-done((bf16[4,8,256]{2,1,0:T(8,128)(2,1)S(1)}, bf16[4,8,256]{2,1,0:T(8,128)(2,1)S(1)}, u32[]{:S(2)}, u32[]{:S(2)}) %collective-permute-start) | collective-permute-done | bytes 16416 | tf_op jit(solution)/shard_map/ppermute | solution.py:345
  2.4 2.9 %collective-permute-start.1 = (bf16[4,8,256]{2,1,0:T(8,128)(2,1)S(1)}, bf16[4,8,256]{2,1,0:T(8,128)(2,1)S(1)}, u32[]{:S(2)}, u32[]{:S(2)}) collective-permute-start(bf16[4,8,256]{2,1,0:T(8,128)(2,1)S(1)} %get-tuple-element.20), channel_id=1, source_target_pairs={{0,2},{1,3},{2,0},{3,1},{4,6},{5,7},{6,4},{7,5},{8,10},{9,11},{10,... | collective-permute-start | bytes 49160 | tf_op jit(solution)/shard_map/ppermute | solution.py:346
  5.3 3.6 %collective-permute-start.2 = (bf16[4,8,1280]{2,1,0:T(8,128)(2,1)S(1)}, bf16[4,8,1280]{2,1,0:T(8,128)(2,1)S(1)}, u32[]{:S(2)}, u32[]{:S(2)}) collective-permute-start(bf16[4,8,1280]{2,1,0:T(8,128)(2,1)S(1)} %get-tuple-element.19), channel_id=1, source_target_pairs={{24,0},{29,1},{26,2},{31,3},{28,4},{25,5},{30,6},{27,7},{16,8},{21... | collective-permute-start | bytes 245768 | tf_op jit(solution)/shard_map/ppermute | solution.py:265
  8.9 0.3 %collective-permute-start.6 = (bf16[4,8,1280]{2,1,0:T(8,128)(2,1)S(1)}, bf16[4,8,1280]{2,1,0:T(8,128)(2,1)S(1)}, u32[]{:S(2)}, u32[]{:S(2)}) collective-permute-start(bf16[4,8,1280]{2,1,0:T(8,128)(2,1)S(1)} %add_dynamic-update-slice_fusion.refs_2_.refs_3_), channel_id=1, source_target_pairs={{8,0},{13,1},{10,2},{15,3},{12,4},{9,5},{14,6},{11,7},{0,8},{5,9},... | collective-permute-start | bytes 245768 | tf_op jit(solution)/shard_map/ppermute | solution.py:265
  9.2 2.6 %collective-permute-start.4 = (bf16[4,8,1280]{2,1,0:T(8,128)(2,1)S(1)}, bf16[4,8,1280]{2,1,0:T(8,128)(2,1)S(1)}, u32[]{:S(2)}, u32[]{:S(2)}) collective-permute-start(bf16[4,8,1280]{2,1,0:T(8,128)(2,1)S(1)} %add_dynamic-update-slice_fusion.refs_2_.refs_3_), channel_id=1, source_target_pairs={{16,0},{21,1},{18,2},{23,3},{20,4},{17,5},{22,6},{19,7},{24,8},{29... | collective-permute-start | bytes 245768 | tf_op jit(solution)/shard_map/ppermute | solution.py:265
  11.8 0.7 %collective-permute-start.5 = (bf16[4,8,1280]{2,1,0:T(8,128)(2,1)S(1)}, bf16[4,8,1280]{2,1,0:T(8,128)(2,1)S(1)}, u32[]{:S(2)}, u32[]{:S(2)}) collective-permute-start(bf16[4,8,1280]{2,1,0:T(8,128)(2,1)S(1)} %add_dynamic-update-slice_fusion.refs_2_.refs_3_), channel_id=1, source_target_pairs={{5,1},{7,3},{1,5},{3,7},{13,9},{15,11},{9,13},{11,15},{21,17},{23,... | collective-permute-start | bytes 245768 | tf_op jit(solution)/shard_map/ppermute | solution.py:265
  12.4 0.0 collective-permute-done.2.refs_4_
  12.5 1.6 %collective-permute-start.3 = (bf16[4,8,256]{2,1,0:T(8,128)(2,1)S(1)}, bf16[4,8,256]{2,1,0:T(8,128)(2,1)S(1)}, u32[]{:S(2)}, u32[]{:S(2)}) collective-permute-start(bf16[4,8,256]{2,1,0:T(8,128)(2,1)S(1)} %slice.4), channel_id=1, source_target_pairs={{0,2},{1,3},{2,0},{3,1},{4,6},{5,7},{6,4},{7,5},{8,10},{9,11},{10,... | collective-permute-start | bytes 49160 | tf_op jit(solution)/shard_map/ppermute | solution.py:268
  14.0 1.5 %collective-permute-start.7 = (bf16[4,8,1280]{2,1,0:T(8,128)(2,1)S(1)}, bf16[4,8,1280]{2,1,0:T(8,128)(2,1)S(1)}, u32[]{:S(2)}, u32[]{:S(2)}) collective-permute-start(bf16[4,8,1280]{2,1,0:T(8,128)(2,1)S(1)} %collective-permute-done.2.refs_4_), channel_id=1, source_target_pairs={{0,1},{1,0},{2,3},{3,2},{4,5},{5,4},{6,7},{7,6},{8,9},{9,8},{10,11... | collective-permute-start | bytes 245768 | tf_op jit(solution)/shard_map/ppermute | solution.py:266
  15.5 0.3 %collective-permute-done.6.refs_7_ = bf16[4,8,1280]{2,1,0:T(8,128)(2,1)S(1)} collective-permute-done((bf16[4,8,1280]{2,1,0:T(8,128)(2,1)S(1)}, bf16[4,8,1280]{2,1,0:T(8,128)(2,1)S(1)}, u32[]{:S(2)}, u32[]{:S(2)}) %collective-permute-start.6) | collective-permute-done | bytes 81952 | tf_op jit(solution)/shard_map/ppermute | solution.py:265
  15.8 0.0 collective-permute-start.10
  15.8 0.9 %collective-permute-start.8 = (bf16[4,8,1280]{2,1,0:T(8,128)(2,1)S(1)}, bf16[4,8,1280]{2,1,0:T(8,128)(2,1)S(1)}, u32[]{:S(2)}, u32[]{:S(2)}) collective-permute-start(bf16[4,8,1280]{2,1,0:T(8,128)(2,1)S(1)} %collective-permute-done.4.refs_5_), channel_id=1, source_target_pairs={{0,1},{1,0},{2,3},{3,2},{4,5},{5,4},{6,7},{7,6},{8,9},{9,8},{10,11... | collective-permute-start | bytes 245768 | tf_op jit(solution)/shard_map/ppermute | solution.py:266
  16.7 0.0 collective-permute-done.5.refs_6_
  16.7 0.0 collective-permute-start.9
  16.7 0.0 collective-permute-done.3
  16.7 1.3 %contract.1 = (bf16[64,8192]{1,0:T(8,128)(2,1)S(1)}, bf16[16,64,128]{2,1,0:T(8,128)(2,1)S(1)}, s32[16,8]{1,0:T(8,128)S(4)}) custom-call(s32[1]{0:T(128)} %bitcast.refs_0_, s32[1]{0:T(128)} %bitcast.1.refs_0_.refs_1_, bf16[4,8,1280]{2,1,0:T(8,128)(2,1)S(1)} %add_dynamic-update-slice_fusion.refs_2_.refs_3_, bf16[4,8,256]{2,1,0:T(8,128)(2,1)S(1)} %slice_add_fusion.refs_3_, ...), custom_call_target="tpu_custom_call" | custom-call | tf_op jit(solution)/shard_map/contract/pallas_call | solution.py:273
  18.1 0.0 collective-permute-done.7.refs_6_
  18.1 0.0 collective-permute-done.10.refs_9_
  18.1 0.6 %respond.1 = (f32[32,128]{1,0:T(8,128)S(1)}, f32[32,128]{1,0:T(8,128)S(1)}) custom-call(s32[1]{0:T(128)} %bitcast.refs_0_, s32[1]{0:T(128)} %bitcast.1.refs_0_.refs_1_, s32[16,8]{1,0:T(8,128)S(4)} %get-tuple-element.14.refs_2_, bf16[4,8,1280]{2,1,0:T(8,128)(2,1)S(1)} %add_dynamic-update-slice_fusion.refs_2_.refs_3_, ...), custom_call_target="tpu_custom_call" | custom-call | tf_op jit(solution)/shard_map/respond/pallas_call | solution.py:286
  18.7 0.6 %collective-permute-start.11 = (f32[32,128]{1,0:T(8,128)S(1)}, f32[32,128]{1,0:T(8,128)S(1)}, u32[]{:S(2)}, u32[]{:S(2)}) collective-permute-start(f32[32,128]{1,0:T(8,128)S(1)} %get-tuple-element.18), channel_id=1, source_target_pairs={{0,1},{1,0},{2,3},{3,2},{4,5},{5,4},{6,7},{7,6},{8,9},{9,8},{10,11... | collective-permute-start | bytes 49160 | tf_op jit(solution)/shard_map/ppermute | solution.py:353
  19.2 0.8 %collective-permute-done.11 = f32[32,128]{1,0:T(8,128)S(1)} collective-permute-done((f32[32,128]{1,0:T(8,128)S(1)}, f32[32,128]{1,0:T(8,128)S(1)}, u32[]{:S(2)}, u32[]{:S(2)}) %collective-permute-start.11) | collective-permute-done | bytes 16416 | tf_op jit(solution)/shard_map/ppermute | solution.py:353
  20.1 0.6 %add.15 = f32[32,128]{1,0:T(8,128)} add(f32[32,128]{1,0:T(8,128)S(1)} %get-tuple-element.17, f32[32,128]{1,0:T(8,128)S(1)} %collective-permute-done.11) | non-fusion elementwise | flops 4096 | bytes 49152 | tf_op jit(solution)/shard_map/add | solution.py:353
  (9 shorter events, 0.0 us)
Async XLA Ops:
  1.0 1.4 %collective-permute-start = (bf16[4,8,256]{2,1,0:T(8,128)(2,1)S(1)}, bf16[4,8,256]{2,1,0:T(8,128)(2,1)S(1)}, u32[]{:S(2)}, u32[]{:S(2)}) collective-permute-start(bf16[4,8,256]{2,1,0:T(8,128)(2,1)S(1)} %get-tuple-element.13), channel_id=1, source_target_pairs={{0,1},{1,0},{2,3},{3,2},{4,5},{5,4},{6,7},{7,6},{8,9},{9,8},{10,11... | collective-permute-start | bytes 49160 | tf_op jit(solution)/shard_map/ppermute | solution.py:345
  2.4 6.5 %collective-permute-start.1 = (bf16[4,8,256]{2,1,0:T(8,128)(2,1)S(1)}, bf16[4,8,256]{2,1,0:T(8,128)(2,1)S(1)}, u32[]{:S(2)}, u32[]{:S(2)}) collective-permute-start(bf16[4,8,256]{2,1,0:T(8,128)(2,1)S(1)} %get-tuple-element.20), channel_id=1, source_target_pairs={{0,2},{1,3},{2,0},{3,1},{4,6},{5,7},{6,4},{7,5},{8,10},{9,11},{10,... | collective-permute-start | bytes 49160 | tf_op jit(solution)/shard_map/ppermute | solution.py:346
  5.3 7.2 %collective-permute-start.2 = (bf16[4,8,1280]{2,1,0:T(8,128)(2,1)S(1)}, bf16[4,8,1280]{2,1,0:T(8,128)(2,1)S(1)}, u32[]{:S(2)}, u32[]{:S(2)}) collective-permute-start(bf16[4,8,1280]{2,1,0:T(8,128)(2,1)S(1)} %get-tuple-element.19), channel_id=1, source_target_pairs={{24,0},{29,1},{26,2},{31,3},{28,4},{25,5},{30,6},{27,7},{16,8},{21... | collective-permute-start | bytes 245768 | tf_op jit(solution)/shard_map/ppermute | solution.py:265
  8.9 6.9 %collective-permute-start.6 = (bf16[4,8,1280]{2,1,0:T(8,128)(2,1)S(1)}, bf16[4,8,1280]{2,1,0:T(8,128)(2,1)S(1)}, u32[]{:S(2)}, u32[]{:S(2)}) collective-permute-start(bf16[4,8,1280]{2,1,0:T(8,128)(2,1)S(1)} %add_dynamic-update-slice_fusion.refs_2_.refs_3_), channel_id=1, source_target_pairs={{8,0},{13,1},{10,2},{15,3},{12,4},{9,5},{14,6},{11,7},{0,8},{5,9},... | collective-permute-start | bytes 245768 | tf_op jit(solution)/shard_map/ppermute | solution.py:265
  9.2 6.7 %collective-permute-start.4 = (bf16[4,8,1280]{2,1,0:T(8,128)(2,1)S(1)}, bf16[4,8,1280]{2,1,0:T(8,128)(2,1)S(1)}, u32[]{:S(2)}, u32[]{:S(2)}) collective-permute-start(bf16[4,8,1280]{2,1,0:T(8,128)(2,1)S(1)} %add_dynamic-update-slice_fusion.refs_2_.refs_3_), channel_id=1, source_target_pairs={{16,0},{21,1},{18,2},{23,3},{20,4},{17,5},{22,6},{19,7},{24,8},{29... | collective-permute-start | bytes 245768 | tf_op jit(solution)/shard_map/ppermute | solution.py:265
  11.8 4.9 %collective-permute-start.5 = (bf16[4,8,1280]{2,1,0:T(8,128)(2,1)S(1)}, bf16[4,8,1280]{2,1,0:T(8,128)(2,1)S(1)}, u32[]{:S(2)}, u32[]{:S(2)}) collective-permute-start(bf16[4,8,1280]{2,1,0:T(8,128)(2,1)S(1)} %add_dynamic-update-slice_fusion.refs_2_.refs_3_), channel_id=1, source_target_pairs={{5,1},{7,3},{1,5},{3,7},{13,9},{15,11},{9,13},{11,15},{21,17},{23,... | collective-permute-start | bytes 245768 | tf_op jit(solution)/shard_map/ppermute | solution.py:265
  12.5 4.3 %collective-permute-start.3 = (bf16[4,8,256]{2,1,0:T(8,128)(2,1)S(1)}, bf16[4,8,256]{2,1,0:T(8,128)(2,1)S(1)}, u32[]{:S(2)}, u32[]{:S(2)}) collective-permute-start(bf16[4,8,256]{2,1,0:T(8,128)(2,1)S(1)} %slice.4), channel_id=1, source_target_pairs={{0,2},{1,3},{2,0},{3,1},{4,6},{5,7},{6,4},{7,5},{8,10},{9,11},{10,... | collective-permute-start | bytes 49160 | tf_op jit(solution)/shard_map/ppermute | solution.py:268
  14.0 4.0 %collective-permute-start.7 = (bf16[4,8,1280]{2,1,0:T(8,128)(2,1)S(1)}, bf16[4,8,1280]{2,1,0:T(8,128)(2,1)S(1)}, u32[]{:S(2)}, u32[]{:S(2)}) collective-permute-start(bf16[4,8,1280]{2,1,0:T(8,128)(2,1)S(1)} %collective-permute-done.2.refs_4_), channel_id=1, source_target_pairs={{0,1},{1,0},{2,3},{3,2},{4,5},{5,4},{6,7},{7,6},{8,9},{9,8},{10,11... | collective-permute-start | bytes 245768 | tf_op jit(solution)/shard_map/ppermute | solution.py:266
  15.8 2.2 %collective-permute-start.10 = (bf16[4,8,1280]{2,1,0:T(8,128)(2,1)S(1)}, bf16[4,8,1280]{2,1,0:T(8,128)(2,1)S(1)}, u32[]{:S(2)}, u32[]{:S(2)}) collective-permute-start(bf16[4,8,1280]{2,1,0:T(8,128)(2,1)S(1)} %collective-permute-done.6.refs_7_), channel_id=1, source_target_pairs={{0,1},{1,0},{2,3},{3,2},{4,5},{5,4},{6,7},{7,6},{8,9},{9,8},{10,11... | collective-permute-start | bytes 245768 | tf_op jit(solution)/shard_map/ppermute | solution.py:266
  15.8 2.2 %collective-permute-start.8 = (bf16[4,8,1280]{2,1,0:T(8,128)(2,1)S(1)}, bf16[4,8,1280]{2,1,0:T(8,128)(2,1)S(1)}, u32[]{:S(2)}, u32[]{:S(2)}) collective-permute-start(bf16[4,8,1280]{2,1,0:T(8,128)(2,1)S(1)} %collective-permute-done.4.refs_5_), channel_id=1, source_target_pairs={{0,1},{1,0},{2,3},{3,2},{4,5},{5,4},{6,7},{7,6},{8,9},{9,8},{10,11... | collective-permute-start | bytes 245768 | tf_op jit(solution)/shard_map/ppermute | solution.py:266
  16.7 1.4 %collective-permute-start.9 = (bf16[4,8,1280]{2,1,0:T(8,128)(2,1)S(1)}, bf16[4,8,1280]{2,1,0:T(8,128)(2,1)S(1)}, u32[]{:S(2)}, u32[]{:S(2)}) collective-permute-start(bf16[4,8,1280]{2,1,0:T(8,128)(2,1)S(1)} %collective-permute-done.5.refs_6_), channel_id=1, source_target_pairs={{0,1},{1,0},{2,3},{3,2},{4,5},{5,4},{6,7},{7,6},{8,9},{9,8},{10,11... | collective-permute-start | bytes 245768 | tf_op jit(solution)/shard_map/ppermute | solution.py:266
  18.7 1.4 %collective-permute-start.11 = (f32[32,128]{1,0:T(8,128)S(1)}, f32[32,128]{1,0:T(8,128)S(1)}, u32[]{:S(2)}, u32[]{:S(2)}) collective-permute-start(f32[32,128]{1,0:T(8,128)S(1)} %get-tuple-element.18), channel_id=1, source_target_pairs={{0,1},{1,0},{2,3},{3,2},{4,5},{5,4},{6,7},{7,6},{8,9},{9,8},{10,11... | collective-permute-start | bytes 49160 | tf_op jit(solution)/shard_map/ppermute | solution.py:353

commit v8 on v7

--- a/solution.py
+++ b/solution.py
@@ -7,6 +7,7 @@
 
 CHUNK = 4
 BASE = 256
+PAIR_STEP = 4096
 PAIRS = ((6, 7), (4, 5), (0, 1), (2, 3))
 F32, BF16 = jnp.float32, jnp.bfloat16
 VMEM = pl.BlockSpec(memory_space=pltpu.VMEM)
@@ -124,9 +125,17 @@
 
 def join_columns(digits, unit_count):
     row, lane = (iota((digits.shape[1], ceil_to(unit_count, 128)), axis) for axis in range(2))
-    join = jnp.where(row == lane, float(BASE), 0.0) + jnp.where(row == unit_count + lane, 1.0, 0.0)
-    join = jnp.where(lane < unit_count, join, 0.0).astype(BF16)
+    join = jnp.zeros(row.shape, F32)
+    for member, step in enumerate((1.0, float(PAIR_STEP))):
+        join += jnp.where(row == 2 * lane + member, BASE * step, 0.0)
+        join += jnp.where(row == unit_count + 2 * lane + member, step, 0.0)
+    join = jnp.where(lane < unit_count // 2, join, 0.0).astype(BF16)
     return jnp.dot(digits, join, preferred_element_type=F32).astype(jnp.int32)
+
+
+def column_pair(joined, row, pair):
+    value = joined[row, pair]
+    return value & (PAIR_STEP - 1), value >> PAIR_STEP.bit_length() - 1
 
 
 def write_rows(total, half, keep_ref, send_ref):
@@ -160,6 +169,12 @@
             small = block[:, block_size * aux_count :]
             small_ref[place + atom] = early_ref[atom] if slot == 0 else small
     atoms = range(count * local_atoms)
+    digits = jnp.concatenate([small_ref[atom, :, column_at:] for atom in atoms], axis=0)
+    joined = join_columns(digits, unit_count)
+    for atom in atoms:
+        for pair in range(unit_count // 2):
+            columns = column_pair(joined, atom * block_size, pair)
+            index_ref[atom, 2 * pair], index_ref[atom, 2 * pair + 1] = columns
     rows = turned([own_rows(rows_ref[atom], outer, row_count) for atom in atoms])
     for chunk in range(chunk_count):
         lane_at = chunk * 2 * CHUNK * block_size
@@ -167,11 +182,6 @@
         smalls = [small_ref[atom, :, tile : tile + 128] for atom in atoms]
         first = chunk * len(atoms) * CHUNK * block_size * block_size
         contract(rows, smalls, spread_small(block_size, lane_at - tile), both_ref, first)
-    digits = jnp.concatenate([small_ref[atom, :, column_at:] for atom in atoms], axis=0)
-    joined = join_columns(digits, unit_count)
-    for atom in atoms:
-        for unit in range(unit_count):
-            index_ref[atom, unit] = joined[atom * block_size, unit]
 
 
 def respond_kernel(unit_count, wide_ref, pair_ref, index_ref, own_ref, both_ref, near_ref, *refs):
@@ -234,7 +244,8 @@
             for member in range(group):
                 for unit in range(chunk * CHUNK, (chunk + 1) * CHUNK):
                     if unit < unit_count:
-                        found.append(rows_ref[joined[member * block_size, unit]])
+                        columns = column_pair(joined, member * block_size, unit // 2)
+                        found.append(rows_ref[columns[unit % 2]])
                     else:
                         found.append(jnp.zeros(rows_ref.shape[1:], BF16))
             total += jnp.dot(

time: 20.9 us -> 20.6 us (0.986)
  Pallas kernels: 2.88 us -> 2.6 us
  waiting for transfers between devices: 2.01 us -> 2.22 us
    pallas_call x1, Pallas kernels: 1.31 us -> 1.04 us  [respond_direct(): pl.pallas_call(kernel_of(contract_kernel, unit_count), out_shape=(pltpu.V...]
  transfers between devices with their start and end apart: 12 -> 12, of which waited for: 3 -> 4; matrix products, arithmetic and copies ran while one was open for 0% -> 0% of each run, Pallas kernels for 6% -> 5%
where the time goes in v8:
time: 20.6 us; the launch traced here: 20.4 us
  starting transfers between devices  14.9 us (72%)
  Pallas kernels  2.6 us (13%)
  waiting for transfers between devices  2.22 us (11%)
  other arithmetic  0.63 us (3%)
    ppermute x4, starting transfers between devices, respond_direct(): lax.ppermute(full if slot else early, ('wide', 'pair'), route)  7.13 us
    ppermute x1, starting transfers between devices, local(): four = two + lax.ppermute(two, 'pair', across)  2.9 us
    ppermute x4, starting transfers between devices, respond_direct(): far.append(lax.ppermute(fetched[-1], 'pair', partner))  2.39 us
    ppermute x1, starting transfers between devices, respond_direct(): small = small + lax.ppermute(small, 'pair', across)  1.56 us
    pallas_call x1, Pallas kernels, respond_direct(): pl.pallas_call(kernel_of(contract_kernel, unit_count), out_shape=(pltpu.V...  1.04 us
    pallas_call x1, Pallas kernels, local(): pl.pallas_call(kernel_of(pack_kernel, unit_count), out_shape=(pltpu.VMEM(...  1.02 us
    ppermute x1, waiting for transfers between devices, local(): return keep + lax.ppermute(send, 'pair', partner)  0.87 us
    ppermute x1, waiting for transfers between devices, local(): two = small + lax.ppermute(small, 'pair', partner)  0.83 us
  transfers between devices with their start and end apart: 12, of which 4 were waited for; matrix products, arithmetic and copies ran while one was open for 0% of the time, Pallas kernels for 5%

profile of v8, /device:TPU:0, one launch (start us, length us, event | category | flops | bytes accessed | tf_op | source)
XLA Modules:
  0.0 20.4 jit_solution(258314718125236819)
XLA Ops:
  0.0 1.0 %pack.1 = (bf16[4,8,1280]{2,1,0:T(8,128)(2,1)S(1)}, bf16[4,8,256]{2,1,0:T(8,128)(2,1)S(1)}) custom-call(s32[1]{0:T(128)} %bitcast.1.refs_0_.refs_1_, s32[2,4]{1,0:T(2,128)} %bitcast.4, s32[2,4]{1,0:T(2,128)} %bitcast.5, bf16[4,8,1024]{2,1,0:T(8,128)(2,1)} %refs_3_.1, bf16[4,2,8,8]{3,2,1,0:T(8,128)(2,1)} %refs_4_.1, bf16[4,2,8,8]{3,2,1,0:T(8,128)(2,1)} %refs_5_.1), custom_call_target="tpu_custom_call" | custom-call | tf_op jit(solution)/shard_map/pack/pallas_call | solution.py:346
  1.0 0.5 %collective-permute-start = (bf16[4,8,256]{2,1,0:T(8,128)(2,1)S(1)}, bf16[4,8,256]{2,1,0:T(8,128)(2,1)S(1)}, u32[]{:S(2)}, u32[]{:S(2)}) collective-permute-start(bf16[4,8,256]{2,1,0:T(8,128)(2,1)S(1)} %get-tuple-element.13), channel_id=1, source_target_pairs={{0,1},{1,0},{2,3},{3,2},{4,5},{5,4},{6,7},{7,6},{8,9},{9,8},{10,11... | collective-permute-start | bytes 49160 | tf_op jit(solution)/shard_map/ppermute | solution.py:356
  1.5 0.8 %collective-permute-done = bf16[4,8,256]{2,1,0:T(8,128)(2,1)S(1)} collective-permute-done((bf16[4,8,256]{2,1,0:T(8,128)(2,1)S(1)}, bf16[4,8,256]{2,1,0:T(8,128)(2,1)S(1)}, u32[]{:S(2)}, u32[]{:S(2)}) %collective-permute-start) | collective-permute-done | bytes 16416 | tf_op jit(solution)/shard_map/ppermute | solution.py:356
  2.4 2.9 %collective-permute-start.1 = (bf16[4,8,256]{2,1,0:T(8,128)(2,1)S(1)}, bf16[4,8,256]{2,1,0:T(8,128)(2,1)S(1)}, u32[]{:S(2)}, u32[]{:S(2)}) collective-permute-start(bf16[4,8,256]{2,1,0:T(8,128)(2,1)S(1)} %get-tuple-element.20), channel_id=1, source_target_pairs={{0,2},{1,3},{2,0},{3,1},{4,6},{5,7},{6,4},{7,5},{8,10},{9,11},{10,... | collective-permute-start | bytes 49160 | tf_op jit(solution)/shard_map/ppermute | solution.py:357
  5.3 3.6 %collective-permute-start.2 = (bf16[4,8,1280]{2,1,0:T(8,128)(2,1)S(1)}, bf16[4,8,1280]{2,1,0:T(8,128)(2,1)S(1)}, u32[]{:S(2)}, u32[]{:S(2)}) collective-permute-start(bf16[4,8,1280]{2,1,0:T(8,128)(2,1)S(1)} %get-tuple-element.19), channel_id=1, source_target_pairs={{24,0},{29,1},{26,2},{31,3},{28,4},{25,5},{30,6},{27,7},{16,8},{21... | collective-permute-start | bytes 245768 | tf_op jit(solution)/shard_map/ppermute | solution.py:276
  8.9 0.0 collective-permute-done.1
  8.9 0.3 %collective-permute-start.6 = (bf16[4,8,1280]{2,1,0:T(8,128)(2,1)S(1)}, bf16[4,8,1280]{2,1,0:T(8,128)(2,1)S(1)}, u32[]{:S(2)}, u32[]{:S(2)}) collective-permute-start(bf16[4,8,1280]{2,1,0:T(8,128)(2,1)S(1)} %add_dynamic-update-slice_fusion.refs_2_.refs_3_), channel_id=1, source_target_pairs={{8,0},{13,1},{10,2},{15,3},{12,4},{9,5},{14,6},{11,7},{0,8},{5,9},... | collective-permute-start | bytes 245768 | tf_op jit(solution)/shard_map/ppermute | solution.py:276
  9.2 2.6 %collective-permute-start.4 = (bf16[4,8,1280]{2,1,0:T(8,128)(2,1)S(1)}, bf16[4,8,1280]{2,1,0:T(8,128)(2,1)S(1)}, u32[]{:S(2)}, u32[]{:S(2)}) collective-permute-start(bf16[4,8,1280]{2,1,0:T(8,128)(2,1)S(1)} %add_dynamic-update-slice_fusion.refs_2_.refs_3_), channel_id=1, source_target_pairs={{16,0},{21,1},{18,2},{23,3},{20,4},{17,5},{22,6},{19,7},{24,8},{29... | collective-permute-start | bytes 245768 | tf_op jit(solution)/shard_map/ppermute | solution.py:276
  11.8 0.7 %collective-permute-start.5 = (bf16[4,8,1280]{2,1,0:T(8,128)(2,1)S(1)}, bf16[4,8,1280]{2,1,0:T(8,128)(2,1)S(1)}, u32[]{:S(2)}, u32[]{:S(2)}) collective-permute-start(bf16[4,8,1280]{2,1,0:T(8,128)(2,1)S(1)} %add_dynamic-update-slice_fusion.refs_2_.refs_3_), channel_id=1, source_target_pairs={{5,1},{7,3},{1,5},{3,7},{13,9},{15,11},{9,13},{11,15},{21,17},{23,... | collective-permute-start | bytes 245768 | tf_op jit(solution)/shard_map/ppermute | solution.py:276
  12.5 1.6 %collective-permute-start.3 = (bf16[4,8,256]{2,1,0:T(8,128)(2,1)S(1)}, bf16[4,8,256]{2,1,0:T(8,128)(2,1)S(1)}, u32[]{:S(2)}, u32[]{:S(2)}) collective-permute-start(bf16[4,8,256]{2,1,0:T(8,128)(2,1)S(1)} %slice.4), channel_id=1, source_target_pairs={{0,2},{1,3},{2,0},{3,1},{4,6},{5,7},{6,4},{7,5},{8,10},{9,11},{10,... | collective-permute-start | bytes 49160 | tf_op jit(solution)/shard_map/ppermute | solution.py:279
  14.0 1.5 %collective-permute-start.7 = (bf16[4,8,1280]{2,1,0:T(8,128)(2,1)S(1)}, bf16[4,8,1280]{2,1,0:T(8,128)(2,1)S(1)}, u32[]{:S(2)}, u32[]{:S(2)}) collective-permute-start(bf16[4,8,1280]{2,1,0:T(8,128)(2,1)S(1)} %collective-permute-done.2.refs_4_), channel_id=1, source_target_pairs={{0,1},{1,0},{2,3},{3,2},{4,5},{5,4},{6,7},{7,6},{8,9},{9,8},{10,11... | collective-permute-start | bytes 245768 | tf_op jit(solution)/shard_map/ppermute | solution.py:277
  15.5 0.3 %collective-permute-done.6.refs_7_ = bf16[4,8,1280]{2,1,0:T(8,128)(2,1)S(1)} collective-permute-done((bf16[4,8,1280]{2,1,0:T(8,128)(2,1)S(1)}, bf16[4,8,1280]{2,1,0:T(8,128)(2,1)S(1)}, u32[]{:S(2)}, u32[]{:S(2)}) %collective-permute-start.6) | collective-permute-done | bytes 81952 | tf_op jit(solution)/shard_map/ppermute | solution.py:276
  15.8 0.0 collective-permute-start.10
  15.8 0.0 collective-permute-done.4.refs_5_
  15.8 0.9 %collective-permute-start.8 = (bf16[4,8,1280]{2,1,0:T(8,128)(2,1)S(1)}, bf16[4,8,1280]{2,1,0:T(8,128)(2,1)S(1)}, u32[]{:S(2)}, u32[]{:S(2)}) collective-permute-start(bf16[4,8,1280]{2,1,0:T(8,128)(2,1)S(1)} %collective-permute-done.4.refs_5_), channel_id=1, source_target_pairs={{0,1},{1,0},{2,3},{3,2},{4,5},{5,4},{6,7},{7,6},{8,9},{9,8},{10,11... | collective-permute-start | bytes 245768 | tf_op jit(solution)/shard_map/ppermute | solution.py:277
  16.7 0.0 collective-permute-start.9
  16.7 0.0 collective-permute-done.3
  16.7 1.0 %contract.1 = (bf16[64,8192]{1,0:T(8,128)(2,1)S(1)}, bf16[16,64,128]{2,1,0:T(8,128)(2,1)S(1)}, s32[16,8]{1,0:T(8,128)S(4)}) custom-call(s32[1]{0:T(128)} %bitcast.refs_0_, s32[1]{0:T(128)} %bitcast.1.refs_0_.refs_1_, bf16[4,8,1280]{2,1,0:T(8,128)(2,1)S(1)} %add_dynamic-update-slice_fusion.refs_2_.refs_3_, bf16[4,8,256]{2,1,0:T(8,128)(2,1)S(1)} %slice_add_fusion.refs_3_, ...), custom_call_target="tpu_custom_call" | custom-call | tf_op jit(solution)/shard_map/contract/pallas_call | solution.py:284
  17.8 0.0 collective-permute-done.7.refs_6_
  17.8 0.2 collective-permute-done.9.refs_8_
  18.0 0.5 %respond.1 = (f32[32,128]{1,0:T(8,128)S(1)}, f32[32,128]{1,0:T(8,128)S(1)}) custom-call(s32[1]{0:T(128)} %bitcast.refs_0_, s32[1]{0:T(128)} %bitcast.1.refs_0_.refs_1_, s32[16,8]{1,0:T(8,128)S(4)} %get-tuple-element.14.refs_2_, bf16[4,8,1280]{2,1,0:T(8,128)(2,1)S(1)} %add_dynamic-update-slice_fusion.refs_2_.refs_3_, ...), custom_call_target="tpu_custom_call" | custom-call | tf_op jit(solution)/shard_map/respond/pallas_call | solution.py:297
  18.6 0.4 %collective-permute-start.11 = (f32[32,128]{1,0:T(8,128)S(1)}, f32[32,128]{1,0:T(8,128)S(1)}, u32[]{:S(2)}, u32[]{:S(2)}) collective-permute-start(f32[32,128]{1,0:T(8,128)S(1)} %get-tuple-element.18), channel_id=1, source_target_pairs={{0,1},{1,0},{2,3},{3,2},{4,5},{5,4},{6,7},{7,6},{8,9},{9,8},{10,11... | collective-permute-start | bytes 49160 | tf_op jit(solution)/shard_map/ppermute | solution.py:364
  18.9 0.9 %collective-permute-done.11 = f32[32,128]{1,0:T(8,128)S(1)} collective-permute-done((f32[32,128]{1,0:T(8,128)S(1)}, f32[32,128]{1,0:T(8,128)S(1)}, u32[]{:S(2)}, u32[]{:S(2)}) %collective-permute-start.11) | collective-permute-done | bytes 16416 | tf_op jit(solution)/shard_map/ppermute | solution.py:364
  19.8 0.6 %add.15 = f32[32,128]{1,0:T(8,128)} add(f32[32,128]{1,0:T(8,128)S(1)} %get-tuple-element.17, f32[32,128]{1,0:T(8,128)S(1)} %collective-permute-done.11) | non-fusion elementwise | flops 4096 | bytes 49152 | tf_op jit(solution)/shard_map/add | solution.py:364
  (9 shorter events, 0.0 us)
Async XLA Ops:
  1.0 1.4 %collective-permute-start = (bf16[4,8,256]{2,1,0:T(8,128)(2,1)S(1)}, bf16[4,8,256]{2,1,0:T(8,128)(2,1)S(1)}, u32[]{:S(2)}, u32[]{:S(2)}) collective-permute-start(bf16[4,8,256]{2,1,0:T(8,128)(2,1)S(1)} %get-tuple-element.13), channel_id=1, source_target_pairs={{0,1},{1,0},{2,3},{3,2},{4,5},{5,4},{6,7},{7,6},{8,9},{9,8},{10,11... | collective-permute-start | bytes 49160 | tf_op jit(solution)/shard_map/ppermute | solution.py:356
  2.4 6.5 %collective-permute-start.1 = (bf16[4,8,256]{2,1,0:T(8,128)(2,1)S(1)}, bf16[4,8,256]{2,1,0:T(8,128)(2,1)S(1)}, u32[]{:S(2)}, u32[]{:S(2)}) collective-permute-start(bf16[4,8,256]{2,1,0:T(8,128)(2,1)S(1)} %get-tuple-element.20), channel_id=1, source_target_pairs={{0,2},{1,3},{2,0},{3,1},{4,6},{5,7},{6,4},{7,5},{8,10},{9,11},{10,... | collective-permute-start | bytes 49160 | tf_op jit(solution)/shard_map/ppermute | solution.py:357
  5.3 7.2 %collective-permute-start.2 = (bf16[4,8,1280]{2,1,0:T(8,128)(2,1)S(1)}, bf16[4,8,1280]{2,1,0:T(8,128)(2,1)S(1)}, u32[]{:S(2)}, u32[]{:S(2)}) collective-permute-start(bf16[4,8,1280]{2,1,0:T(8,128)(2,1)S(1)} %get-tuple-element.19), channel_id=1, source_target_pairs={{24,0},{29,1},{26,2},{31,3},{28,4},{25,5},{30,6},{27,7},{16,8},{21... | collective-permute-start | bytes 245768 | tf_op jit(solution)/shard_map/ppermute | solution.py:276
  8.9 6.9 %collective-permute-start.6 = (bf16[4,8,1280]{2,1,0:T(8,128)(2,1)S(1)}, bf16[4,8,1280]{2,1,0:T(8,128)(2,1)S(1)}, u32[]{:S(2)}, u32[]{:S(2)}) collective-permute-start(bf16[4,8,1280]{2,1,0:T(8,128)(2,1)S(1)} %add_dynamic-update-slice_fusion.refs_2_.refs_3_), channel_id=1, source_target_pairs={{8,0},{13,1},{10,2},{15,3},{12,4},{9,5},{14,6},{11,7},{0,8},{5,9},... | collective-permute-start | bytes 245768 | tf_op jit(solution)/shard_map/ppermute | solution.py:276
  9.2 6.7 %collective-permute-start.4 = (bf16[4,8,1280]{2,1,0:T(8,128)(2,1)S(1)}, bf16[4,8,1280]{2,1,0:T(8,128)(2,1)S(1)}, u32[]{:S(2)}, u32[]{:S(2)}) collective-permute-start(bf16[4,8,1280]{2,1,0:T(8,128)(2,1)S(1)} %add_dynamic-update-slice_fusion.refs_2_.refs_3_), channel_id=1, source_target_pairs={{16,0},{21,1},{18,2},{23,3},{20,4},{17,5},{22,6},{19,7},{24,8},{29... | collective-permute-start | bytes 245768 | tf_op jit(solution)/shard_map/ppermute | solution.py:276
  11.8 4.9 %collective-permute-start.5 = (bf16[4,8,1280]{2,1,0:T(8,128)(2,1)S(1)}, bf16[4,8,1280]{2,1,0:T(8,128)(2,1)S(1)}, u32[]{:S(2)}, u32[]{:S(2)}) collective-permute-start(bf16[4,8,1280]{2,1,0:T(8,128)(2,1)S(1)} %add_dynamic-update-slice_fusion.refs_2_.refs_3_), channel_id=1, source_target_pairs={{5,1},{7,3},{1,5},{3,7},{13,9},{15,11},{9,13},{11,15},{21,17},{23,... | collective-permute-start | bytes 245768 | tf_op jit(solution)/shard_map/ppermute | solution.py:276
  12.5 4.3 %collective-permute-start.3 = (bf16[4,8,256]{2,1,0:T(8,128)(2,1)S(1)}, bf16[4,8,256]{2,1,0:T(8,128)(2,1)S(1)}, u32[]{:S(2)}, u32[]{:S(2)}) collective-permute-start(bf16[4,8,256]{2,1,0:T(8,128)(2,1)S(1)} %slice.4), channel_id=1, source_target_pairs={{0,2},{1,3},{2,0},{3,1},{4,6},{5,7},{6,4},{7,5},{8,10},{9,11},{10,... | collective-permute-start | bytes 49160 | tf_op jit(solution)/shard_map/ppermute | solution.py:279
  14.0 3.8 %collective-permute-start.7 = (bf16[4,8,1280]{2,1,0:T(8,128)(2,1)S(1)}, bf16[4,8,1280]{2,1,0:T(8,128)(2,1)S(1)}, u32[]{:S(2)}, u32[]{:S(2)}) collective-permute-start(bf16[4,8,1280]{2,1,0:T(8,128)(2,1)S(1)} %collective-permute-done.2.refs_4_), channel_id=1, source_target_pairs={{0,1},{1,0},{2,3},{3,2},{4,5},{5,4},{6,7},{7,6},{8,9},{9,8},{10,11... | collective-permute-start | bytes 245768 | tf_op jit(solution)/shard_map/ppermute | solution.py:277
  15.8 2.0 %collective-permute-start.10 = (bf16[4,8,1280]{2,1,0:T(8,128)(2,1)S(1)}, bf16[4,8,1280]{2,1,0:T(8,128)(2,1)S(1)}, u32[]{:S(2)}, u32[]{:S(2)}) collective-permute-start(bf16[4,8,1280]{2,1,0:T(8,128)(2,1)S(1)} %collective-permute-done.6.refs_7_), channel_id=1, source_target_pairs={{0,1},{1,0},{2,3},{3,2},{4,5},{5,4},{6,7},{7,6},{8,9},{9,8},{10,11... | collective-permute-start | bytes 245768 | tf_op jit(solution)/shard_map/ppermute | solution.py:277
  15.8 2.0 %collective-permute-start.8 = (bf16[4,8,1280]{2,1,0:T(8,128)(2,1)S(1)}, bf16[4,8,1280]{2,1,0:T(8,128)(2,1)S(1)}, u32[]{:S(2)}, u32[]{:S(2)}) collective-permute-start(bf16[4,8,1280]{2,1,0:T(8,128)(2,1)S(1)} %collective-permute-done.4.refs_5_), channel_id=1, source_target_pairs={{0,1},{1,0},{2,3},{3,2},{4,5},{5,4},{6,7},{7,6},{8,9},{9,8},{10,11... | collective-permute-start | bytes 245768 | tf_op jit(solution)/shard_map/ppermute | solution.py:277
  16.7 1.3 %collective-permute-start.9 = (bf16[4,8,1280]{2,1,0:T(8,128)(2,1)S(1)}, bf16[4,8,1280]{2,1,0:T(8,128)(2,1)S(1)}, u32[]{:S(2)}, u32[]{:S(2)}) collective-permute-start(bf16[4,8,1280]{2,1,0:T(8,128)(2,1)S(1)} %collective-permute-done.5.refs_6_), channel_id=1, source_target_pairs={{0,1},{1,0},{2,3},{3,2},{4,5},{5,4},{6,7},{7,6},{8,9},{9,8},{10,11... | collective-permute-start | bytes 245768 | tf_op jit(solution)/shard_map/ppermute | solution.py:277
  18.6 1.2 %collective-permute-start.11 = (f32[32,128]{1,0:T(8,128)S(1)}, f32[32,128]{1,0:T(8,128)S(1)}, u32[]{:S(2)}, u32[]{:S(2)}) collective-permute-start(f32[32,128]{1,0:T(8,128)S(1)} %get-tuple-element.18), channel_id=1, source_target_pairs={{0,1},{1,0},{2,3},{3,2},{4,5},{5,4},{6,7},{7,6},{8,9},{9,8},{10,11... | collective-permute-start | bytes 49160 | tf_op jit(solution)/shard_map/ppermute | solution.py:364

commit v9 on v8

--- a/solution.py
+++ b/solution.py
@@ -202,15 +202,22 @@
         owner = place * 2 + (side ^ half) % 2
         for atom in range(local_atoms):
             rows_ref[owner * local_atoms + atom] = near_ref[place * local_atoms + atom]
-    found = []
+    total = jnp.zeros((both_ref.shape[0], aux_count), F32)
+    depth = CHUNK * block_size * block_size
     for chunk in range(chunk_count):
         for atom in range(count * local_atoms):
+            found = []
             for unit in range(chunk * CHUNK, (chunk + 1) * CHUNK):
                 if unit < unit_count:
                     found.append(rows_ref[index_ref[atom, unit]])
                 else:
                     found.append(jnp.zeros(rows_ref.shape[1:], BF16))
-    total = jnp.dot(both_ref[...], jnp.concatenate(found, axis=0), preferred_element_type=F32)
+            at = (chunk * count * local_atoms + atom) * depth
+            total += jnp.dot(
+                both_ref[:, at : at + depth],
+                jnp.concatenate(found, axis=0),
+                preferred_element_type=F32,
+            )
     write_rows(total, half, keep_ref, send_ref)
 
 

time: 20.6 us -> 20.6 us (level)
  no operation moved by 1% of the time
where the time goes in v9:
time: 20.6 us; the launch traced here: 20.4 us
  starting transfers between devices  14.9 us (72%)
  Pallas kernels  2.6 us (13%)
  waiting for transfers between devices  2.22 us (11%)
  other arithmetic  0.63 us (3%)
    ppermute x4, starting transfers between devices, respond_direct(): lax.ppermute(full if slot else early, ('wide', 'pair'), route)  7.13 us
    ppermute x1, starting transfers between devices, local(): four = two + lax.ppermute(two, 'pair', across)  2.9 us
    ppermute x4, starting transfers between devices, respond_direct(): far.append(lax.ppermute(fetched[-1], 'pair', partner))  2.39 us
    ppermute x1, starting transfers between devices, respond_direct(): small = small + lax.ppermute(small, 'pair', across)  1.56 us
    pallas_call x1, Pallas kernels, respond_direct(): pl.pallas_call(kernel_of(contract_kernel, unit_count), out_shape=(pltpu.V...  1.04 us
    pallas_call x1, Pallas kernels, local(): pl.pallas_call(kernel_of(pack_kernel, unit_count), out_shape=(pltpu.VMEM(...  1.02 us
    ppermute x1, waiting for transfers between devices, local(): return keep + lax.ppermute(send, 'pair', partner)  0.87 us
    ppermute x1, waiting for transfers between devices, local(): two = small + lax.ppermute(small, 'pair', partner)  0.83 us
  transfers between devices with their start and end apart: 12, of which 4 were waited for; matrix products, arithmetic and copies ran while one was open for 0% of the time, Pallas kernels for 5%

profile of v9, /device:TPU:0, one launch (start us, length us, event | category | flops | bytes accessed | tf_op | source)
XLA Modules:
  0.0 20.4 jit_solution(4949231413966468976)
XLA Ops:
  0.0 1.0 %pack.1 = (bf16[4,8,1280]{2,1,0:T(8,128)(2,1)S(1)}, bf16[4,8,256]{2,1,0:T(8,128)(2,1)S(1)}) custom-call(s32[1]{0:T(128)} %bitcast.1.refs_0_.refs_1_, s32[2,4]{1,0:T(2,128)} %bitcast.4, s32[2,4]{1,0:T(2,128)} %bitcast.5, bf16[4,8,1024]{2,1,0:T(8,128)(2,1)} %refs_3_.1, bf16[4,2,8,8]{3,2,1,0:T(8,128)(2,1)} %refs_4_.1, bf16[4,2,8,8]{3,2,1,0:T(8,128)(2,1)} %refs_5_.1), custom_call_target="tpu_custom_call" | custom-call | tf_op jit(solution)/shard_map/pack/pallas_call | solution.py:353
  1.0 0.5 %collective-permute-start = (bf16[4,8,256]{2,1,0:T(8,128)(2,1)S(1)}, bf16[4,8,256]{2,1,0:T(8,128)(2,1)S(1)}, u32[]{:S(2)}, u32[]{:S(2)}) collective-permute-start(bf16[4,8,256]{2,1,0:T(8,128)(2,1)S(1)} %get-tuple-element.13), channel_id=1, source_target_pairs={{0,1},{1,0},{2,3},{3,2},{4,5},{5,4},{6,7},{7,6},{8,9},{9,8},{10,11... | collective-permute-start | bytes 49160 | tf_op jit(solution)/shard_map/ppermute | solution.py:363
  1.5 0.8 %collective-permute-done = bf16[4,8,256]{2,1,0:T(8,128)(2,1)S(1)} collective-permute-done((bf16[4,8,256]{2,1,0:T(8,128)(2,1)S(1)}, bf16[4,8,256]{2,1,0:T(8,128)(2,1)S(1)}, u32[]{:S(2)}, u32[]{:S(2)}) %collective-permute-start) | collective-permute-done | bytes 16416 | tf_op jit(solution)/shard_map/ppermute | solution.py:363
  2.4 2.9 %collective-permute-start.1 = (bf16[4,8,256]{2,1,0:T(8,128)(2,1)S(1)}, bf16[4,8,256]{2,1,0:T(8,128)(2,1)S(1)}, u32[]{:S(2)}, u32[]{:S(2)}) collective-permute-start(bf16[4,8,256]{2,1,0:T(8,128)(2,1)S(1)} %get-tuple-element.20), channel_id=1, source_target_pairs={{0,2},{1,3},{2,0},{3,1},{4,6},{5,7},{6,4},{7,5},{8,10},{9,11},{10,... | collective-permute-start | bytes 49160 | tf_op jit(solution)/shard_map/ppermute | solution.py:364
  5.3 3.6 %collective-permute-start.2 = (bf16[4,8,1280]{2,1,0:T(8,128)(2,1)S(1)}, bf16[4,8,1280]{2,1,0:T(8,128)(2,1)S(1)}, u32[]{:S(2)}, u32[]{:S(2)}) collective-permute-start(bf16[4,8,1280]{2,1,0:T(8,128)(2,1)S(1)} %get-tuple-element.19), channel_id=1, source_target_pairs={{24,0},{29,1},{26,2},{31,3},{28,4},{25,5},{30,6},{27,7},{16,8},{21... | collective-permute-start | bytes 245768 | tf_op jit(solution)/shard_map/ppermute | solution.py:283
  8.9 0.0 collective-permute-done.1
  8.9 0.3 %collective-permute-start.6 = (bf16[4,8,1280]{2,1,0:T(8,128)(2,1)S(1)}, bf16[4,8,1280]{2,1,0:T(8,128)(2,1)S(1)}, u32[]{:S(2)}, u32[]{:S(2)}) collective-permute-start(bf16[4,8,1280]{2,1,0:T(8,128)(2,1)S(1)} %add_dynamic-update-slice_fusion.refs_2_.refs_3_), channel_id=1, source_target_pairs={{8,0},{13,1},{10,2},{15,3},{12,4},{9,5},{14,6},{11,7},{0,8},{5,9},... | collective-permute-start | bytes 245768 | tf_op jit(solution)/shard_map/ppermute | solution.py:283
  9.2 2.6 %collective-permute-start.4 = (bf16[4,8,1280]{2,1,0:T(8,128)(2,1)S(1)}, bf16[4,8,1280]{2,1,0:T(8,128)(2,1)S(1)}, u32[]{:S(2)}, u32[]{:S(2)}) collective-permute-start(bf16[4,8,1280]{2,1,0:T(8,128)(2,1)S(1)} %add_dynamic-update-slice_fusion.refs_2_.refs_3_), channel_id=1, source_target_pairs={{16,0},{21,1},{18,2},{23,3},{20,4},{17,5},{22,6},{19,7},{24,8},{29... | collective-permute-start | bytes 245768 | tf_op jit(solution)/shard_map/ppermute | solution.py:283
  11.8 0.7 %collective-permute-start.5 = (bf16[4,8,1280]{2,1,0:T(8,128)(2,1)S(1)}, bf16[4,8,1280]{2,1,0:T(8,128)(2,1)S(1)}, u32[]{:S(2)}, u32[]{:S(2)}) collective-permute-start(bf16[4,8,1280]{2,1,0:T(8,128)(2,1)S(1)} %add_dynamic-update-slice_fusion.refs_2_.refs_3_), channel_id=1, source_target_pairs={{5,1},{7,3},{1,5},{3,7},{13,9},{15,11},{9,13},{11,15},{21,17},{23,... | collective-permute-start | bytes 245768 | tf_op jit(solution)/shard_map/ppermute | solution.py:283
  12.5 1.6 %collective-permute-start.3 = (bf16[4,8,256]{2,1,0:T(8,128)(2,1)S(1)}, bf16[4,8,256]{2,1,0:T(8,128)(2,1)S(1)}, u32[]{:S(2)}, u32[]{:S(2)}) collective-permute-start(bf16[4,8,256]{2,1,0:T(8,128)(2,1)S(1)} %slice.4), channel_id=1, source_target_pairs={{0,2},{1,3},{2,0},{3,1},{4,6},{5,7},{6,4},{7,5},{8,10},{9,11},{10,... | collective-permute-start | bytes 49160 | tf_op jit(solution)/shard_map/ppermute | solution.py:286
  14.0 1.5 %collective-permute-start.7 = (bf16[4,8,1280]{2,1,0:T(8,128)(2,1)S(1)}, bf16[4,8,1280]{2,1,0:T(8,128)(2,1)S(1)}, u32[]{:S(2)}, u32[]{:S(2)}) collective-permute-start(bf16[4,8,1280]{2,1,0:T(8,128)(2,1)S(1)} %collective-permute-done.2.refs_4_), channel_id=1, source_target_pairs={{0,1},{1,0},{2,3},{3,2},{4,5},{5,4},{6,7},{7,6},{8,9},{9,8},{10,11... | collective-permute-start | bytes 245768 | tf_op jit(solution)/shard_map/ppermute | solution.py:284
  15.5 0.3 %collective-permute-done.6.refs_7_ = bf16[4,8,1280]{2,1,0:T(8,128)(2,1)S(1)} collective-permute-done((bf16[4,8,1280]{2,1,0:T(8,128)(2,1)S(1)}, bf16[4,8,1280]{2,1,0:T(8,128)(2,1)S(1)}, u32[]{:S(2)}, u32[]{:S(2)}) %collective-permute-start.6) | collective-permute-done | bytes 81952 | tf_op jit(solution)/shard_map/ppermute | solution.py:283
  15.8 0.0 collective-permute-start.10
  15.8 0.0 collective-permute-done.4.refs_5_
  15.8 0.9 %collective-permute-start.8 = (bf16[4,8,1280]{2,1,0:T(8,128)(2,1)S(1)}, bf16[4,8,1280]{2,1,0:T(8,128)(2,1)S(1)}, u32[]{:S(2)}, u32[]{:S(2)}) collective-permute-start(bf16[4,8,1280]{2,1,0:T(8,128)(2,1)S(1)} %collective-permute-done.4.refs_5_), channel_id=1, source_target_pairs={{0,1},{1,0},{2,3},{3,2},{4,5},{5,4},{6,7},{7,6},{8,9},{9,8},{10,11... | collective-permute-start | bytes 245768 | tf_op jit(solution)/shard_map/ppermute | solution.py:284
  16.7 0.0 collective-permute-start.9
  16.7 0.0 collective-permute-done.3
  16.7 1.0 %contract.1 = (bf16[64,8192]{1,0:T(8,128)(2,1)S(1)}, bf16[16,64,128]{2,1,0:T(8,128)(2,1)S(1)}, s32[16,8]{1,0:T(8,128)S(4)}) custom-call(s32[1]{0:T(128)} %bitcast.refs_0_, s32[1]{0:T(128)} %bitcast.1.refs_0_.refs_1_, bf16[4,8,1280]{2,1,0:T(8,128)(2,1)S(1)} %add_dynamic-update-slice_fusion.refs_2_.refs_3_, bf16[4,8,256]{2,1,0:T(8,128)(2,1)S(1)} %slice_add_fusion.refs_3_, ...), custom_call_target="tpu_custom_call" | custom-call | tf_op jit(solution)/shard_map/contract/pallas_call | solution.py:291
  17.8 0.0 collective-permute-done.7.refs_6_
  17.8 0.2 collective-permute-done.9.refs_8_
  18.0 0.5 %respond.1 = (f32[32,128]{1,0:T(8,128)S(1)}, f32[32,128]{1,0:T(8,128)S(1)}) custom-call(s32[1]{0:T(128)} %bitcast.refs_0_, s32[1]{0:T(128)} %bitcast.1.refs_0_.refs_1_, s32[16,8]{1,0:T(8,128)S(4)} %get-tuple-element.14.refs_2_, bf16[4,8,1280]{2,1,0:T(8,128)(2,1)S(1)} %add_dynamic-update-slice_fusion.refs_2_.refs_3_, ...), custom_call_target="tpu_custom_call" | custom-call | tf_op jit(solution)/shard_map/respond/pallas_call | solution.py:304
  18.6 0.4 %collective-permute-start.11 = (f32[32,128]{1,0:T(8,128)S(1)}, f32[32,128]{1,0:T(8,128)S(1)}, u32[]{:S(2)}, u32[]{:S(2)}) collective-permute-start(f32[32,128]{1,0:T(8,128)S(1)} %get-tuple-element.18), channel_id=1, source_target_pairs={{0,1},{1,0},{2,3},{3,2},{4,5},{5,4},{6,7},{7,6},{8,9},{9,8},{10,11... | collective-permute-start | bytes 49160 | tf_op jit(solution)/shard_map/ppermute | solution.py:371
  18.9 0.9 %collective-permute-done.11 = f32[32,128]{1,0:T(8,128)S(1)} collective-permute-done((f32[32,128]{1,0:T(8,128)S(1)}, f32[32,128]{1,0:T(8,128)S(1)}, u32[]{:S(2)}, u32[]{:S(2)}) %collective-permute-start.11) | collective-permute-done | bytes 16416 | tf_op jit(solution)/shard_map/ppermute | solution.py:371
  19.8 0.6 %add.15 = f32[32,128]{1,0:T(8,128)} add(f32[32,128]{1,0:T(8,128)S(1)} %get-tuple-element.17, f32[32,128]{1,0:T(8,128)S(1)} %collective-permute-done.11) | non-fusion elementwise | flops 4096 | bytes 49152 | tf_op jit(solution)/shard_map/add | solution.py:371
  (9 shorter events, 0.0 us)
Async XLA Ops:
  1.0 1.4 %collective-permute-start = (bf16[4,8,256]{2,1,0:T(8,128)(2,1)S(1)}, bf16[4,8,256]{2,1,0:T(8,128)(2,1)S(1)}, u32[]{:S(2)}, u32[]{:S(2)}) collective-permute-start(bf16[4,8,256]{2,1,0:T(8,128)(2,1)S(1)} %get-tuple-element.13), channel_id=1, source_target_pairs={{0,1},{1,0},{2,3},{3,2},{4,5},{5,4},{6,7},{7,6},{8,9},{9,8},{10,11... | collective-permute-start | bytes 49160 | tf_op jit(solution)/shard_map/ppermute | solution.py:363
  2.4 6.5 %collective-permute-start.1 = (bf16[4,8,256]{2,1,0:T(8,128)(2,1)S(1)}, bf16[4,8,256]{2,1,0:T(8,128)(2,1)S(1)}, u32[]{:S(2)}, u32[]{:S(2)}) collective-permute-start(bf16[4,8,256]{2,1,0:T(8,128)(2,1)S(1)} %get-tuple-element.20), channel_id=1, source_target_pairs={{0,2},{1,3},{2,0},{3,1},{4,6},{5,7},{6,4},{7,5},{8,10},{9,11},{10,... | collective-permute-start | bytes 49160 | tf_op jit(solution)/shard_map/ppermute | solution.py:364
  5.3 7.2 %collective-permute-start.2 = (bf16[4,8,1280]{2,1,0:T(8,128)(2,1)S(1)}, bf16[4,8,1280]{2,1,0:T(8,128)(2,1)S(1)}, u32[]{:S(2)}, u32[]{:S(2)}) collective-permute-start(bf16[4,8,1280]{2,1,0:T(8,128)(2,1)S(1)} %get-tuple-element.19), channel_id=1, source_target_pairs={{24,0},{29,1},{26,2},{31,3},{28,4},{25,5},{30,6},{27,7},{16,8},{21... | collective-permute-start | bytes 245768 | tf_op jit(solution)/shard_map/ppermute | solution.py:283
  8.9 6.9 %collective-permute-start.6 = (bf16[4,8,1280]{2,1,0:T(8,128)(2,1)S(1)}, bf16[4,8,1280]{2,1,0:T(8,128)(2,1)S(1)}, u32[]{:S(2)}, u32[]{:S(2)}) collective-permute-start(bf16[4,8,1280]{2,1,0:T(8,128)(2,1)S(1)} %add_dynamic-update-slice_fusion.refs_2_.refs_3_), channel_id=1, source_target_pairs={{8,0},{13,1},{10,2},{15,3},{12,4},{9,5},{14,6},{11,7},{0,8},{5,9},... | collective-permute-start | bytes 245768 | tf_op jit(solution)/shard_map/ppermute | solution.py:283
  9.2 6.7 %collective-permute-start.4 = (bf16[4,8,1280]{2,1,0:T(8,128)(2,1)S(1)}, bf16[4,8,1280]{2,1,0:T(8,128)(2,1)S(1)}, u32[]{:S(2)}, u32[]{:S(2)}) collective-permute-start(bf16[4,8,1280]{2,1,0:T(8,128)(2,1)S(1)} %add_dynamic-update-slice_fusion.refs_2_.refs_3_), channel_id=1, source_target_pairs={{16,0},{21,1},{18,2},{23,3},{20,4},{17,5},{22,6},{19,7},{24,8},{29... | collective-permute-start | bytes 245768 | tf_op jit(solution)/shard_map/ppermute | solution.py:283
  11.8 4.9 %collective-permute-start.5 = (bf16[4,8,1280]{2,1,0:T(8,128)(2,1)S(1)}, bf16[4,8,1280]{2,1,0:T(8,128)(2,1)S(1)}, u32[]{:S(2)}, u32[]{:S(2)}) collective-permute-start(bf16[4,8,1280]{2,1,0:T(8,128)(2,1)S(1)} %add_dynamic-update-slice_fusion.refs_2_.refs_3_), channel_id=1, source_target_pairs={{5,1},{7,3},{1,5},{3,7},{13,9},{15,11},{9,13},{11,15},{21,17},{23,... | collective-permute-start | bytes 245768 | tf_op jit(solution)/shard_map/ppermute | solution.py:283
  12.5 4.3 %collective-permute-start.3 = (bf16[4,8,256]{2,1,0:T(8,128)(2,1)S(1)}, bf16[4,8,256]{2,1,0:T(8,128)(2,1)S(1)}, u32[]{:S(2)}, u32[]{:S(2)}) collective-permute-start(bf16[4,8,256]{2,1,0:T(8,128)(2,1)S(1)} %slice.4), channel_id=1, source_target_pairs={{0,2},{1,3},{2,0},{3,1},{4,6},{5,7},{6,4},{7,5},{8,10},{9,11},{10,... | collective-permute-start | bytes 49160 | tf_op jit(solution)/shard_map/ppermute | solution.py:286
  14.0 3.8 %collective-permute-start.7 = (bf16[4,8,1280]{2,1,0:T(8,128)(2,1)S(1)}, bf16[4,8,1280]{2,1,0:T(8,128)(2,1)S(1)}, u32[]{:S(2)}, u32[]{:S(2)}) collective-permute-start(bf16[4,8,1280]{2,1,0:T(8,128)(2,1)S(1)} %collective-permute-done.2.refs_4_), channel_id=1, source_target_pairs={{0,1},{1,0},{2,3},{3,2},{4,5},{5,4},{6,7},{7,6},{8,9},{9,8},{10,11... | collective-permute-start | bytes 245768 | tf_op jit(solution)/shard_map/ppermute | solution.py:284
  15.8 2.0 %collective-permute-start.10 = (bf16[4,8,1280]{2,1,0:T(8,128)(2,1)S(1)}, bf16[4,8,1280]{2,1,0:T(8,128)(2,1)S(1)}, u32[]{:S(2)}, u32[]{:S(2)}) collective-permute-start(bf16[4,8,1280]{2,1,0:T(8,128)(2,1)S(1)} %collective-permute-done.6.refs_7_), channel_id=1, source_target_pairs={{0,1},{1,0},{2,3},{3,2},{4,5},{5,4},{6,7},{7,6},{8,9},{9,8},{10,11... | collective-permute-start | bytes 245768 | tf_op jit(solution)/shard_map/ppermute | solution.py:284
  15.8 2.0 %collective-permute-start.8 = (bf16[4,8,1280]{2,1,0:T(8,128)(2,1)S(1)}, bf16[4,8,1280]{2,1,0:T(8,128)(2,1)S(1)}, u32[]{:S(2)}, u32[]{:S(2)}) collective-permute-start(bf16[4,8,1280]{2,1,0:T(8,128)(2,1)S(1)} %collective-permute-done.4.refs_5_), channel_id=1, source_target_pairs={{0,1},{1,0},{2,3},{3,2},{4,5},{5,4},{6,7},{7,6},{8,9},{9,8},{10,11... | collective-permute-start | bytes 245768 | tf_op jit(solution)/shard_map/ppermute | solution.py:284
  16.7 1.3 %collective-permute-start.9 = (bf16[4,8,1280]{2,1,0:T(8,128)(2,1)S(1)}, bf16[4,8,1280]{2,1,0:T(8,128)(2,1)S(1)}, u32[]{:S(2)}, u32[]{:S(2)}) collective-permute-start(bf16[4,8,1280]{2,1,0:T(8,128)(2,1)S(1)} %collective-permute-done.5.refs_6_), channel_id=1, source_target_pairs={{0,1},{1,0},{2,3},{3,2},{4,5},{5,4},{6,7},{7,6},{8,9},{9,8},{10,11... | collective-permute-start | bytes 245768 | tf_op jit(solution)/shard_map/ppermute | solution.py:284
  18.6 1.2 %collective-permute-start.11 = (f32[32,128]{1,0:T(8,128)S(1)}, f32[32,128]{1,0:T(8,128)S(1)}, u32[]{:S(2)}, u32[]{:S(2)}) collective-permute-start(f32[32,128]{1,0:T(8,128)S(1)} %get-tuple-element.18), channel_id=1, source_target_pairs={{0,1},{1,0},{2,3},{3,2},{4,5},{5,4},{6,7},{7,6},{8,9},{9,8},{10,11... | collective-permute-start | bytes 49160 | tf_op jit(solution)/shard_map/ppermute | solution.py:371
